TPU v7x, 32 devices: a whole 2x2x4 slice. The times are simulated.
32 devices in a mesh: seq: 8 (over y, x, core), wsh: 4 (over z).
Axes of the slice: x: 2, y: 2, z: 4, core: 2. Of those that a mesh axis runs over, the one named last changes fastest.
Arguments:
- tokens: bfloat16 [4, 4096, 1024], P('wsh', 'seq'), may hold values from -6 to 6
- doc_start: int32 [4, 4096], P('wsh', 'seq'), may hold values from 0 to 4095, as said below
- norm1_gain: float32 [1024], P('wsh'), may hold values from 0.5 to 1.5
- in_weight: float32 [1024, 3072], P('wsh'), may hold values from -0.1875 to 0.1875
- conv_weight: float32 [1024, 3], P('wsh'), may hold values from -3 to 3
- out_weight: float32 [1024, 1024], P('wsh'), may hold values from -0.1875 to 0.1875
- norm2_gain: float32 [1024], P('wsh'), may hold values from 0.5 to 1.5
- gate_up_weight: float32 [1024, 9216], P('wsh'), may hold values from -0.1875 to 0.1875
- down_weight: float32 [4608, 1024], P('wsh'), may hold values from -0.09375 to 0.09375
- out_grad: bfloat16 [4, 4096, 1024], P('wsh', 'seq'), may hold values from -6 to 6
Outputs:
- block_out: bfloat16 [4, 4096, 1024], P('wsh', 'seq')
- input_grad: bfloat16 [4, 4096, 1024], P('wsh', 'seq')
- norm1_grad: float32 [1024], P('wsh')
- in_grad: float32 [1024, 3072], P('wsh')
- conv_grad: float32 [1024, 3], P('wsh')
- out_proj_grad: float32 [1024, 1024], P('wsh')
- norm2_grad: float32 [1024], P('wsh')
- gate_up_grad: float32 [1024, 9216], P('wsh')
- down_grad: float32 [4608, 1024], P('wsh')
Inputs may be any that keep to these rules, and one draw needn't show every extreme that they name: `doc_start`: each value is the position of its token's document's first token; a document begins at position 0, at the last position 4095, and at least once in every run of 512 positions that starts at a multiple of 512, never at the first two positions of such a run after the first.
All inputs are finite; a program needn't handle non-finite values.
Results may differ from a plain program's by a relative error of at most 0.012.
The roundings to bfloat16 on the way count: a program that leaves them out, or rounds other values in their place, can miss the bound.
Values may be sent and summed in bfloat16 or wider, within the bound.
A program may use at most 256 MiB of HBM per device.

v0:
```python
import jax
import jax.numpy as jnp
from jax import lax
from jax.sharding import PartitionSpec as P

epsilon = 1e-06


def shifted(value, axis, steps):
    count = lax.axis_size(axis)
    leading, last = (max(0, -steps), min(count, count - steps))
    return lax.ppermute(value, axis, [(source, source + steps) for source in range(leading, last)])


def inner(left, right):
    return lax.dot_general(
        left, right, (((0,), (0,)), ((), ())), preferred_element_type=jnp.float32
    )


def outer(left, right):
    return lax.dot_general(
        left, right, (((1,), (1,)), ((), ())), preferred_element_type=jnp.float32
    )


def local(
    tokens,
    doc_start,
    norm1_gain,
    in_weight,
    conv_weight,
    out_weight,
    norm2_gain,
    gate_up_weight,
    down_weight,
    out_grad,
):
    masters = (
        norm1_gain,
        in_weight,
        conv_weight,
        out_weight,
        norm2_gain,
        gate_up_weight,
        down_weight,
    )
    copies = (
        masters[0].astype(jnp.bfloat16),
        masters[1].astype(jnp.bfloat16),
        masters[2].astype(jnp.bfloat16),
        masters[3].astype(jnp.bfloat16),
        masters[4].astype(jnp.bfloat16),
        masters[5].astype(jnp.bfloat16),
        masters[6].astype(jnp.bfloat16),
    )
    full = (
        lax.all_gather(copies[0], "wsh", axis=0, tiled=True),
        lax.all_gather(copies[1], "wsh", axis=0, tiled=True),
        lax.all_gather(copies[2], "wsh", axis=0, tiled=True),
        lax.all_gather(copies[3], "wsh", axis=0, tiled=True),
        lax.all_gather(copies[4], "wsh", axis=0, tiled=True),
        lax.all_gather(copies[5], "wsh", axis=0, tiled=True),
        lax.all_gather(copies[6], "wsh", axis=0, tiled=True),
    )
    gain_one = full[0].astype(jnp.float32)
    w_in = full[1]
    taps = full[2].astype(jnp.float32)
    w_out = full[3]
    gain_two = full[4].astype(jnp.float32)
    w_gu = full[5]
    w_down = full[6]
    xf = tokens[0].astype(jnp.float32)
    starts = doc_start[0]
    rows = xf.shape[0]
    width = xf.shape[1]
    hidden = w_down.shape[0]
    rate_one = lax.rsqrt(jnp.mean(xf * xf, axis=-1, keepdims=True) + epsilon)
    normed = xf * rate_one
    normed_low = (normed * gain_one).astype(jnp.bfloat16)
    proj = jnp.dot(normed_low, w_in, preferred_element_type=jnp.float32)
    bpart = proj[:, :width]
    cpart = proj[:, width : 2 * width]
    xpart = proj[:, 2 * width :]
    gated = (bpart * xpart).astype(jnp.bfloat16)
    edge = shifted(gated[rows - 2 :], "seq", 1)
    extended = jnp.concatenate([edge, gated], 0).astype(jnp.float32)
    place = lax.axis_index("seq") * rows + jnp.arange(rows, dtype=jnp.int32)
    keep_one = (place - 1 >= starts).astype(jnp.float32)[:, None]
    keep_two = (place - 2 >= starts).astype(jnp.float32)[:, None]
    current = extended[2:]
    lag_one = extended[1:-1]
    lag_two = extended[:-2]
    mixed = taps[:, 0] * current
    mixed = mixed + keep_one * taps[:, 1] * lag_one
    mixed = mixed + keep_two * taps[:, 2] * lag_two
    zed = (cpart * mixed).astype(jnp.bfloat16)
    first = xf + jnp.dot(zed, w_out, preferred_element_type=jnp.float32)
    rate_two = lax.rsqrt(jnp.mean(first * first, axis=-1, keepdims=True) + epsilon)
    normed_two = first * rate_two
    second_low = (normed_two * gain_two).astype(jnp.bfloat16)
    both = jnp.dot(second_low, w_gu, preferred_element_type=jnp.float32)
    gate = both[:, :hidden]
    upper = both[:, hidden:]
    sigma = jax.nn.sigmoid(gate)
    swish = gate * sigma
    act = (swish * upper).astype(jnp.bfloat16)
    result = first + jnp.dot(act, w_down, preferred_element_type=jnp.float32)
    cotan = out_grad[0]
    grad_down = inner(act, cotan)
    grad_act = outer(cotan, w_down)
    grad_gate = grad_act * upper * (sigma * (1.0 + gate * (1.0 - sigma)))
    grad_upper = grad_act * swish
    grad_both = jnp.concatenate([grad_gate, grad_upper], 1).astype(jnp.bfloat16)
    grad_gu = inner(second_low, grad_both)
    grad_second = outer(grad_both, w_gu)
    grad_gain_two = jnp.sum(grad_second * normed_two, axis=0)
    scaled_two = grad_second * gain_two
    grad_first = cotan.astype(jnp.float32) + rate_two * (
        scaled_two - normed_two * jnp.mean(scaled_two * normed_two, axis=-1, keepdims=True)
    )
    grad_branch = grad_first.astype(jnp.bfloat16)
    grad_outw = inner(zed, grad_branch)
    grad_zed = outer(grad_branch, w_out)
    grad_cpart = grad_zed * mixed
    grad_mixed = grad_zed * cpart
    term_one = keep_one * grad_mixed
    term_two = keep_two * grad_mixed
    grad_taps = jnp.stack(
        [
            jnp.sum(grad_mixed * current, axis=0),
            jnp.sum(term_one * lag_one, axis=0),
            jnp.sum(term_two * lag_two, axis=0),
        ],
        axis=1,
    )
    grad_ext = jnp.pad(taps[:, 0] * grad_mixed, ((2, 0), (0, 0)))
    grad_ext = grad_ext + jnp.pad(taps[:, 1] * term_one, ((1, 1), (0, 0)))
    grad_ext = grad_ext + jnp.pad(taps[:, 2] * term_two, ((0, 2), (0, 0)))
    returned = shifted(grad_ext[:2], "seq", -1)
    grad_gated = grad_ext[2:] + jnp.concatenate(
        [jnp.zeros((rows - 2, width), jnp.float32), returned], 0
    )
    grad_proj = jnp.concatenate([grad_gated * xpart, grad_cpart, grad_gated * bpart], 1).astype(
        jnp.bfloat16
    )
    grad_inw = inner(normed_low, grad_proj)
    grad_normed = outer(grad_proj, w_in)
    grad_gain_one = jnp.sum(grad_normed * normed, axis=0)
    scaled_one = grad_normed * gain_one
    grad_input = grad_first + rate_one * (
        scaled_one - normed * jnp.mean(scaled_one * normed, axis=-1, keepdims=True)
    )
    shards = (
        lax.psum_scatter(
            grad_gain_one.astype(jnp.bfloat16), "wsh", scatter_dimension=0, tiled=True
        ).astype(jnp.float32),
        lax.psum_scatter(
            grad_inw.astype(jnp.bfloat16), "wsh", scatter_dimension=0, tiled=True
        ).astype(jnp.float32),
        lax.psum_scatter(
            grad_taps.astype(jnp.bfloat16), "wsh", scatter_dimension=0, tiled=True
        ).astype(jnp.float32),
        lax.psum_scatter(
            grad_outw.astype(jnp.bfloat16), "wsh", scatter_dimension=0, tiled=True
        ).astype(jnp.float32),
        lax.psum_scatter(
            grad_gain_two.astype(jnp.bfloat16), "wsh", scatter_dimension=0, tiled=True
        ).astype(jnp.float32),
        lax.psum_scatter(
            grad_gu.astype(jnp.bfloat16), "wsh", scatter_dimension=0, tiled=True
        ).astype(jnp.float32),
        lax.psum_scatter(
            grad_down.astype(jnp.bfloat16), "wsh", scatter_dimension=0, tiled=True
        ).astype(jnp.float32),
    )
    total = lax.psum(
        (shards[0], shards[1], shards[2], shards[3], shards[4], shards[5], shards[6]), "seq"
    )
    return (
        result.astype(jnp.bfloat16)[None],
        grad_input.astype(jnp.bfloat16)[None],
        total[0],
        total[1],
        total[2],
        total[3],
        total[4],
        total[5],
        total[6],
    )


def solution(mesh):
    in_specs = (
        P("wsh", "seq", None),
        P("wsh", "seq"),
        P("wsh"),
        P("wsh", None),
        P("wsh", None),
        P("wsh", None),
        P("wsh"),
        P("wsh", None),
        P("wsh", None),
        P("wsh", "seq", None),
    )
    out_specs = (
        P("wsh", "seq", None),
        P("wsh", "seq", None),
        P("wsh"),
        P("wsh", None),
        P("wsh", None),
        P("wsh", None),
        P("wsh"),
        P("wsh", None),
        P("wsh", None),
    )
    return jax.shard_map(local, mesh=mesh, in_specs=in_specs, out_specs=out_specs, check_vma=False)
```

profile of v0, /device:TPU:1, one launch (start us, length us, event | category | flops | bytes accessed | tf_op | source)
XLA Modules:
  0.0 1732.8 jit_solution(15681097623872215757)
XLA Ops:
  7.2 3.3 convert_element_type.133
  10.6 0.9 convert_element_type.141
  11.6 6.5 convert_element_type.145
  18.2 4.5 convert_element_type.147
  22.7 0.6 copy-done.20
  23.3 12.4 all-gather
  35.8 9.8 all_gather.23
  45.9 82.7 %all-gather.7.cloned.1.call-done = bf16[1024,3072]{1,0:T(8,128)(2,1)} async-done(((bf16[256,3072]{1,0:T(8,128)(2,1)}), bf16[1024,3072]{1,0:T(8,128)(2,1)}) %all-gather.7.cloned.1.call-update) | async-done | bytes 6291472 | tf_op jit(solution)/shard_map/all_gather | solution.py:59
  128.5 5.7 fusion.24
  134.7 3.4 collective-permute-start
  138.2 6.4 all-gather.1
  144.9 2.6 multiply_convert_fusion.7
  147.5 27.2 %all-gather.9.cloned.1.call-done = bf16[1024,1024]{1,0:T(8,128)(2,1)} async-done(((bf16[256,1024]{1,0:T(8,128)(2,1)}), bf16[1024,1024]{1,0:T(8,128)(2,1)}) %all-gather.9.cloned.1.call-update) | async-done | bytes 2097168 | tf_op jit(solution)/shard_map/all_gather | solution.py:61
  174.7 4.5 multiply_reduce_fusion.5
  179.2 319.2 %all-gather.11.cloned.1.call-done = bf16[1024,9216]{1,0:T(8,128)(2,1)} async-done(((bf16[256,9216]{1,0:T(8,128)(2,1)}), bf16[1024,9216]{1,0:T(8,128)(2,1)}) %all-gather.11.cloned.1.call-update) | async-done | bytes 18874384 | tf_op jit(solution)/shard_map/all_gather | solution.py:63
  498.5 18.3 %fusion.32 = f32[512,9216]{1,0:T(8,128)} fusion(bf16[1024,9216]{1,0:T(8,128)(2,1)} %all-gather.11.cloned.1.call-done, f32[512,1024]{1,0:T(8,128)} %get-tuple-element.43, f32[1024]{0:T(1024)S(1)} %bitcast.54, f32[512]{0:T(512)S(1)} %add_rsqrt_fusion), kind=kOutput, calls=%fused_computation.76 | convolution fusion | flops 9665249280 | bytes 39852032 | tf_op jit(solution)/shard_map/dot_general | solution.py:102
  516.8 149.6 %all-gather.13.cloned.1.call-done = bf16[4608,1024]{1,0:T(8,128)(2,1)} async-done(((bf16[1152,1024]{1,0:T(8,128)(2,1)}), bf16[4608,1024]{1,0:T(8,128)(2,1)}) %all-gather.13.cloned.1.call-update) | async-done | bytes 9437200 | tf_op jit(solution)/shard_map/all_gather | solution.py:64
  666.4 18.0 %multiply_convert_fusion.1 = (bf16[512,4608]{1,0:T(8,128)(2,1)}, bf16[512,4608]{1,0:T(8,128)(2,1)}, bf16[512,4608]{1,0:T(8,128)(2,1)}) fusion(f32[512,9216]{1,0:T(8,128)} %fusion.32, bf16[4608,1024]{1,0:T(8,128)(2,1)} %all-gather.13.cloned.1.call-done, bf16[1,512,1024]{2,1,0:T(8,128)(2,1)} %param.19), kind=kOutput, calls=%fused_computation.4 | convolution fusion | flops 4867227648 | bytes 43515904 | tf_op jit(solution)/shard_map/dot_general | solution.py:22
  684.3 16.0 multiply_reduce_fusion
  700.4 0.6 multiply_add_fusion
  701.0 1.0 copy-done.19
  702.0 1.3 fusion.21
  703.3 1.0 copy-done.4
  704.3 3.7 multiply_reduce_fusion.3
  708.1 0.9 copy.19
  709.1 4.5 convolution_convert_fusion.3
  713.6 1.5 copy-done.3
  715.7 2.6 collective-permute-start.1
  718.3 1.0 pad_add_fusion
  719.3 1.8 collective-permute-done.1
  721.1 0.8 multiply_convert_fusion.5
  722.0 0.9 copy-done.8
  723.3 5.9 convolution_convert_fusion.2
  729.2 1.1 copy-done.14
  730.4 9.8 convolution_convert_fusion.1
  740.3 1.5 copy-done.7
  741.8 17.2 convolution_convert_fusion
  759.0 0.6 copy-done.22
  759.6 0.6 dynamic-slice
  760.9 10.0 fusion.14
  770.9 8.0 fusion.12
  778.9 7.7 all-reduce.7
  786.7 3.1 fusion.16
  789.9 0.9 copy.20
  790.8 93.1 %reduce-scatter.8.cloned.1.call-done = bf16[256,3072]{1,0:T(8,128)(2,1)} async-done(((bf16[1024,3072]{1,0:T(8,128)(2,1)}), bf16[256,3072]{1,0:T(8,128)(2,1)}) %reduce-scatter.8.cloned.1.call-update) | async-done | bytes 1572880 | tf_op jit(solution)/shard_map/reduce_scatter | solution.py:158
  883.9 164.2 %reduce-scatter.14.cloned.1.call-done = bf16[1152,1024]{1,0:T(8,128)(2,1)} async-done(((bf16[4608,1024]{1,0:T(8,128)(2,1)}), bf16[1152,1024]{1,0:T(8,128)(2,1)}) %reduce-scatter.14.cloned.1.call-update) | async-done | bytes 2359312 | tf_op jit(solution)/shard_map/reduce_scatter | solution.py:173
  1048.1 317.3 %reduce-scatter.12.cloned.1.call-done = bf16[256,9216]{1,0:T(8,128)(2,1)} async-done(((bf16[1024,9216]{1,0:T(8,128)(2,1)}), bf16[256,9216]{1,0:T(8,128)(2,1)}) %reduce-scatter.12.cloned.1.call-update) | async-done | bytes 4718608 | tf_op jit(solution)/shard_map/reduce_scatter | solution.py:170
  1365.4 360.4 %all-reduce.9 = (f32[256]{0:T(256)}, f32[256,3072]{1,0:T(8,128)}, f32[256,3]{0,1:T(4,128)}, f32[256,1024]{1,0:T(8,128)}, f32[256]{0:T(256)}, /*index=5*/f32[256,9216]{1,0:T(8,128)}, f32[1152,1024]{1,0:T(8,128)}) all-reduce(f32[256]{0:T(256)S(1)} %get-tuple-element.47, ...), channel_id=1, replica_groups=mesh['seq'=8,'wsh'=4] {'seq'}, use_global_device_ids=true, to_apply=%region_6.0 | all-reduce | flops 4588800 | bytes 27533824 | tf_op jit(solution)/shard_map/psum | solution.py:177
  (88 shorter events, 2.6 us)
Async XLA Ops:
  7.2 3.5 copy-start.12
  7.2 121.4 %all-gather.7.cloned.1.call-start = ((), (), s32[]{:S(2)}) async-start(), calls=%async_computation.5 | async-start | bytes 7864320 | tf_op jit(solution)/shard_map/all_gather | solution.py:59
  10.6 164.1 %all-gather.9.cloned.1.call-start = ((), (), s32[]{:S(2)}) async-start(), calls=%async_computation.6 | async-start | bytes 2621440 | tf_op jit(solution)/shard_map/all_gather | solution.py:61
  11.5 486.9 %all-gather.11.cloned.1.call-start = ((), (), s32[]{:S(2)}) async-start(), calls=%async_computation.7 | async-start | bytes 23592960 | tf_op jit(solution)/shard_map/all_gather | solution.py:63
  18.1 648.2 %all-gather.13.cloned.1.call-start = ((), (), s32[]{:S(2)}) async-start(), calls=%async_computation.8 | async-start | bytes 11796480 | tf_op jit(solution)/shard_map/all_gather | solution.py:64
  22.6 0.7 copy-start.20
  22.6 13.1 copy-start.17
  22.6 23.0 %copy-start.5 = (bf16[1,512,1024]{2,1,0:T(8,128)(2,1)S(1)}, bf16[1,512,1024]{2,1,0:T(8,128)(2,1)}, u32[]{:S(2)}) copy-start(bf16[1,512,1024]{2,1,0:T(8,128)(2,1)} %param.10) | copy-start | bytes 3145732
  22.7 767.2 %reduce-scatter.16.cloned.1.call-start = ((), (), s32[]{:S(2)}) async-start(), calls=%async_computation.13 | async-start | bytes 327680
  134.3 10.6 copy-start
  134.3 3.8 copy-start.18
  134.3 3.8 copy-start.21
  134.7 9.9 collective-permute-start
  684.3 16.1 copy-start.6
  684.3 16.1 copy-start.13
  700.4 1.6 copy-start.19
  702.0 1.3 copy-start.1
  702.0 2.3 copy-start.4
  709.0 81.8 %reduce-scatter.10.cloned.1.call-start = ((), (), s32[]{:S(2)}) async-start(), calls=%async_computation.10 | async-start | bytes 2621440 | tf_op jit(solution)/shard_map/reduce_scatter | solution.py:164
  713.6 1.6 copy-start.3
  713.6 170.3 %reduce-scatter.8.cloned.1.call-start = ((), (), s32[]{:S(2)}) async-start(), calls=%async_computation.9 | async-start | bytes 7864320 | tf_op jit(solution)/shard_map/reduce_scatter | solution.py:158
  715.7 5.4 slice-start
  715.7 5.4 slice-start.1
  715.7 5.4 collective-permute-start.1
  719.3 4.0 copy-start.15
  722.0 1.0 copy-start.8
  722.0 1.3 copy-start.10
  729.2 1.2 copy-start.14
  729.2 319.0 %reduce-scatter.14.cloned.1.call-start = ((), (), s32[]{:S(2)}) async-start(), calls=%async_computation.12 | async-start | bytes 11796480 | tf_op jit(solution)/shard_map/reduce_scatter | solution.py:173
  740.2 1.6 copy-start.7
  740.2 625.2 %reduce-scatter.12.cloned.1.call-start = ((), (), s32[]{:S(2)}) async-start(), calls=%async_computation.11 | async-start | bytes 23592960 | tf_op jit(solution)/shard_map/reduce_scatter | solution.py:170
  759.0 0.7 copy-start.22
  760.9 10.0 copy-start.9
  760.9 10.0 copy-start.11
  760.9 10.0 copy-start.16
  770.9 15.8 copy-start.2
Sparse Core Ops, SparseCore 0:
  10.7 117.7 all-gather.6
  130.7 43.9 all-gather.8
  176.9 321.5 all-gather.10
  500.5 165.8 all-gather.12
  709.1 15.9 reduce-scatter.15
  727.4 43.6 reduce-scatter.9
  773.4 110.4 reduce-scatter.7
  886.8 161.2 reduce-scatter.13
  1050.5 314.8 reduce-scatter.11
where the time goes:
time: 1740 us; the launch traced here: 1730 us
  waiting for transfers between devices  1160 us (67%)
  blocking collectives  397 us (23%)
  matrix products  119 us (7%)
  other arithmetic  28.5 us (2%)
    psum x1, blocking collectives, local(): lax.psum((shards[0], shards[1], shards[2], shards[3], shards[4], shards[5...  360 us
    all_gather x1, waiting for transfers between devices, local(): lax.all_gather(copies[5], 'wsh', axis=0, tiled=True)  319 us
    reduce_scatter x1, waiting for transfers between devices, local(): lax.psum_scatter(grad_gu.astype(jnp.bfloat16), 'wsh', scatter_dimension=0...  317 us
    reduce_scatter x1, waiting for transfers between devices, local(): lax.psum_scatter(grad_down.astype(jnp.bfloat16), 'wsh', scatter_dimension...  164 us
    all_gather x1, waiting for transfers between devices, local(): lax.all_gather(copies[6], 'wsh', axis=0, tiled=True)  150 us
    reduce_scatter x1, waiting for transfers between devices, local(): lax.psum_scatter(grad_inw.astype(jnp.bfloat16), 'wsh', scatter_dimension=...  93.1 us
    all_gather x1, waiting for transfers between devices, local(): lax.all_gather(copies[1], 'wsh', axis=0, tiled=True)  82.7 us
    dot_general x4, matrix products, outer(): lax.dot_general(left, right, (((1,), (1,)), ((), ())), preferred_element_...  43.3 us
  transfers between devices with their start and end apart: 11, of which 8 were waited for; matrix products, arithmetic and copies ran while one was open for 6% of the time, Pallas kernels for 0%

commit v1 on v0

v1 whole, which is shorter than its diff:
```python
import jax
import jax.numpy as jnp
from jax import lax
from jax.sharding import PartitionSpec as P

epsilon = 1e-06
low = jnp.bfloat16
full = jnp.float32


def inner(left, right):
    return lax.dot_general(left, right, (((0,), (0,)), ((), ())), preferred_element_type=full)


def outer(left, right):
    return lax.dot_general(left, right, (((1,), (1,)), ((), ())), preferred_element_type=full)


def plain(left, right):
    return jnp.dot(left, right, preferred_element_type=full)


def build(seq, wsh):
    def flip(value, bit):
        return lax.ppermute(value, "seq", [(i, i ^ (1 << bit)) for i in range(seq)])

    def zflip(value, mask):
        return lax.ppermute(value, "wsh", [(i, i ^ mask) for i in range(wsh)])

    def chosen(value, pairs):
        return lax.ppermute(
            value, ("seq", "wsh"), [(a * wsh + b, c * wsh + d) for (a, b), (c, d) in pairs]
        )

    def take(buf, at):
        start, size = [], []
        for dim in range(buf.ndim):
            index = at[dim] if dim < len(at) else None
            start.append(0 if index is None else index)
            size.append(buf.shape[dim] if index is None else 1)
        return lax.dynamic_slice(buf, start, size)

    def put(buf, value, at):
        start = [
            0 if dim >= len(at) or at[dim] is None else at[dim] for dim in range(buf.ndim)
        ]
        return lax.dynamic_update_slice(buf, value, start)

    def local(
        tokens,
        doc_start,
        norm1_gain,
        in_weight,
        conv_weight,
        out_weight,
        norm2_gain,
        gate_up_weight,
        down_weight,
        out_grad,
    ):
        me = lax.axis_index("seq")
        z = lax.axis_index("wsh")
        core, xbit, ybit = me % 2, (me // 2) % 2, (me // 4) % 2
        quarter = me % 4
        cot = out_grad[0]
        rows, width = cot.shape
        part = width // wsh
        hidden = down_weight.shape[0] * wsh
        hq = hidden // 4

        def by_z(value):
            return jnp.concatenate(
                [lax.dynamic_slice_in_dim(value, (z ^ j) * part, part, 1) for j in range(wsh)], 1
            )

        extra = jnp.concatenate(
            [norm1_gain[:, None], norm2_gain[:, None], conv_weight], 1
        ).astype(low)
        extra = jnp.pad(extra, ((0, 0), (0, 128 - extra.shape[1])))
        shard_a = in_weight[:, : 2 * width].astype(low)
        shard_b = jnp.concatenate(
            [in_weight[:, 2 * width :].astype(low), out_weight.astype(low), extra], 1
        )

        def gather_conv(shard, order):
            cols = shard.shape[1]
            buf = jnp.zeros((2, 2, 2, 2, 2, part // 8, cols), low)
            buf = put(buf, shard.reshape(1, 1, 2, 2, 2, part // 8, cols), ())
            got = zflip(take(buf, (0, 0, ybit, xbit, core)), 2)
            buf = put(buf, got, (1, 0, ybit, xbit, core))
            got = zflip(take(buf, (None, 0, ybit, xbit, core)), 1)
            buf = put(buf, got, (None, 1, ybit, xbit, core))
            buf = buf.reshape(4, 2, 2, 2, part // 8, cols)
            away = buf[1:]
            for step in order:
                index = [None, ybit, xbit, core]
                for done in order[: order.index(step)]:
                    index[{2: 1, 1: 2, 0: 3}[done]] = None
                got = flip(take(away, index), step)
                spot = {2: 1, 1: 2, 0: 3}[step]
                index[spot] = 1 - index[spot]
                away = put(away, got, index)
            return jnp.concatenate([shard, away.reshape(3 * part, cols)], 0)

        w_a = gather_conv(shard_a, (1, 2, 0))
        w_b = gather_conv(shard_b, (2, 1, 0))
        w_x = w_b[:, :width]
        w_out = w_b[:, width : 2 * width]
        small = w_b[:, 2 * width : 2 * width + 8].astype(full).T
        gain_one, gain_two = small[0:1], small[1:2]
        taps = [by_z(small[k : k + 1]) for k in (2, 3, 4)]

        def gather_group(value):
            pair = jnp.concatenate([value, flip(value, 1)], 0)
            return jnp.concatenate([pair, flip(pair, 0)], 0)

        cot_all = gather_group(cot)

        gate_up = jnp.concatenate(
            [
                lax.dynamic_slice_in_dim(gate_up_weight, quarter * hq, hq, 1),
                lax.dynamic_slice_in_dim(gate_up_weight, hidden + quarter * hq, hq, 1),
            ],
            1,
        ).astype(low)
        buf = jnp.zeros((2, 2, 2, part // 2, 2 * hq), low)
        buf = put(buf, gate_up.reshape(1, 1, 2, part // 2, 2 * hq), ())
        buf = put(buf, zflip(take(buf, (0, 0, ybit)), 2), (1, 0, ybit))
        buf = put(buf, zflip(take(buf, (None, 0, ybit)), 1), (None, 1, ybit))
        buf = buf.reshape(4, 2, part // 2, 2 * hq)
        away = put(buf[1:], flip(take(buf[1:], (None, ybit)), 2), (None, 1 - ybit))
        w_gu = jnp.concatenate([gate_up, away.reshape(3 * part, 2 * hq)], 0)

        halves = down_weight.astype(low).reshape(2, hq // 2, width)
        half = take(halves, (ybit,))
        got = chosen(half, [((s, s % 4), (s, s % 4 ^ 2)) for s in range(seq)])
        half = jnp.where((z ^ quarter) == 2, got, half)
        got = chosen(
            half, [((s, s % 4 ^ m), (s, s % 4 ^ m ^ 1)) for s in range(seq) for m in (0, 2)]
        )
        half = jnp.where((z ^ quarter) % 2 == 1, got, half)
        other = flip(half, 2)
        w_down = put(put(halves, half, (ybit,)), other, (1 - ybit,)).reshape(hq, width)

        xf = tokens[0].astype(full)
        starts = doc_start[0]
        rate_one = lax.rsqrt(jnp.mean(xf * xf, axis=-1, keepdims=True) + epsilon)
        normed = xf * rate_one
        normed_z = by_z(normed)
        h = (normed_z * gain_one).astype(low)
        proj_a = plain(h, w_a)
        bpart, cpart = proj_a[:, :width], proj_a[:, width:]
        xpart = plain(h, w_x)
        gated = (bpart * xpart).astype(low)
        edge = lax.ppermute(gated[rows - 2 :], "seq", [(i, i + 1) for i in range(seq - 1)])
        extended = jnp.concatenate([edge, gated], 0).astype(full)
        place = me * rows + jnp.arange(rows, dtype=jnp.int32)
        keep_one = (place - 1 >= starts).astype(full)[:, None]
        keep_two = (place - 2 >= starts).astype(full)[:, None]
        current = extended[2:]
        lag_one = extended[1:-1]
        lag_two = extended[:-2]
        mixed = taps[0] * current + keep_one * taps[1] * lag_one + keep_two * taps[2] * lag_two
        zed = by_z((cpart * mixed).astype(low))
        first = xf + plain(zed, w_out)
        rate_two = lax.rsqrt(jnp.mean(first * first, axis=-1, keepdims=True) + epsilon)
        normed_two = by_z(first * rate_two)
        second = (normed_two * gain_two).astype(low)

        second_all = gather_group(second)
        both = plain(second_all, w_gu)
        gate, upper = both[:, :hq], both[:, hq:]
        sigma = jax.nn.sigmoid(gate)
        swish = gate * sigma
        act = (swish * upper).astype(low)
        grad_act = outer(cot_all, w_down)
        grad_gate = grad_act * upper * (sigma * (1.0 + gate * (1.0 - sigma)))
        grad_both = jnp.concatenate([grad_gate, grad_act * swish], 1).astype(low)

        def scatter_group(value):
            mine, theirs = value[: 2 * rows], value[2 * rows :]
            mine = mine + flip(theirs.astype(low), 0).astype(full)
            return mine[:rows] + flip(mine[rows:].astype(low), 1).astype(full)

        result = first + scatter_group(plain(act, w_down))
        grad_second = scatter_group(outer(grad_both, w_gu))
        grad_down = inner(act, cot_all).astype(low)
        grad_gu = inner(second_all, grad_both).astype(low)

        def plus(a, b):
            return (a.astype(full) + b.astype(full)).astype(low)

        def upper_bits(value):
            for bit in range(3, seq.bit_length() - 1):
                value = plus(value, flip(value, bit))
            return value

        buf = grad_gu.reshape(4, 2, part // 2, 2 * hq)
        buf = plus(take(buf, (None, ybit)), flip(take(buf, (None, 1 - ybit)), 2))
        buf = buf.reshape(2, 2, part // 2, 2 * hq)
        buf = plus(buf[:, 0], zflip(buf[:, 1], 1))
        buf = upper_bits(plus(buf[0], zflip(buf[1], 2)))

        def spread_gu(piece, order):
            home = jnp.zeros((2, 2, 2, part // 2, hq), low)
            index = [xbit, core, ybit]
            home = put(home, piece.reshape(1, 1, 1, part // 2, hq), index)
            for step in order:
                got = flip(take(home, index), step)
                spot = {1: 0, 0: 1, 2: 2}[step]
                index[spot] = 1 - index[spot]
                home = put(home, got, index)
                index[spot] = None
            home = home.reshape(4, part, hq)
            return jnp.concatenate([home[i] for i in range(4)], 1)

        total_gu = jnp.concatenate(
            [spread_gu(buf[:, :hq], (1, 2, 0)), spread_gu(buf[:, hq:], (2, 1, 0))], 1
        ).astype(full)

        buf = grad_down.reshape(2, hq // 2, width)
        half = plus(take(buf, (ybit,)), flip(take(buf, (1 - ybit,)), 2))
        half = plus(
            half,
            chosen(
                half, [((s, s % 4 ^ m ^ 1), (s, s % 4 ^ m)) for s in range(seq) for m in (0, 2)]
            ),
        )
        half = plus(half, chosen(half, [((s, s % 4 ^ 2), (s, s % 4)) for s in range(seq)]))
        half = upper_bits(half)
        got = chosen(half, [((s, s % 4), (s ^ 2, s % 4)) for s in range(seq)])
        half = jnp.where(quarter == z, half, got)
        evens = [(s, b) for s in range(seq) for b in range(wsh) if (s ^ b) % 2 == 0]
        other = chosen(half, [((s, b), (s ^ 4, b)) for s, b in evens])
        home = put(put(jnp.zeros((2, hq // 2, width), low), half, (ybit,)), other, (1 - ybit,))
        got = chosen(home, [((s, b), (s ^ 1, b)) for s, b in evens])
        total_down = jnp.where((me ^ z) % 2 == 0, home, got).reshape(hq, width).astype(full)

        grad_gain_two = jnp.sum(grad_second * normed_two, axis=0)
        scaled_two = grad_second * gain_two
        grad_first = cot.astype(full) + by_z(
            rate_two
            * (scaled_two - normed_two * jnp.mean(scaled_two * normed_two, axis=-1, keepdims=True))
        )
        grad_branch = grad_first.astype(low)
        grad_outw = inner(zed, grad_branch)
        grad_zed = by_z(outer(grad_branch, w_out))
        grad_cpart = grad_zed * mixed
        grad_mixed = grad_zed * cpart
        term_one = keep_one * grad_mixed
        term_two = keep_two * grad_mixed
        grad_taps = [
            jnp.sum(grad_mixed * current, axis=0),
            jnp.sum(term_one * lag_one, axis=0),
            jnp.sum(term_two * lag_two, axis=0),
        ]
        grad_ext = jnp.pad(taps[0] * grad_mixed, ((2, 0), (0, 0)))
        grad_ext = grad_ext + jnp.pad(taps[1] * term_one, ((1, 1), (0, 0)))
        grad_ext = grad_ext + jnp.pad(taps[2] * term_two, ((0, 2), (0, 0)))
        returned = lax.ppermute(grad_ext[:2], "seq", [(i + 1, i) for i in range(seq - 1)])
        grad_gated = grad_ext[2:] + jnp.pad(returned, ((rows - 2, 0), (0, 0)))
        grad_proj = jnp.concatenate(
            [grad_gated * xpart, grad_cpart, grad_gated * bpart], 1
        ).astype(low)
        grad_a = inner(h, grad_proj[:, : 2 * width]).astype(low)
        grad_x = inner(h, grad_proj[:, 2 * width :])
        grad_normed = outer(grad_proj[:, : 2 * width], w_a) + outer(
            grad_proj[:, 2 * width :], w_x
        )
        grad_gain_one = jnp.sum(grad_normed * normed_z, axis=0)
        scaled_one = grad_normed * gain_one
        grad_input = grad_first + by_z(
            rate_one
            * (scaled_one - normed_z * jnp.mean(scaled_one * normed_z, axis=-1, keepdims=True))
        )
        tail = jnp.stack(
            [grad_gain_one, grad_gain_two] + [by_z(g[None])[0] for g in grad_taps], 1
        )
        tail = jnp.pad(tail, ((0, 0), (0, 128 - tail.shape[1])))
        grad_b = jnp.concatenate([grad_x, grad_outw, tail], 1).astype(low)

        def sum_conv(value, order):
            cols = value.shape[1]
            where = {2: 1, 1: 2, 0: 3}
            buf = value.reshape(4, 2, 2, 2, part // 8, cols)
            mine = {2: ybit, 1: xbit, 0: core}
            for step in (0,) + order:
                send, keep = [None] * 4, [None] * 4
                send[where[step]], keep[where[step]] = 1 - mine[step], mine[step]
                if buf.shape[where[step]] == 1:
                    raise ValueError
                got = flip(take(buf, send), step)
                buf = plus(take(buf, keep), got)
            buf = buf.reshape(2, 2, part // 8, cols)
            buf = plus(buf[:, 0], zflip(buf[:, 1], 1))
            buf = upper_bits(plus(buf[0], zflip(buf[1], 2)))
            home = jnp.zeros((2, 2, 2, part // 8, cols), low)
            index = [ybit, xbit, core]
            home = put(home, buf.reshape(1, 1, 1, part // 8, cols), index)
            for step in order[::-1] + (0,):
                got = flip(take(home, index), step)
                spot = where[step] - 1
                index[spot] = 1 - index[spot]
                home = put(home, got, index)
                index[spot] = None
            return home.reshape(part, cols).astype(full)

        total_a = sum_conv(grad_a, (1, 2))
        total_b = sum_conv(grad_b, (2, 1))
        tail = total_b[:, 2 * width :]
        return (
            result.astype(low)[None],
            grad_input.astype(low)[None],
            tail[:, 0],
            jnp.concatenate([total_a, total_b[:, :width]], 1),
            tail[:, 2:5],
            total_b[:, width : 2 * width],
            tail[:, 1],
            total_gu,
            total_down,
        )

    return local


def solution(mesh):
    in_specs = (
        P("wsh", "seq", None),
        P("wsh", "seq"),
        P("wsh"),
        P("wsh", None),
        P("wsh", None),
        P("wsh", None),
        P("wsh"),
        P("wsh", None),
        P("wsh", None),
        P("wsh", "seq", None),
    )
    out_specs = (
        P("wsh", "seq", None),
        P("wsh", "seq", None),
        P("wsh"),
        P("wsh", None),
        P("wsh", None),
        P("wsh", None),
        P("wsh"),
        P("wsh", None),
        P("wsh", None),
    )
    local = build(mesh.shape["seq"], mesh.shape["wsh"])
    return jax.shard_map(local, mesh=mesh, in_specs=in_specs, out_specs=out_specs, check_vma=False)
```

time: 1740 us -> 597 us (0.34)
  waiting for transfers between devices: 1160 us -> 186 us
  blocking collectives: 397 us -> 0 us
  starting transfers between devices: 6.43 us -> 133 us
  local copies, waits for them, and re-layouts: 11.3 us -> 94.7 us
  other arithmetic: 28.5 us -> 65.4 us
    all_gather x4 -> x0, waiting for transfers between devices: 579 us -> none  [the longest x1 319 us: local(): lax.all_gather(copies[5], 'wsh', axis=0, tiled=True)]
    reduce_scatter x4 -> x0, waiting for transfers between devices: 575 us -> none  [the longest x1 317 us: local(): lax.psum_scatter(grad_gu.astype(jnp.bfloat16), 'wsh', scatter_dimension=0...]
    psum x1 -> x0, blocking collectives: 360 us -> none  [local(): lax.psum((shards[0], shards[1], shards[2], shards[3], shards[4], shards[5...]
    ppermute x2 -> x57, waiting for transfers between devices: 1.8 us -> 186 us  [the longest x36 138 us: flip(): return lax.ppermute(value, 'seq', [(i, i ^ 1 << bit) for i in range(seq)])]
    ppermute x2 -> x57, starting transfers between devices: 6.05 us -> 133 us  [the longest x36 58.1 us: flip(): return lax.ppermute(value, 'seq', [(i, i ^ 1 << bit) for i in range(seq)])]
    dynamic_slice x0 -> x65, local copies, waits for them, and re-layouts: none -> 30 us  [the longest x31 17.3 us: by_z(): lax.dynamic_slice_in_dim(value, (z ^ j) * part, part, 1)]
    all_gather x3 -> x0, blocking collectives: 28.6 us -> none  [the longest x1 12.4 us: local(): lax.all_gather(copies[0], 'wsh', axis=0, tiled=True)]
    dot_general x4 -> x5, matrix products: 37.4 us -> 30.8 us  [inner(): lax.dot_general(left, right, (((0,), (0,)), ((), ())), preferred_element_...]
  transfers between devices with their start and end apart: 11 -> 57, of which waited for: 8 -> 23; matrix products, arithmetic and copies ran while one was open for 6% -> 34% of each run, Pallas kernels for 0% -> 0%
where the time goes in v1:
time: 597 us; the launch traced here: 588 us
  waiting for transfers between devices  186 us (31%)
  starting transfers between devices  133 us (22%)
  matrix products  106 us (18%)
  local copies, waits for them, and re-layouts  94.7 us (16%)
  other arithmetic  65.4 us (11%)
    ppermute x36, waiting for transfers between devices, flip(): return lax.ppermute(value, 'seq', [(i, i ^ 1 << bit) for i in range(seq)])  138 us
    ppermute x36, starting transfers between devices, flip(): return lax.ppermute(value, 'seq', [(i, i ^ 1 << bit) for i in range(seq)])  58.1 us
    ppermute x12, starting transfers between devices, zflip(): return lax.ppermute(value, 'wsh', [(i, i ^ mask) for i in range(wsh)])  54.9 us
    ppermute x12, waiting for transfers between devices, zflip(): return lax.ppermute(value, 'wsh', [(i, i ^ mask) for i in range(wsh)])  47.6 us
    dot_general x5, matrix products, outer(): lax.dot_general(left, right, (((1,), (1,)), ((), ())), preferred_element_...  40.4 us
    dot_general x5, matrix products, plain(): return jnp.dot(left, right, preferred_element_type=full)  34.8 us
    dot_general x5, matrix products, inner(): lax.dot_general(left, right, (((0,), (0,)), ((), ())), preferred_element_...  30.8 us
    unnamed x187, local copies, waits for them, and re-layouts  26.9 us
  transfers between devices with their start and end apart: 57, of which 23 were waited for; matrix products, arithmetic and copies ran while one was open for 34% of the time, Pallas kernels for 0%

profile of v1, /device:TPU:1, one launch (start us, length us, event | category | flops | bytes accessed | tf_op | source)
XLA Modules:
  0.0 588.0 jit_solution(9898186809981619017)
XLA Ops:
  5.5 3.1 collective-permute-start
  32.0 16.8 %collective-permute-start.6 = (bf16[2,1,1,1,1,32,2048]{6,5,4,3,2,1,0:T(8,128)(2,1)S(1)}, bf16[2,1,1,1,1,32,2048]{6,5,4,3,2,1,0:T(8,128)(2,1)S(1)}, u32[]{:S(2)}, u32[]{:S(2)}) collective-permute-start(bf16[2,1,1,1,1,32,2048]{6,5,4,3,2,1,0:T(8,128)(2,1)S(1)} %constant_dynamic-slice_fusion.55), channel_id=1, source_target_pairs={{0,1},{1,0},{2,3},{3,2},{4,5},{5,4},{6,7},{7,6},{8,9},{9,8},{10,11... | collective-permute-start | bytes 786440 | tf_op jit(solution)/shard_map/ppermute | solution.py:28
  50.6 4.4 collective-permute-done.6
  58.2 2.8 collective-permute-done.1
  68.8 7.9 %collective-permute-done.8 = bf16[3,1,2,1,32,2048]{5,4,3,2,1,0:T(8,128)(2,1)S(1)} collective-permute-done((bf16[3,1,2,1,32,2048]{5,4,3,2,1,0:T(8,128)(2,1)S(1)}, bf16[3,1,2,1,32,2048]{5,4,3,2,1,0:T(8,128)(2,1)S(1)}, u32[]{:S(2)}, u32[]{:S(2)}) %collective-permute-start.8) | collective-permute-done | bytes 786464 | tf_op jit(solution)/shard_map/ppermute | solution.py:25
  77.0 21.2 %collective-permute-start.9 = (bf16[3,2,2,1,32,2048]{5,4,3,2,1,0:T(8,128)(2,1)S(1)}, bf16[3,2,2,1,32,2048]{5,4,3,2,1,0:T(8,128)(2,1)S(1)}, u32[]{:S(2)}, u32[]{:S(2)}) collective-permute-start(bf16[3,2,2,1,32,2048]{5,4,3,2,1,0:T(8,128)(2,1)S(1)} %constant_dynamic-slice_fusion.52), channel_id=1, source_target_pairs={{0,4},{4,0},{8,12},{12,8},{16,20},{20,16},{24,28},{28,24},{1,5},{5... | collective-permute-start | bytes 4718600 | tf_op jit(solution)/shard_map/ppermute | solution.py:25
  98.5 3.0 collective-permute-start.4
  128.7 3.7 fusion.11
  135.0 3.0 collective-permute-start.10
  154.3 15.0 %collective-permute-done.11 = bf16[512,1024]{1,0:T(8,128)(2,1)S(1)} collective-permute-done((bf16[512,1024]{1,0:T(8,128)(2,1)S(1)}, bf16[512,1024]{1,0:T(8,128)(2,1)S(1)}, u32[]{:S(2)}, u32[]{:S(2)}) %collective-permute-start.11) | collective-permute-done | bytes 1048608 | tf_op jit(solution)/shard_map/ppermute | solution.py:25
  176.3 20.8 %collective-permute-done.21 = bf16[512,1024]{1,0:T(8,128)(2,1)} collective-permute-done((bf16[512,1024]{1,0:T(8,128)(2,1)}, bf16[512,1024]{1,0:T(8,128)(2,1)}, u32[]{:S(2)}, u32[]{:S(2)}) %collective-permute-start.21) | collective-permute-done | bytes 1048608 | tf_op jit(solution)/shard_map/ppermute | solution.py:25
  201.9 11.3 %collective-permute-done.18 = bf16[1,576,1024]{2,1,0:T(8,128)(2,1)S(1)} collective-permute-done((bf16[1,576,1024]{2,1,0:T(8,128)(2,1)S(1)}, bf16[1,576,1024]{2,1,0:T(8,128)(2,1)S(1)}, u32[]{:S(2)}, u32[]{:S(2)}) %collective-permute-start.18) | collective-permute-done | bytes 1179680 | tf_op jit(solution)/shard_map/ppermute | solution.py:25
  213.4 16.9 %fusion.18 = f32[2048,2304]{1,0:T(8,128)} fusion(bf16[768,2304]{1,0:T(8,128)(2,1)S(1)} %bitcast.219, bf16[256,1152]{1,0:T(8,128)(2,1)S(1)} %copy-done.54, bf16[256,1152]{1,0:T(8,128)(2,1)S(1)} %copy-done.51, bf16[1024,1024]{1,0:T(8,128)(2,1)} %collective-permute-done.12, bf16[512,1024]{1,0:T(8,128)(2,1)} %copy-done.66, bf16[512,1024]{1,0:T(8,128)(2,1)S(1)} %copy-done.48), kind=kOutput, calls=%fused_computation.91 | convolution fusion | flops 9690415104 | bytes 27787264 | tf_op jit(solution)/shard_map/dot_general | solution.py:20
  230.3 18.0 %multiply_convert_fusion.1 = (bf16[2048,1152]{1,0:T(8,128)(2,1)}, bf16[2048,1152]{1,0:T(8,128)(2,1)}, bf16[2048,1152]{1,0:T(8,128)(2,1)}) fusion(f32[2048,2304]{1,0:T(8,128)} %fusion.18, bf16[1152,1024]{1,0:T(8,128)(2,1)} %bitcast.213, bf16[1024,1024]{1,0:T(8,128)(2,1)} %collective-permute-done.22, bf16[512,1024]{1,0:T(8,128)(2,1)} %collective-permute-done.21, ...), kind=kOutput, calls=%fused_computation.7 | convolution fusion | flops 4879810560 | bytes 39583744 | tf_op jit(solution)/shard_map/dot_general | solution.py:16
  248.3 10.3 %fusion.67 = f32[2048,1024]{1,0:T(8,128)} fusion(bf16[2048,1152]{1,0:T(8,128)(2,1)} %get-tuple-element.65, bf16[1152,1024]{1,0:T(8,128)(2,1)} %bitcast.214), kind=kOutput, calls=%fused_computation.313 | convolution fusion | flops 4831838208 | bytes 15466496 | tf_op jit(solution)/shard_map/dot_general | solution.py:20
  258.6 7.2 %convolution_convert_fusion = bf16[1152,1024]{1,0:T(8,128)(2,1)S(1)} fusion(bf16[2048,1152]{1,0:T(8,128)(2,1)S(1)} %copy-done.84, bf16[1024,1024]{1,0:T(8,128)(2,1)} %collective-permute-done.22, bf16[512,1024]{1,0:T(8,128)(2,1)} %collective-permute-done.21, bf16[512,1024]{1,0:T(8,128)(2,1)} %bitcast.20), kind=kOutput, calls=%fused_computation.29 | convolution fusion | flops 4845600768 | bytes 11272192 | tf_op jit(solution)/shard_map/dot_general | solution.py:12
  267.0 14.5 %fusion.7 = f32[2048,1024]{1,0:T(8,128)} fusion(bf16[2048,1152]{1,0:T(8,128)(2,1)} %get-tuple-element.64, bf16[2048,1152]{1,0:T(8,128)(2,1)} %get-tuple-element.63, bf16[768,2304]{1,0:T(8,128)(2,1)S(1)} %bitcast.220, bf16[256,1152]{1,0:T(8,128)(2,1)S(1)} %copy-done.55, bf16[256,1152]{1,0:T(8,128)(2,1)S(1)} %copy-done.52), kind=kOutput, calls=%fused_computation.14 | convolution fusion | flops 9696706560 | bytes 22544384 | tf_op jit(solution)/shard_map/dot_general | solution.py:16
  281.5 3.8 slice.407
  285.4 6.8 %collective-permute-start.23 = (bf16[1024,1024]{1,0:T(8,128)(2,1)}, bf16[1024,1024]{1,0:T(8,128)(2,1)}, u32[]{:S(2)}, u32[]{:S(2)}) collective-permute-start(bf16[1024,1024]{1,0:T(8,128)(2,1)} %slice.407), channel_id=1, source_target_pairs={{0,4},{4,0},{8,12},{12,8},{16,20},{20,16},{24,28},{28,24},{1,5},{5... | collective-permute-start | bytes 6291464 | tf_op jit(solution)/shard_map/ppermute | solution.py:25
  292.2 3.8 slice.408
  296.1 14.5 %fusion.8 = bf16[1024,2304]{1,0:T(8,128)(2,1)S(1)} fusion(bf16[2048,1152]{1,0:T(8,128)(2,1)} %get-tuple-element.64, bf16[2048,1152]{1,0:T(8,128)(2,1)} %get-tuple-element.63, bf16[1024,1024]{1,0:T(8,128)(2,1)} %collective-permute-done.12, bf16[512,1024]{1,0:T(8,128)(2,1)} %copy-done.66, bf16[512,1024]{1,0:T(8,128)(2,1)S(1)} %copy-done.49), kind=kOutput, calls=%fused_computation.15 | convolution fusion | flops 9697492992 | bytes 18350080 | tf_op jit(solution)/shard_map/dot_general | solution.py:12
  315.8 6.0 %collective-permute-start.52 = (bf16[1,576,1024]{2,1,0:T(8,128)(2,1)}, bf16[1,576,1024]{2,1,0:T(8,128)(2,1)}, u32[]{:S(2)}, u32[]{:S(2)}) collective-permute-start(bf16[1,576,1024]{2,1,0:T(8,128)(2,1)} %add_convert_fusion.5), channel_id=1, source_target_pairs={{1,0},{3,2},{4,5},{6,7},{11,10},{9,8},{14,15},{12,13},{17,16},{19,... | collective-permute-start | bytes 3538952 | tf_op jit(solution)/shard_map/ppermute | solution.py:31
  326.5 3.6 slice_add_fusion
  331.9 3.6 slice_add_fusion.1
  335.8 3.1 add_convert_fusion.4
  340.7 25.6 %collective-permute-done.42 = bf16[4,1,128,2304]{3,2,1,0:T(8,128)(2,1)} collective-permute-done((bf16[4,1,128,2304]{3,2,1,0:T(8,128)(2,1)}, bf16[4,1,128,2304]{3,2,1,0:T(8,128)(2,1)}, u32[]{:S(2)}, u32[]{:S(2)}) %collective-permute-start.42) | collective-permute-done | bytes 2359328 | tf_op jit(solution)/shard_map/ppermute | solution.py:25
  371.0 3.1 collective-permute-start.43
  384.6 3.7 collective-permute-start.25
  389.9 4.0 convolution_convert_fusion.2
  407.7 3.9 multiply_reduce_fusion.4
  412.0 2.9 pad_maximum_fusion.6
  420.2 18.4 %collective-permute-start.44 = (bf16[128,2304]{1,0:T(8,128)(2,1)S(1)}, bf16[128,2304]{1,0:T(8,128)(2,1)S(1)}, u32[]{:S(2)}, u32[]{:S(2)}) collective-permute-start(bf16[128,2304]{1,0:T(8,128)(2,1)S(1)} %slice_bitcast_fusion.10), channel_id=1, source_target_pairs={{0,2},{1,3},{2,0},{3,1},{4,6},{5,7},{6,4},{7,5},{8,10},{9,11},{10,... | collective-permute-start | bytes 1769480 | tf_op jit(solution)/shard_map/ppermute | solution.py:28
  444.0 20.3 %collective-permute-done.44 = bf16[128,2304]{1,0:T(8,128)(2,1)S(1)} collective-permute-done((bf16[128,2304]{1,0:T(8,128)(2,1)S(1)}, bf16[128,2304]{1,0:T(8,128)(2,1)S(1)}, u32[]{:S(2)}, u32[]{:S(2)}) %collective-permute-start.44) | collective-permute-done | bytes 589856 | tf_op jit(solution)/shard_map/ppermute | solution.py:28
  466.3 6.8 %collective-permute-done.48 = bf16[1,1,1,128,1152]{4,3,2,1,0:T(8,128)(2,1)S(1)} collective-permute-done((bf16[1,1,1,128,1152]{4,3,2,1,0:T(8,128)(2,1)S(1)}, bf16[1,1,1,128,1152]{4,3,2,1,0:T(8,128)(2,1)S(1)}, u32[]{:S(2)}, u32[]{:S(2)}) %collective-permute-start.48) | collective-permute-done | bytes 294944 | tf_op jit(solution)/shard_map/ppermute | solution.py:25
  476.5 10.4 %collective-permute-done.49 = bf16[1,1,2,128,1152]{4,3,2,1,0:T(8,128)(2,1)S(1)} collective-permute-done((bf16[1,1,2,128,1152]{4,3,2,1,0:T(8,128)(2,1)S(1)}, bf16[1,1,2,128,1152]{4,3,2,1,0:T(8,128)(2,1)S(1)}, u32[]{:S(2)}, u32[]{:S(2)}) %collective-permute-start.49) | collective-permute-done | bytes 589856 | tf_op jit(solution)/shard_map/ppermute | solution.py:25
  498.0 4.9 convert_element_type.376
  502.8 13.7 %collective-permute-done.35 = bf16[4,2,1,1,32,2048]{5,4,3,2,1,0:T(8,128)(2,1)S(1)} collective-permute-done((bf16[4,2,1,1,32,2048]{5,4,3,2,1,0:T(8,128)(2,1)S(1)}, bf16[4,2,1,1,32,2048]{5,4,3,2,1,0:T(8,128)(2,1)S(1)}, u32[]{:S(2)}, u32[]{:S(2)}) %collective-permute-start.35) | collective-permute-done | bytes 1048608 | tf_op jit(solution)/shard_map/ppermute | solution.py:25
  517.4 3.5 collective-permute-done.27
  522.2 10.0 %collective-permute-done.36 = bf16[4,1,1,1,32,2048]{5,4,3,2,1,0:T(8,128)(2,1)S(1)} collective-permute-done((bf16[4,1,1,1,32,2048]{5,4,3,2,1,0:T(8,128)(2,1)S(1)}, bf16[4,1,1,1,32,2048]{5,4,3,2,1,0:T(8,128)(2,1)S(1)}, u32[]{:S(2)}, u32[]{:S(2)}) %collective-permute-start.36) | collective-permute-done | bytes 524320 | tf_op jit(solution)/shard_map/ppermute | solution.py:25
  532.3 4.1 collective-permute-start.37
  536.5 4.0 collective-permute-done.37
  540.6 5.3 collective-permute-start.38
  547.1 4.8 collective-permute-done.38
  552.2 3.3 collective-permute-done.29
  556.3 7.9 %collective-permute-done.30 = bf16[32,2176]{1,0:T(8,128)(2,1)S(1)} collective-permute-done((bf16[32,2176]{1,0:T(8,128)(2,1)S(1)}, bf16[32,2176]{1,0:T(8,128)(2,1)S(1)}, u32[]{:S(2)}, u32[]{:S(2)}) %collective-permute-start.30) | collective-permute-done | bytes 139296 | tf_op jit(solution)/shard_map/ppermute | solution.py:28
  568.6 5.2 collective-permute-done.40
  576.4 2.9 collective-permute-start.33
  579.9 2.9 bitcast_convert_fusion
  (475 shorter events, 188.2 us)
Async XLA Ops:
  5.5 43.3 %collective-permute-start = (bf16[1,1,1,1,1,32,2176]{6,5,4,3,2,1,0:T(8,128)(2,1)S(1)}, bf16[1,1,1,1,1,32,2176]{6,5,4,3,2,1,0:T(8,128)(2,1)S(1)}, u32[]{:S(2)}, u32[]{:S(2)}) collective-permute-start(bf16[1,1,1,1,1,32,2176]{6,5,4,3,2,1,0:T(8,128)(2,1)S(1)} %pad_dynamic-slice_fusion), channel_id=1, source_target_pairs={{0,2},{1,3},{2,0},{3,1},{4,6},{5,7},{6,4},{7,5},{8,10},{9,11},{10,... | collective-permute-start | bytes 417800 | tf_op jit(solution)/shard_map/ppermute | solution.py:28
  10.0 20.4 %collective-permute-start.5 = (bf16[1,1,1,1,1,32,2048]{6,5,4,3,2,1,0:T(8,128)(2,1)S(1)}, bf16[1,1,1,1,1,32,2048]{6,5,4,3,2,1,0:T(8,128)(2,1)S(1)}, u32[]{:S(2)}, u32[]{:S(2)}) collective-permute-start(bf16[1,1,1,1,1,32,2048]{6,5,4,3,2,1,0:T(8,128)(2,1)S(1)} %pad_dynamic-slice_fusion.1), channel_id=1, source_target_pairs={{0,2},{1,3},{2,0},{3,1},{4,6},{5,7},{6,4},{7,5},{8,10},{9,11},{10,... | collective-permute-start | bytes 393224 | tf_op jit(solution)/shard_map/ppermute | solution.py:28
  16.2 86.9 %collective-permute-start.13 = (bf16[1,1,1,128,2304]{4,3,2,1,0:T(8,128)(2,1)}, bf16[1,1,1,128,2304]{4,3,2,1,0:T(8,128)(2,1)}, u32[]{:S(2)}, u32[]{:S(2)}) collective-permute-start(bf16[1,1,1,128,2304]{4,3,2,1,0:T(8,128)(2,1)} %constant_dynamic-slice_fusion.31), channel_id=1, source_target_pairs={{0,2},{1,3},{2,0},{3,1},{4,6},{5,7},{6,4},{7,5},{8,10},{9,11},{10,... | collective-permute-start | bytes 1769480 | tf_op jit(solution)/shard_map/ppermute | solution.py:28
  23.6 122.7 %collective-permute-start.16 = (bf16[1,576,1024]{2,1,0:T(8,128)(2,1)}, bf16[1,576,1024]{2,1,0:T(8,128)(2,1)}, u32[]{:S(2)}, u32[]{:S(2)}) collective-permute-start(bf16[1,576,1024]{2,1,0:T(8,128)(2,1)} %constant_dynamic-slice_fusion.28), channel_id=1, source_target_pairs={{0,2},{5,7},{10,8},{15,13},{16,18},{21,23},{26,24},{31,29}} | collective-permute-start | bytes 3538952 | tf_op jit(solution)/shard_map/ppermute | solution.py:31
  32.0 23.0 %collective-permute-start.6 = (bf16[2,1,1,1,1,32,2048]{6,5,4,3,2,1,0:T(8,128)(2,1)S(1)}, bf16[2,1,1,1,1,32,2048]{6,5,4,3,2,1,0:T(8,128)(2,1)S(1)}, u32[]{:S(2)}, u32[]{:S(2)}) collective-permute-start(bf16[2,1,1,1,1,32,2048]{6,5,4,3,2,1,0:T(8,128)(2,1)S(1)} %constant_dynamic-slice_fusion.55), channel_id=1, source_target_pairs={{0,1},{1,0},{2,3},{3,2},{4,5},{5,4},{6,7},{7,6},{8,9},{9,8},{10,11... | collective-permute-start | bytes 786440 | tf_op jit(solution)/shard_map/ppermute | solution.py:28
  50.5 10.5 %collective-permute-start.1 = (bf16[2,1,1,1,1,32,2176]{6,5,4,3,2,1,0:T(8,128)(2,1)S(1)}, bf16[2,1,1,1,1,32,2176]{6,5,4,3,2,1,0:T(8,128)(2,1)S(1)}, u32[]{:S(2)}, u32[]{:S(2)}) collective-permute-start(bf16[2,1,1,1,1,32,2176]{6,5,4,3,2,1,0:T(8,128)(2,1)S(1)} %constant_dynamic-slice_fusion.59), channel_id=1, source_target_pairs={{0,1},{1,0},{2,3},{3,2},{4,5},{5,4},{6,7},{7,6},{8,9},{9,8},{10,11... | collective-permute-start | bytes 835592 | tf_op jit(solution)/shard_map/ppermute | solution.py:28
  64.9 11.8 %collective-permute-start.8 = (bf16[3,1,2,1,32,2048]{5,4,3,2,1,0:T(8,128)(2,1)S(1)}, bf16[3,1,2,1,32,2048]{5,4,3,2,1,0:T(8,128)(2,1)S(1)}, u32[]{:S(2)}, u32[]{:S(2)}) collective-permute-start(bf16[3,1,2,1,32,2048]{5,4,3,2,1,0:T(8,128)(2,1)S(1)} %constant_dynamic-slice_fusion.53), channel_id=1, source_target_pairs={{0,16},{4,20},{8,24},{12,28},{16,0},{20,4},{24,8},{28,12},{1,17},{... | collective-permute-start | bytes 2359304 | tf_op jit(solution)/shard_map/ppermute | solution.py:25
  68.4 29.8 %collective-permute-start.3 = (bf16[3,2,1,1,32,2176]{5,4,3,2,1,0:T(8,128)(2,1)S(1)}, bf16[3,2,1,1,32,2176]{5,4,3,2,1,0:T(8,128)(2,1)S(1)}, u32[]{:S(2)}, u32[]{:S(2)}) collective-permute-start(bf16[3,2,1,1,32,2176]{5,4,3,2,1,0:T(8,128)(2,1)S(1)} %constant_dynamic-slice_fusion.57), channel_id=1, source_target_pairs={{0,8},{4,12},{8,0},{12,4},{16,24},{20,28},{24,16},{28,20},{1,9},{5... | collective-permute-start | bytes 2506760 | tf_op jit(solution)/shard_map/ppermute | solution.py:25
  77.0 30.4 %collective-permute-start.9 = (bf16[3,2,2,1,32,2048]{5,4,3,2,1,0:T(8,128)(2,1)S(1)}, bf16[3,2,2,1,32,2048]{5,4,3,2,1,0:T(8,128)(2,1)S(1)}, u32[]{:S(2)}, u32[]{:S(2)}) collective-permute-start(bf16[3,2,2,1,32,2048]{5,4,3,2,1,0:T(8,128)(2,1)S(1)} %constant_dynamic-slice_fusion.52), channel_id=1, source_target_pairs={{0,4},{4,0},{8,12},{12,8},{16,20},{20,16},{24,28},{28,24},{1,5},{5... | collective-permute-start | bytes 4718600 | tf_op jit(solution)/shard_map/ppermute | solution.py:25
  98.5 9.2 %collective-permute-start.4 = (bf16[3,2,2,1,32,2176]{5,4,3,2,1,0:T(8,128)(2,1)S(1)}, bf16[3,2,2,1,32,2176]{5,4,3,2,1,0:T(8,128)(2,1)S(1)}, u32[]{:S(2)}, u32[]{:S(2)}) collective-permute-start(bf16[3,2,2,1,32,2176]{5,4,3,2,1,0:T(8,128)(2,1)S(1)} %constant_dynamic-slice_fusion.56), channel_id=1, source_target_pairs={{0,4},{4,0},{8,12},{12,8},{16,20},{20,16},{24,28},{28,24},{1,5},{5... | collective-permute-start | bytes 5013512 | tf_op jit(solution)/shard_map/ppermute | solution.py:25
  107.4 42.7 %collective-permute-start.14 = (bf16[2,1,1,128,2304]{4,3,2,1,0:T(8,128)(2,1)}, bf16[2,1,1,128,2304]{4,3,2,1,0:T(8,128)(2,1)}, u32[]{:S(2)}, u32[]{:S(2)}) collective-permute-start(bf16[2,1,1,128,2304]{4,3,2,1,0:T(8,128)(2,1)} %constant_dynamic-slice_fusion.30), channel_id=1, source_target_pairs={{0,1},{1,0},{2,3},{3,2},{4,5},{5,4},{6,7},{7,6},{8,9},{9,8},{10,11... | collective-permute-start | bytes 3538952 | tf_op jit(solution)/shard_map/ppermute | solution.py:28
  144.6 24.7 %collective-permute-start.11 = (bf16[512,1024]{1,0:T(8,128)(2,1)S(1)}, bf16[512,1024]{1,0:T(8,128)(2,1)S(1)}, u32[]{:S(2)}, u32[]{:S(2)}) collective-permute-start(bf16[512,1024]{1,0:T(8,128)(2,1)S(1)} %multiply_convert_fusion.6), channel_id=1, source_target_pairs={{0,8},{4,12},{8,0},{12,4},{16,24},{20,28},{24,16},{28,20},{1,9},{5... | collective-permute-start | bytes 3145736 | tf_op jit(solution)/shard_map/ppermute | solution.py:25
  148.8 24.7 %collective-permute-start.17 = (bf16[1,576,1024]{2,1,0:T(8,128)(2,1)}, bf16[1,576,1024]{2,1,0:T(8,128)(2,1)}, u32[]{:S(2)}, u32[]{:S(2)}) collective-permute-start(bf16[1,576,1024]{2,1,0:T(8,128)(2,1)} %broadcast_select_fusion.2), channel_id=1, source_target_pairs={{0,1},{2,3},{5,4},{7,6},{10,11},{8,9},{15,14},{13,12},{16,17},{18,... | collective-permute-start | bytes 3538952 | tf_op jit(solution)/shard_map/ppermute | solution.py:31
  153.3 46.5 %collective-permute-start.15 = (bf16[3,1,128,2304]{3,2,1,0:T(8,128)(2,1)}, bf16[3,1,128,2304]{3,2,1,0:T(8,128)(2,1)}, u32[]{:S(2)}, u32[]{:S(2)}) collective-permute-start(bf16[3,1,128,2304]{3,2,1,0:T(8,128)(2,1)} %constant_dynamic-slice_fusion.29), channel_id=1, source_target_pairs={{0,16},{4,20},{8,24},{12,28},{16,0},{20,4},{24,8},{28,12},{1,17},{... | collective-permute-start | bytes 5308424 | tf_op jit(solution)/shard_map/ppermute | solution.py:25
  170.9 42.4 %collective-permute-start.12 = (bf16[1024,1024]{1,0:T(8,128)(2,1)}, bf16[1024,1024]{1,0:T(8,128)(2,1)}, u32[]{:S(2)}, u32[]{:S(2)}) collective-permute-start(bf16[1024,1024]{1,0:T(8,128)(2,1)} %pad_maximum_fusion.19), channel_id=1, source_target_pairs={{0,4},{4,0},{8,12},{12,8},{16,20},{20,16},{24,28},{28,24},{1,5},{5... | collective-permute-start | bytes 6291464 | tf_op jit(solution)/shard_map/ppermute | solution.py:25
  172.1 25.0 %collective-permute-start.21 = (bf16[512,1024]{1,0:T(8,128)(2,1)}, bf16[512,1024]{1,0:T(8,128)(2,1)}, u32[]{:S(2)}, u32[]{:S(2)}) collective-permute-start(bf16[512,1024]{1,0:T(8,128)(2,1)} %bitcast.20), channel_id=1, source_target_pairs={{0,8},{4,12},{8,0},{12,4},{16,24},{20,28},{24,16},{28,20},{1,9},{5... | collective-permute-start | bytes 3145736 | tf_op jit(solution)/shard_map/ppermute | solution.py:25
  176.3 36.9 %collective-permute-start.18 = (bf16[1,576,1024]{2,1,0:T(8,128)(2,1)S(1)}, bf16[1,576,1024]{2,1,0:T(8,128)(2,1)S(1)}, u32[]{:S(2)}, u32[]{:S(2)}) collective-permute-start(bf16[1,576,1024]{2,1,0:T(8,128)(2,1)S(1)} %get-tuple-element.60), channel_id=1, source_target_pairs={{0,16},{4,20},{8,24},{12,28},{16,0},{20,4},{24,8},{28,12},{1,17},{... | collective-permute-start | bytes 3538952 | tf_op jit(solution)/shard_map/ppermute | solution.py:25
  198.9 31.4 %collective-permute-start.22 = (bf16[1024,1024]{1,0:T(8,128)(2,1)S(1)}, bf16[1024,1024]{1,0:T(8,128)(2,1)}, u32[]{:S(2)}, u32[]{:S(2)}) collective-permute-start(bf16[1024,1024]{1,0:T(8,128)(2,1)S(1)} %pad_maximum_fusion.20), channel_id=1, source_target_pairs={{0,4},{4,0},{8,12},{12,8},{16,20},{20,16},{24,28},{28,24},{1,5},{5... | collective-permute-start | bytes 6291464 | tf_op jit(solution)/shard_map/ppermute | solution.py:25
  265.9 48.4 %collective-permute-start.51 = (bf16[1,576,1024]{2,1,0:T(8,128)(2,1)S(1)}, bf16[1,576,1024]{2,1,0:T(8,128)(2,1)S(1)}, u32[]{:S(2)}, u32[]{:S(2)}) collective-permute-start(bf16[1,576,1024]{2,1,0:T(8,128)(2,1)S(1)} %constant_dynamic-slice_fusion), channel_id=1, source_target_pairs={{0,16},{4,20},{8,24},{12,28},{16,0},{20,4},{24,8},{28,12},{1,17},{... | collective-permute-start | bytes 3538952 | tf_op jit(solution)/shard_map/ppermute | solution.py:25
  285.4 41.1 %collective-permute-start.23 = (bf16[1024,1024]{1,0:T(8,128)(2,1)}, bf16[1024,1024]{1,0:T(8,128)(2,1)}, u32[]{:S(2)}, u32[]{:S(2)}) collective-permute-start(bf16[1024,1024]{1,0:T(8,128)(2,1)} %slice.407), channel_id=1, source_target_pairs={{0,4},{4,0},{8,12},{12,8},{16,20},{20,16},{24,28},{28,24},{1,5},{5... | collective-permute-start | bytes 6291464 | tf_op jit(solution)/shard_map/ppermute | solution.py:25
  296.0 35.8 %collective-permute-start.19 = (bf16[1024,1024]{1,0:T(8,128)(2,1)}, bf16[1024,1024]{1,0:T(8,128)(2,1)}, u32[]{:S(2)}, u32[]{:S(2)}) collective-permute-start(bf16[1024,1024]{1,0:T(8,128)(2,1)} %slice.408), channel_id=1, source_target_pairs={{0,4},{4,0},{8,12},{12,8},{16,20},{20,16},{24,28},{28,24},{1,5},{5... | collective-permute-start | bytes 6291464 | tf_op jit(solution)/shard_map/ppermute | solution.py:25
  313.5 52.7 %collective-permute-start.42 = (bf16[4,1,128,2304]{3,2,1,0:T(8,128)(2,1)}, bf16[4,1,128,2304]{3,2,1,0:T(8,128)(2,1)}, u32[]{:S(2)}, u32[]{:S(2)}) collective-permute-start(bf16[4,1,128,2304]{3,2,1,0:T(8,128)(2,1)} %constant_dynamic-slice_fusion.7), channel_id=1, source_target_pairs={{0,16},{4,20},{8,24},{12,28},{16,0},{20,4},{24,8},{28,12},{1,17},{... | collective-permute-start | bytes 7077896 | tf_op jit(solution)/shard_map/ppermute | solution.py:25
  315.8 20.1 %collective-permute-start.52 = (bf16[1,576,1024]{2,1,0:T(8,128)(2,1)}, bf16[1,576,1024]{2,1,0:T(8,128)(2,1)}, u32[]{:S(2)}, u32[]{:S(2)}) collective-permute-start(bf16[1,576,1024]{2,1,0:T(8,128)(2,1)} %add_convert_fusion.5), channel_id=1, source_target_pairs={{1,0},{3,2},{4,5},{6,7},{11,10},{9,8},{14,15},{12,13},{17,16},{19,... | collective-permute-start | bytes 3538952 | tf_op jit(solution)/shard_map/ppermute | solution.py:31
  330.2 43.9 %collective-permute-start.24 = (bf16[512,1024]{1,0:T(8,128)(2,1)S(1)}, bf16[512,1024]{1,0:T(8,128)(2,1)S(1)}, u32[]{:S(2)}, u32[]{:S(2)}) collective-permute-start(bf16[512,1024]{1,0:T(8,128)(2,1)S(1)} %slice.409), channel_id=1, source_target_pairs={{0,8},{4,12},{8,0},{12,4},{16,24},{20,28},{24,16},{28,20},{1,9},{5... | collective-permute-start | bytes 3145736 | tf_op jit(solution)/shard_map/ppermute | solution.py:25
  335.6 58.4 %collective-permute-start.20 = (bf16[512,1024]{1,0:T(8,128)(2,1)S(1)}, bf16[512,1024]{1,0:T(8,128)(2,1)S(1)}, u32[]{:S(2)}, u32[]{:S(2)}) collective-permute-start(bf16[512,1024]{1,0:T(8,128)(2,1)S(1)} %slice.410), channel_id=1, source_target_pairs={{0,8},{4,12},{8,0},{12,4},{16,24},{20,28},{24,16},{28,20},{1,9},{5... | collective-permute-start | bytes 3145736 | tf_op jit(solution)/shard_map/ppermute | solution.py:25
  339.0 102.3 %collective-permute-start.53 = (bf16[1,576,1024]{2,1,0:T(8,128)(2,1)}, bf16[1,576,1024]{2,1,0:T(8,128)(2,1)}, u32[]{:S(2)}, u32[]{:S(2)}) collective-permute-start(bf16[1,576,1024]{2,1,0:T(8,128)(2,1)} %add_convert_fusion.4), channel_id=1, source_target_pairs={{2,0},{7,5},{8,10},{13,15},{18,16},{23,21},{24,26},{29,31}} | collective-permute-start | bytes 3538952 | tf_op jit(solution)/shard_map/ppermute | solution.py:31
  371.0 46.1 %collective-permute-start.43 = (bf16[2,128,2304]{2,1,0:T(8,128)(2,1)}, bf16[2,128,2304]{2,1,0:T(8,128)(2,1)}, u32[]{:S(2)}, u32[]{:S(2)}) collective-permute-start(bf16[2,128,2304]{2,1,0:T(8,128)(2,1)} %slice_bitcast_fusion), channel_id=1, source_target_pairs={{0,1},{1,0},{2,3},{3,2},{4,5},{5,4},{6,7},{7,6},{8,9},{9,8},{10,11... | collective-permute-start | bytes 3538952 | tf_op jit(solution)/shard_map/ppermute | solution.py:28
  384.6 11.0 %collective-permute-start.25 = (f32[2,1024]{1,0:T(2,128)S(1)}, f32[2,1024]{1,0:T(2,128)S(1)}, u32[]{:S(2)}, u32[]{:S(2)}) collective-permute-start(f32[2,1024]{1,0:T(2,128)S(1)} %pad_add_fusion.1), channel_id=1, source_target_pairs={{4,0},{8,4},{12,8},{16,12},{20,16},{24,20},{28,24},{5,1},{9,5},{13... | collective-permute-start | bytes 24584 | tf_op jit(solution)/shard_map/ppermute | solution.py:260
  406.8 83.5 %collective-permute-start.34 = (bf16[4,2,2,1,32,2048]{5,4,3,2,1,0:T(8,128)(2,1)}, bf16[4,2,2,1,32,2048]{5,4,3,2,1,0:T(8,128)(2,1)}, u32[]{:S(2)}, u32[]{:S(2)}) collective-permute-start(bf16[4,2,2,1,32,2048]{5,4,3,2,1,0:T(8,128)(2,1)} %constant_dynamic-slice_fusion.13), channel_id=1, source_target_pairs={{0,4},{4,0},{8,12},{12,8},{16,20},{20,16},{24,28},{28,24},{1,5},{5... | collective-permute-start | bytes 6291464 | tf_op jit(solution)/shard_map/ppermute | solution.py:25
  415.1 78.4 %collective-permute-start.26 = (bf16[4,2,2,1,32,2176]{5,4,3,2,1,0:T(8,128)(2,1)S(1)}, bf16[4,2,2,1,32,2176]{5,4,3,2,1,0:T(8,128)(2,1)S(1)}, u32[]{:S(2)}, u32[]{:S(2)}) collective-permute-start(bf16[4,2,2,1,32,2176]{5,4,3,2,1,0:T(8,128)(2,1)S(1)} %constant_dynamic-slice_fusion.19), channel_id=1, source_target_pairs={{0,4},{4,0},{8,12},{12,8},{16,20},{20,16},{24,28},{28,24},{1,5},{5... | collective-permute-start | bytes 6684680 | tf_op jit(solution)/shard_map/ppermute | solution.py:25
  420.2 44.2 %collective-permute-start.44 = (bf16[128,2304]{1,0:T(8,128)(2,1)S(1)}, bf16[128,2304]{1,0:T(8,128)(2,1)S(1)}, u32[]{:S(2)}, u32[]{:S(2)}) collective-permute-start(bf16[128,2304]{1,0:T(8,128)(2,1)S(1)} %slice_bitcast_fusion.10), channel_id=1, source_target_pairs={{0,2},{1,3},{2,0},{3,1},{4,6},{5,7},{6,4},{7,5},{8,10},{9,11},{10,... | collective-permute-start | bytes 1769480 | tf_op jit(solution)/shard_map/ppermute | solution.py:28
  443.3 31.6 %collective-permute-start.54 = (bf16[1,576,1024]{2,1,0:T(8,128)(2,1)S(1)}, bf16[1,576,1024]{2,1,0:T(8,128)(2,1)S(1)}, u32[]{:S(2)}, u32[]{:S(2)}) collective-permute-start(bf16[1,576,1024]{2,1,0:T(8,128)(2,1)S(1)} %add_convert_fusion.3), channel_id=1, source_target_pairs={{0,8},{5,13},{10,2},{15,7},{16,24},{21,29},{26,18},{31,23}} | collective-permute-start | bytes 3538952 | tf_op jit(solution)/shard_map/ppermute | solution.py:31
  464.9 8.3 %collective-permute-start.48 = (bf16[1,1,1,128,1152]{4,3,2,1,0:T(8,128)(2,1)S(1)}, bf16[1,1,1,128,1152]{4,3,2,1,0:T(8,128)(2,1)S(1)}, u32[]{:S(2)}, u32[]{:S(2)}) collective-permute-start(bf16[1,1,1,128,1152]{4,3,2,1,0:T(8,128)(2,1)S(1)} %constant_dynamic-slice_fusion.3), channel_id=1, source_target_pairs={{0,16},{4,20},{8,24},{12,28},{16,0},{20,4},{24,8},{28,12},{1,17},{... | collective-permute-start | bytes 884744 | tf_op jit(solution)/shard_map/ppermute | solution.py:25
  466.2 7.9 %collective-permute-start.45 = (bf16[1,1,1,128,1152]{4,3,2,1,0:T(8,128)(2,1)S(1)}, bf16[1,1,1,128,1152]{4,3,2,1,0:T(8,128)(2,1)S(1)}, u32[]{:S(2)}, u32[]{:S(2)}) collective-permute-start(bf16[1,1,1,128,1152]{4,3,2,1,0:T(8,128)(2,1)S(1)} %constant_dynamic-slice_fusion.6), channel_id=1, source_target_pairs={{0,8},{4,12},{8,0},{12,4},{16,24},{20,28},{24,16},{28,20},{1,9},{5... | collective-permute-start | bytes 884744 | tf_op jit(solution)/shard_map/ppermute | solution.py:25
  473.3 13.7 %collective-permute-start.49 = (bf16[1,1,2,128,1152]{4,3,2,1,0:T(8,128)(2,1)S(1)}, bf16[1,1,2,128,1152]{4,3,2,1,0:T(8,128)(2,1)S(1)}, u32[]{:S(2)}, u32[]{:S(2)}) collective-permute-start(bf16[1,1,2,128,1152]{4,3,2,1,0:T(8,128)(2,1)S(1)} %constant_dynamic-slice_fusion.2), channel_id=1, source_target_pairs={{0,8},{4,12},{8,0},{12,4},{16,24},{20,28},{24,16},{28,20},{1,9},{5... | collective-permute-start | bytes 1769480 | tf_op jit(solution)/shard_map/ppermute | solution.py:25
  474.3 15.1 %collective-permute-start.46 = (bf16[2,1,1,128,1152]{4,3,2,1,0:T(8,128)(2,1)S(1)}, bf16[2,1,1,128,1152]{4,3,2,1,0:T(8,128)(2,1)S(1)}, u32[]{:S(2)}, u32[]{:S(2)}) collective-permute-start(bf16[2,1,1,128,1152]{4,3,2,1,0:T(8,128)(2,1)S(1)} %constant_dynamic-slice_fusion.5), channel_id=1, source_target_pairs={{0,16},{4,20},{8,24},{12,28},{16,0},{20,4},{24,8},{28,12},{1,17},{... | collective-permute-start | bytes 1769480 | tf_op jit(solution)/shard_map/ppermute | solution.py:25
  475.8 19.4 %collective-permute-start.55 = (bf16[1,576,1024]{2,1,0:T(8,128)(2,1)S(1)}, bf16[1,576,1024]{2,1,0:T(8,128)(2,1)S(1)}, u32[]{:S(2)}, u32[]{:S(2)}) collective-permute-start(bf16[1,576,1024]{2,1,0:T(8,128)(2,1)S(1)} %get-tuple-element.57), channel_id=1, source_target_pairs={{0,16},{2,18},{5,21},{7,23},{8,24},{10,26},{13,29},{15,31},{16,0},... | collective-permute-start | bytes 3538952 | tf_op jit(solution)/shard_map/ppermute | solution.py:31
  487.1 10.2 %collective-permute-start.50 = (bf16[2,1,2,128,1152]{4,3,2,1,0:T(8,128)(2,1)S(1)}, bf16[2,1,2,128,1152]{4,3,2,1,0:T(8,128)(2,1)S(1)}, u32[]{:S(2)}, u32[]{:S(2)}) collective-permute-start(bf16[2,1,2,128,1152]{4,3,2,1,0:T(8,128)(2,1)S(1)} %constant_dynamic-slice_fusion.1), channel_id=1, source_target_pairs={{0,4},{4,0},{8,12},{12,8},{16,20},{20,16},{24,28},{28,24},{1,5},{5... | collective-permute-start | bytes 3538952 | tf_op jit(solution)/shard_map/ppermute | solution.py:25
  492.8 23.7 %collective-permute-start.35 = (bf16[4,2,1,1,32,2048]{5,4,3,2,1,0:T(8,128)(2,1)S(1)}, bf16[4,2,1,1,32,2048]{5,4,3,2,1,0:T(8,128)(2,1)S(1)}, u32[]{:S(2)}, u32[]{:S(2)}) collective-permute-start(bf16[4,2,1,1,32,2048]{5,4,3,2,1,0:T(8,128)(2,1)S(1)} %constant_dynamic-slice_fusion.12), channel_id=1, source_target_pairs={{0,8},{4,12},{8,0},{12,4},{16,24},{20,28},{24,16},{28,20},{1,9},{5... | collective-permute-start | bytes 3145736 | tf_op jit(solution)/shard_map/ppermute | solution.py:25
  494.2 26.7 %collective-permute-start.27 = (bf16[4,1,2,1,32,2176]{5,4,3,2,1,0:T(8,128)(2,1)S(1)}, bf16[4,1,2,1,32,2176]{5,4,3,2,1,0:T(8,128)(2,1)S(1)}, u32[]{:S(2)}, u32[]{:S(2)}) collective-permute-start(bf16[4,1,2,1,32,2176]{5,4,3,2,1,0:T(8,128)(2,1)S(1)} %constant_dynamic-slice_fusion.18), channel_id=1, source_target_pairs={{0,16},{4,20},{8,24},{12,28},{16,0},{20,4},{24,8},{28,12},{1,17},{... | collective-permute-start | bytes 3342344 | tf_op jit(solution)/shard_map/ppermute | solution.py:25
  495.3 84.4 %collective-permute-start.56 = (bf16[2,576,1024]{2,1,0:T(8,128)(2,1)S(1)}, bf16[2,576,1024]{2,1,0:T(8,128)(2,1)S(1)}, u32[]{:S(2)}, u32[]{:S(2)}) collective-permute-start(bf16[2,576,1024]{2,1,0:T(8,128)(2,1)S(1)} %constant_dynamic-update-slice_fusion), channel_id=1, source_target_pairs={{0,4},{2,6},{5,1},{7,3},{8,12},{10,14},{13,9},{15,11},{16,20},{18,... | collective-permute-start | bytes 7077896 | tf_op jit(solution)/shard_map/ppermute | solution.py:31
  517.0 15.2 %collective-permute-start.36 = (bf16[4,1,1,1,32,2048]{5,4,3,2,1,0:T(8,128)(2,1)S(1)}, bf16[4,1,1,1,32,2048]{5,4,3,2,1,0:T(8,128)(2,1)S(1)}, u32[]{:S(2)}, u32[]{:S(2)}) collective-permute-start(bf16[4,1,1,1,32,2048]{5,4,3,2,1,0:T(8,128)(2,1)S(1)} %constant_dynamic-slice_fusion.11), channel_id=1, source_target_pairs={{0,16},{4,20},{8,24},{12,28},{16,0},{20,4},{24,8},{28,12},{1,17},{... | collective-permute-start | bytes 1572872 | tf_op jit(solution)/shard_map/ppermute | solution.py:25
  521.3 15.1 %collective-permute-start.28 = (bf16[4,1,1,1,32,2176]{5,4,3,2,1,0:T(8,128)(2,1)S(1)}, bf16[4,1,1,1,32,2176]{5,4,3,2,1,0:T(8,128)(2,1)S(1)}, u32[]{:S(2)}, u32[]{:S(2)}) collective-permute-start(bf16[4,1,1,1,32,2176]{5,4,3,2,1,0:T(8,128)(2,1)S(1)} %constant_dynamic-slice_fusion.17), channel_id=1, source_target_pairs={{0,8},{4,12},{8,0},{12,4},{16,24},{20,28},{24,16},{28,20},{1,9},{5... | collective-permute-start | bytes 1671176 | tf_op jit(solution)/shard_map/ppermute | solution.py:25
  532.3 8.2 %collective-permute-start.37 = (bf16[2,32,2048]{2,1,0:T(8,128)(2,1)S(1)}, bf16[2,32,2048]{2,1,0:T(8,128)(2,1)S(1)}, u32[]{:S(2)}, u32[]{:S(2)}) collective-permute-start(bf16[2,32,2048]{2,1,0:T(8,128)(2,1)S(1)} %slice_bitcast_fusion.16), channel_id=1, source_target_pairs={{0,1},{1,0},{2,3},{3,2},{4,5},{5,4},{6,7},{7,6},{8,9},{9,8},{10,11... | collective-permute-start | bytes 786440 | tf_op jit(solution)/shard_map/ppermute | solution.py:28
  540.6 11.3 %collective-permute-start.38 = (bf16[32,2048]{1,0:T(8,128)(2,1)S(1)}, bf16[32,2048]{1,0:T(8,128)(2,1)S(1)}, u32[]{:S(2)}, u32[]{:S(2)}) collective-permute-start(bf16[32,2048]{1,0:T(8,128)(2,1)S(1)} %slice_bitcast_fusion.20), channel_id=1, source_target_pairs={{0,2},{1,3},{2,0},{3,1},{4,6},{5,7},{6,4},{7,5},{8,10},{9,11},{10,... | collective-permute-start | bytes 393224 | tf_op jit(solution)/shard_map/ppermute | solution.py:28
  546.0 9.5 %collective-permute-start.29 = (bf16[2,32,2176]{2,1,0:T(8,128)(2,1)S(1)}, bf16[2,32,2176]{2,1,0:T(8,128)(2,1)S(1)}, u32[]{:S(2)}, u32[]{:S(2)}) collective-permute-start(bf16[2,32,2176]{2,1,0:T(8,128)(2,1)S(1)} %slice_bitcast_fusion.14), channel_id=1, source_target_pairs={{0,1},{1,0},{2,3},{3,2},{4,5},{5,4},{6,7},{7,6},{8,9},{9,8},{10,11... | collective-permute-start | bytes 835592 | tf_op jit(solution)/shard_map/ppermute | solution.py:28
  555.6 8.6 %collective-permute-start.30 = (bf16[32,2176]{1,0:T(8,128)(2,1)S(1)}, bf16[32,2176]{1,0:T(8,128)(2,1)S(1)}, u32[]{:S(2)}, u32[]{:S(2)}) collective-permute-start(bf16[32,2176]{1,0:T(8,128)(2,1)S(1)} %slice_bitcast_fusion.18), channel_id=1, source_target_pairs={{0,2},{1,3},{2,0},{3,1},{4,6},{5,7},{6,4},{7,5},{8,10},{9,11},{10,... | collective-permute-start | bytes 417800 | tf_op jit(solution)/shard_map/ppermute | solution.py:28
  564.7 9.1 %collective-permute-start.40 = (bf16[2,1,1,32,2048]{4,3,2,1,0:T(8,128)(2,1)S(1)}, bf16[2,1,1,32,2048]{4,3,2,1,0:T(8,128)(2,1)S(1)}, u32[]{:S(2)}, u32[]{:S(2)}) collective-permute-start(bf16[2,1,1,32,2048]{4,3,2,1,0:T(8,128)(2,1)S(1)} %constant_dynamic-slice_fusion.9), channel_id=1, source_target_pairs={{0,8},{4,12},{8,0},{12,4},{16,24},{20,28},{24,16},{28,20},{1,9},{5... | collective-permute-start | bytes 786440 | tf_op jit(solution)/shard_map/ppermute | solution.py:25
  (98 other events, 674.2 us)

commit v2 on v1

--- a/solution.py
+++ b/solution.py
@@ -1,11 +1,392 @@
+import functools
 import jax
 import jax.numpy as jnp
 from jax import lax
+from jax.experimental import pallas as pl
+from jax.experimental.pallas import tpu as pltpu
 from jax.sharding import PartitionSpec as P
 
-epsilon = 1e-06
 low = jnp.bfloat16
 full = jnp.float32
+MESH = pl.DeviceIdType.MESH
+epsilon = 1e-06
+MIB = 1 << 20
+
+
+def mirrored(index, weight):
+    return index + weight - 2 * weight * ((index // weight) % 2)
+
+
+class Net:
+    def __init__(self, me, z, send_sems, recv_sems, local_sems):
+        self.me, self.z = me, z
+        self.send_sems, self.recv_sems, self.local_sems = send_sems, recv_sems, local_sems
+        self.count = self.local_count = 0
+
+    def seat(self, name):
+        me, z = self.me, self.z
+        return {
+            "core": {"seq": mirrored(me, 1), "wsh": z},
+            "x": {"seq": mirrored(me, 2), "wsh": z},
+            "y": {"seq": mirrored(me, 4), "wsh": z},
+            "z1": {"seq": me, "wsh": mirrored(z, 1)},
+            "z2": {"seq": me, "wsh": mirrored(z, 2)},
+            "z3": {"seq": me, "wsh": 3 - z},
+        }[name]
+
+    def make(self, src, dst, seat, k=None):
+        if k is None:
+            k = self.count
+            self.count += 1
+        return pltpu.make_async_remote_copy(
+            src_ref=src,
+            dst_ref=dst,
+            send_sem=self.send_sems.at[k],
+            recv_sem=self.recv_sems.at[k],
+            device_id=self.seat(seat) if isinstance(seat, str) else seat,
+            device_id_type=MESH,
+        )
+
+    def send(self, src, dst, seat):
+        copy = self.make(src, dst, seat)
+        copy.start()
+        return copy
+
+    def move(self, src, dst):
+        k = self.local_count
+        self.local_count += 1
+        copy = pltpu.make_async_copy(src, dst, self.local_sems.at[k])
+        copy.start()
+        return copy
+
+
+def greet(seats):
+    barrier = pltpu.get_barrier_semaphore()
+    for seat in seats:
+        pl.semaphore_signal(barrier, inc=1, device_id=seat, device_id_type=MESH)
+    pl.semaphore_wait(barrier, len(seats))
+
+
+def gather_kernel(
+    seq,
+    x_hbm, e_hbm, starts_ref, small_ref, win_hbm, wout_hbm, wgu_hbm, wdn_hbm,
+    wc_out, wgu_out, wdn_out, e_out, h2_out, proj_out, first_out, zed_out, gext_out, small_out,
+    wc, winf, woutf, wguf, wdnf, wgu_own, wdn_own, x_ref, h_ref, proj, gext, zed, first, h2, small_all,
+    send_sems, recv_sems, local_sems,
+):
+    me, z = lax.axis_index("seq"), lax.axis_index("wsh")
+    net = Net(me, z, send_sems, recv_sems, local_sems)
+    core, xbit, ybit = me % 2, (me // 2) % 2, (me // 4) % 2
+    quarter = me % 4
+    rows, width = x_hbm.shape
+    part = width // 4
+    hq = wdn_hbm.shape[0]
+    hidden = 4 * hq
+    half = part // 2
+    z1, z2, z3 = mirrored(z, 1), mirrored(z, 2), 3 - z
+    after = {"seq": lax.rem(me + 1, seq), "wsh": z}
+    before = {"seq": lax.rem(me + seq - 1, seq), "wsh": z}
+
+    load_wout = net.move(wout_hbm, woutf)
+    load_win = net.move(win_hbm, winf)
+    load_x = net.move(x_hbm, x_ref.at[pl.ds(16, rows)])
+    gate_at = pl.multiple_of(quarter * hq, 128)
+    up_at = pl.multiple_of(hidden + quarter * hq, 128)
+    load_gate = net.move(wgu_hbm.at[:, pl.ds(gate_at, hq)], wguf.at[:, pl.ds(0, hq)])
+    load_up = net.move(wgu_hbm.at[:, pl.ds(up_at, hq)], wguf.at[:, pl.ds(hq, hq)])
+    load_dn = net.move(wdn_hbm, wdnf)
+    keep_e = net.move(e_hbm, e_out.at[0])
+
+    greet([net.seat(n) for n in ("core", "x", "y", "z1", "z2", "z3")] + [before])
+
+    small_all[z] = small_ref[...]
+    smalls = [net.send(small_ref, small_all.at[z], n) for n in ("z1", "z2", "z3")]
+    halo = net.send(x_hbm.at[pl.ds(rows - 16, 16)], x_ref.at[pl.ds(0, 16)], after)
+
+    load_win.wait()
+    load_wout.wait()
+    piece = part // 8
+
+    def cast_block(i, carry):
+        at = pl.ds(pl.multiple_of(i * piece, piece), piece)
+        wc[z, i // 2, i % 2, :, : 3 * width] = winf[at].astype(low)
+        wc[z, i // 2, i % 2, :, 3 * width :] = woutf[at].astype(low)
+        return carry
+
+    lax.fori_loop(0, 8, cast_block, 0)
+    spot = ybit * 2 + xbit
+    spot_x = ybit * 2 + 1 - xbit
+    spot_y = (1 - ybit) * 2 + xbit
+    cols = [pl.ds(0, 2 * width), pl.ds(2 * width, 2 * width)]
+
+    def own(zz):
+        return wc.at[zz, spot, core]
+
+    a1 = net.send(own(z), own(z), "z1")
+    a2 = net.send(own(z), own(z), "z2")
+
+    load_gate.wait()
+    load_up.wait()
+    wgu_own[...] = wguf[...].astype(low)
+    keep_gu = net.move(wgu_own, wgu_out.at[z])
+    load_dn.wait()
+    cast_rows = hq // 4
+
+    def cast_dn(i, carry):
+        at = pl.ds(pl.multiple_of(i * cast_rows, cast_rows), cast_rows)
+        wdn_own[at] = wdnf[at].astype(low)
+        return carry
+
+    lax.fori_loop(0, 4, cast_dn, 0)
+
+    def spread(zz):
+        bx = net.send(own(zz), own(zz), "x")
+        by = net.send(own(zz), own(zz), "y")
+        return bx, by
+
+    def onward(zz, b):
+        bx, by = b
+        bx.wait_recv()
+        d0 = net.send(wc.at[zz, spot_x, core, :, cols[0]], wc.at[zz, spot_x, core, :, cols[0]], "y")
+        by.wait_recv()
+        d1 = net.send(wc.at[zz, spot_y, core, :, cols[1]], wc.at[zz, spot_y, core, :, cols[1]], "x")
+        return d0, d1
+
+    def across(zz, d):
+        d[0].wait_recv()
+        d[1].wait_recv()
+        return net.send(wc.at[zz, :, core], wc.at[zz, :, core], "core")
+
+    a1.wait_recv()
+    b1 = spread(z1)
+    a2.wait_recv()
+    a3 = net.send(own(z2), own(z2), "z1")
+    b2 = spread(z2)
+
+    def gu(zz, yy):
+        return wgu_out.at[zz, pl.ds(pl.multiple_of(yy * half, half), half)]
+
+    gu_own = wgu_own.at[pl.ds(pl.multiple_of(ybit * half, half), half)]
+    f1 = net.send(gu_own, gu(z, ybit), "z1")
+    f2 = net.send(gu_own, gu(z, ybit), "z2")
+    d1 = onward(z1, b1)
+    d2 = onward(z2, b2)
+    a3.wait_recv()
+    b3 = spread(z3)
+    same0 = (z % 2) == (quarter % 2)
+    same1 = (z // 2) == (quarter // 2)
+    holder = same0 & same1
+    dn_own = wdn_own.at[pl.ds(pl.multiple_of(ybit * (hq // 2), 32), hq // 2)]
+    dn_spot = wdn_out.at[ybit]
+    dn2 = net.make(dn_own, dn_spot, "z2")
+    dn1a = net.make(dn_own, dn_spot, "z1")
+    dn1b = net.make(dn_spot, dn_spot, "z1", net.count - 1)
+    dny = net.make(dn_spot, dn_spot, "y")
+    keep_dn = [
+        pltpu.make_async_copy(
+            wdn_own.at[pl.ds(i * (hq // 2), hq // 2)], wdn_out.at[i], local_sems.at[18 + i]
+        )
+        for i in range(2)
+    ]
+
+    @pl.when(holder)
+    def _():
+        dn2.start()
+        dn1a.start()
+        for copy in keep_dn:
+            copy.start()
+
+    ex = net.send(e_hbm, e_out.at[1], "x")
+    ec = net.send(e_hbm, e_out.at[2], "core")
+    c1 = across(z1, d1)
+    c2 = across(z2, d2)
+    d3 = onward(z3, b3)
+    f1.wait_recv()
+    g1 = net.send(gu(z1, ybit), gu(z1, ybit), "y")
+    c3 = across(z3, d3)
+    f2.wait_recv()
+    f3 = net.send(gu(z2, ybit), gu(z2, ybit), "z1")
+    g2 = net.send(gu(z2, ybit), gu(z2, ybit), "y")
+
+    for s in smalls:
+        s.wait_recv()
+    load_x.wait()
+    halo.wait_recv()
+
+    def row_of(k):
+        return jnp.concatenate([small_all[i, k : k + 1, :] for i in range(4)], 1).astype(full)
+
+    gain_one, gain_two = row_of(0), row_of(1)
+
+    def norm_one(i, carry):
+        at = pl.ds(pl.multiple_of(i * 176, 16), 176)
+        xf = x_ref[at].astype(full)
+        rate = lax.rsqrt(jnp.mean(xf * xf, axis=-1, keepdims=True) + epsilon)
+        h_ref[at] = (xf * rate * gain_one).astype(low)
+        return carry
+
+    lax.fori_loop(0, (rows + 16) // 176, norm_one, 0)
+    for c in (c1, c2, c3):
+        c.wait_recv()
+
+    def project(i, carry):
+        at = pl.ds(pl.multiple_of(i * 512, 512), 512)
+        proj[:, at] = jnp.dot(
+            h_ref[...], wc[:, :, :, :, at].reshape(width, 512), preferred_element_type=full
+        )
+        return carry
+
+    lax.fori_loop(0, 6, project, 0)
+    keep_wc = net.move(wc, wc_out)
+    keep_proj = net.move(proj.at[pl.ds(16, rows)], proj_out)
+
+    place = me * rows + lax.broadcasted_iota(jnp.int32, (rows, 1), 0)
+    starts = starts_ref[...]
+    keep_one = (place - 1 >= starts).astype(full)
+    keep_two = (place - 2 >= starts).astype(full)
+    cw = 128
+
+    def mix(i, carry):
+        at = pl.ds(pl.multiple_of(i * cw, cw), cw)
+        xat = pl.ds(pl.multiple_of(2 * width + i * cw, cw), cw)
+        cat = pl.ds(pl.multiple_of(width + i * cw, cw), cw)
+        gext[:, at] = (proj[:, at] * proj[:, xat]).astype(low).astype(full)
+        zi = i // (part // cw)
+        inside = pl.ds(pl.multiple_of((i % (part // cw)) * cw, cw), cw)
+        taps = small_all[zi, :, inside].astype(full)
+        mixed = (
+            taps[2:3] * gext[16:, at]
+            + keep_one * taps[3:4] * gext[15 : rows + 15, at]
+            + keep_two * taps[4:5] * gext[14 : rows + 14, at]
+        )
+        zed[:, at] = (proj[16:, cat] * mixed).astype(low)
+        return carry
+
+    lax.fori_loop(0, width // cw, mix, 0)
+    keep_zed = net.move(zed, zed_out)
+    keep_gext = net.move(gext, gext_out)
+
+    def project_out(i, carry):
+        at = pl.ds(pl.multiple_of(i * 512, 512), 512)
+        wat = pl.ds(pl.multiple_of(3 * width + i * 512, 512), 512)
+        first[:, at] = x_ref[16:, at].astype(full) + jnp.dot(
+            zed[...], wc[:, :, :, :, wat].reshape(width, 512), preferred_element_type=full
+        )
+        return carry
+
+    lax.fori_loop(0, 2, project_out, 0)
+    keep_first = net.move(first, first_out)
+
+    def norm_two(i, carry):
+        at = pl.ds(pl.multiple_of(i * 128, 128), 128)
+        xf = first[at]
+        rate = lax.rsqrt(jnp.mean(xf * xf, axis=-1, keepdims=True) + epsilon)
+        h2[at] = (xf * rate * gain_two).astype(low)
+        return carry
+
+    lax.fori_loop(0, rows // 128, norm_two, 0)
+    keep_h2 = net.move(h2, h2_out.at[0])
+    hx = net.send(h2, h2_out.at[1], "x")
+    hc = net.send(h2, h2_out.at[2], "core")
+    keep_small = net.move(small_all, small_out)
+
+    ex.wait_recv()
+    exc = net.send(e_out.at[1], e_out.at[3], "core")
+
+    @pl.when(same0 & ~same1)
+    def _():
+        dn2.wait_recv()
+        dn1b.start()
+        dny.start()
+
+    f3.wait_recv()
+    g3 = net.send(gu(z3, ybit), gu(z3, ybit), "y")
+
+    @pl.when(~same0)
+    def _():
+        dn1a.wait_recv()
+        dny.start()
+
+    hx.wait_recv()
+    hxc = net.send(h2_out.at[1], h2_out.at[3], "core")
+    for c in (g1, g2, g3, ec, exc, hc, hxc):
+        c.wait_recv()
+
+    @pl.when(~holder)
+    def _():
+        dny.wait()
+
+    @pl.when(holder)
+    def _():
+        dn2.wait_send()
+        dn1a.wait_send()
+        for copy in keep_dn:
+            copy.wait()
+
+    @pl.when(same0 & ~same1)
+    def _():
+        dn1b.wait_send()
+
+    for c in (
+        *smalls, halo, a1, a2, a3, *b1, *b2, *b3, *d1, *d2, *d3, c1, c2, c3,
+        f1, f2, f3, g1, g2, g3, ex, ec, exc, hx, hc, hxc,
+    ):
+        c.wait_send()
+    for c in (keep_e, keep_gu, keep_wc, keep_proj, keep_zed, keep_gext, keep_first, keep_h2, keep_small):
+        c.wait()
+
+
+def gather(seq, x, e, starts, small, win, wout, wgu, wdn):
+    rows, width = x.shape
+    part = width // 4
+    hq = wdn.shape[0]
+    shape = jax.ShapeDtypeStruct
+    anyspace = pl.BlockSpec(memory_space=pl.ANY)
+    vmem = pl.BlockSpec(memory_space=pltpu.VMEM)
+    conv = (4, 4, 2, part // 8, 4 * width)
+    outs = [
+        shape(conv, low),
+        shape((4, part, 2 * hq), low),
+        shape((2, hq // 2, width), low),
+        shape((4, rows, width), low),
+        shape((4, rows, width), low),
+        shape((rows, 3 * width), full),
+        shape((rows, width), full),
+        shape((rows, width), low),
+        shape((rows + 16, width), full),
+        shape((4, 16, part), low),
+    ]
+    scratch = [
+        pltpu.VMEM(conv, low),
+        pltpu.VMEM((part, 3 * width), full),
+        pltpu.VMEM((part, width), full),
+        pltpu.VMEM((part, 2 * hq), full),
+        pltpu.VMEM((hq, width), full),
+        pltpu.VMEM((part, 2 * hq), low),
+        pltpu.VMEM((hq, width), low),
+        pltpu.VMEM((rows + 16, width), low),
+        pltpu.VMEM((rows + 16, width), low),
+        pltpu.VMEM((rows + 16, 3 * width), full),
+        pltpu.VMEM((rows + 16, width), full),
+        pltpu.VMEM((rows, width), low),
+        pltpu.VMEM((rows, width), full),
+        pltpu.VMEM((rows, width), low),
+        pltpu.VMEM((4, 16, part), low),
+        pltpu.SemaphoreType.DMA((48,)),
+        pltpu.SemaphoreType.DMA((48,)),
+        pltpu.SemaphoreType.DMA((20,)),
+    ]
+    return pl.pallas_call(
+        functools.partial(gather_kernel, seq),
+        out_shape=outs,
+        in_specs=[anyspace, anyspace, vmem, vmem] + [anyspace] * 4,
+        out_specs=[anyspace] * len(outs),
+        scratch_shapes=scratch,
+        compiler_params=pltpu.CompilerParams(
+            collective_id=0, has_side_effects=True, vmem_limit_bytes=56 * MIB
+        ),
+        name="gather",
+    )(x, e, starts, small, win, wout, wgu, wdn)
 
 
 def inner(left, right):
@@ -73,101 +454,36 @@
                 [lax.dynamic_slice_in_dim(value, (z ^ j) * part, part, 1) for j in range(wsh)], 1
             )
 
-        extra = jnp.concatenate(
-            [norm1_gain[:, None], norm2_gain[:, None], conv_weight], 1
+        small = jnp.concatenate(
+            [norm1_gain[None], norm2_gain[None], conv_weight.T], 0
         ).astype(low)
-        extra = jnp.pad(extra, ((0, 0), (0, 128 - extra.shape[1])))
-        shard_a = in_weight[:, : 2 * width].astype(low)
-        shard_b = jnp.concatenate(
-            [in_weight[:, 2 * width :].astype(low), out_weight.astype(low), extra], 1
-        )
-
-        def gather_conv(shard, order):
-            cols = shard.shape[1]
-            buf = jnp.zeros((2, 2, 2, 2, 2, part // 8, cols), low)
-            buf = put(buf, shard.reshape(1, 1, 2, 2, 2, part // 8, cols), ())
-            got = zflip(take(buf, (0, 0, ybit, xbit, core)), 2)
-            buf = put(buf, got, (1, 0, ybit, xbit, core))
-            got = zflip(take(buf, (None, 0, ybit, xbit, core)), 1)
-            buf = put(buf, got, (None, 1, ybit, xbit, core))
-            buf = buf.reshape(4, 2, 2, 2, part // 8, cols)
-            away = buf[1:]
-            for step in order:
-                index = [None, ybit, xbit, core]
-                for done in order[: order.index(step)]:
-                    index[{2: 1, 1: 2, 0: 3}[done]] = None
-                got = flip(take(away, index), step)
-                spot = {2: 1, 1: 2, 0: 3}[step]
-                index[spot] = 1 - index[spot]
-                away = put(away, got, index)
-            return jnp.concatenate([shard, away.reshape(3 * part, cols)], 0)
-
-        w_a = gather_conv(shard_a, (1, 2, 0))
-        w_b = gather_conv(shard_b, (2, 1, 0))
-        w_x = w_b[:, :width]
-        w_out = w_b[:, width : 2 * width]
-        small = w_b[:, 2 * width : 2 * width + 8].astype(full).T
-        gain_one, gain_two = small[0:1], small[1:2]
-        taps = [by_z(small[k : k + 1]) for k in (2, 3, 4)]
-
-        def gather_group(value):
-            pair = jnp.concatenate([value, flip(value, 1)], 0)
-            return jnp.concatenate([pair, flip(pair, 0)], 0)
-
-        cot_all = gather_group(cot)
-
-        gate_up = jnp.concatenate(
-            [
-                lax.dynamic_slice_in_dim(gate_up_weight, quarter * hq, hq, 1),
-                lax.dynamic_slice_in_dim(gate_up_weight, hidden + quarter * hq, hq, 1),
-            ],
-            1,
-        ).astype(low)
-        buf = jnp.zeros((2, 2, 2, part // 2, 2 * hq), low)
-        buf = put(buf, gate_up.reshape(1, 1, 2, part // 2, 2 * hq), ())
-        buf = put(buf, zflip(take(buf, (0, 0, ybit)), 2), (1, 0, ybit))
-        buf = put(buf, zflip(take(buf, (None, 0, ybit)), 1), (None, 1, ybit))
-        buf = buf.reshape(4, 2, part // 2, 2 * hq)
-        away = put(buf[1:], flip(take(buf[1:], (None, ybit)), 2), (None, 1 - ybit))
-        w_gu = jnp.concatenate([gate_up, away.reshape(3 * part, 2 * hq)], 0)
-
-        halves = down_weight.astype(low).reshape(2, hq // 2, width)
-        half = take(halves, (ybit,))
-        got = chosen(half, [((s, s % 4), (s, s % 4 ^ 2)) for s in range(seq)])
-        half = jnp.where((z ^ quarter) == 2, got, half)
-        got = chosen(
-            half, [((s, s % 4 ^ m), (s, s % 4 ^ m ^ 1)) for s in range(seq) for m in (0, 2)]
-        )
-        half = jnp.where((z ^ quarter) % 2 == 1, got, half)
-        other = flip(half, 2)
-        w_down = put(put(halves, half, (ybit,)), other, (1 - ybit,)).reshape(hq, width)
-
+        small = jnp.pad(small, ((0, 16 - small.shape[0]), (0, 0)))
+        w_c, w_gu, w_down, cot_all, second_all, proj, first, zed, gext, small_all = gather(
+            seq, tokens[0], cot, doc_start.T, small, in_weight, out_weight, gate_up_weight, down_weight
+        )
+        w_c = w_c.reshape(width, 4 * width)
+        w_gu = w_gu.reshape(width, 2 * hq)
+        w_down = w_down.reshape(hq, width)
+        cot_all = cot_all.reshape(4 * rows, width)
+        second_all = second_all.reshape(4 * rows, width)
+        w_a, w_x, w_out = w_c[:, : 2 * width], w_c[:, 2 * width : 3 * width], w_c[:, 3 * width :]
+        vec = jnp.concatenate([small_all[i] for i in range(4)], 1).astype(full)
+        gain_one, gain_two = vec[0:1], vec[1:2]
+        taps = [vec[k : k + 1] for k in (2, 3, 4)]
         xf = tokens[0].astype(full)
         starts = doc_start[0]
         rate_one = lax.rsqrt(jnp.mean(xf * xf, axis=-1, keepdims=True) + epsilon)
         normed = xf * rate_one
-        normed_z = by_z(normed)
-        h = (normed_z * gain_one).astype(low)
-        proj_a = plain(h, w_a)
-        bpart, cpart = proj_a[:, :width], proj_a[:, width:]
-        xpart = plain(h, w_x)
-        gated = (bpart * xpart).astype(low)
-        edge = lax.ppermute(gated[rows - 2 :], "seq", [(i, i + 1) for i in range(seq - 1)])
-        extended = jnp.concatenate([edge, gated], 0).astype(full)
+        h = (normed * gain_one).astype(low)
+        bpart, cpart, xpart = proj[:, :width], proj[:, width : 2 * width], proj[:, 2 * width :]
         place = me * rows + jnp.arange(rows, dtype=jnp.int32)
         keep_one = (place - 1 >= starts).astype(full)[:, None]
         keep_two = (place - 2 >= starts).astype(full)[:, None]
-        current = extended[2:]
-        lag_one = extended[1:-1]
-        lag_two = extended[:-2]
+        current, lag_one, lag_two = gext[16:], gext[15 : rows + 15], gext[14 : rows + 14]
         mixed = taps[0] * current + keep_one * taps[1] * lag_one + keep_two * taps[2] * lag_two
-        zed = by_z((cpart * mixed).astype(low))
-        first = xf + plain(zed, w_out)
         rate_two = lax.rsqrt(jnp.mean(first * first, axis=-1, keepdims=True) + epsilon)
-        normed_two = by_z(first * rate_two)
-        second = (normed_two * gain_two).astype(low)
-
-        second_all = gather_group(second)
+        normed_two = first * rate_two
+
         both = plain(second_all, w_gu)
         gate, upper = both[:, :hq], both[:, hq:]
         sigma = jax.nn.sigmoid(gate)
@@ -185,7 +501,7 @@
         result = first + scatter_group(plain(act, w_down))
         grad_second = scatter_group(outer(grad_both, w_gu))
         grad_down = inner(act, cot_all).astype(low)
-        grad_gu = inner(second_all, grad_both).astype(low)
+        grad_gu = inner(by_z(second_all), grad_both).astype(low)
 
         def plus(a, b):
             return (a.astype(full) + b.astype(full)).astype(low)
@@ -238,13 +554,12 @@
 
         grad_gain_two = jnp.sum(grad_second * normed_two, axis=0)
         scaled_two = grad_second * gain_two
-        grad_first = cot.astype(full) + by_z(
-            rate_two
-            * (scaled_two - normed_two * jnp.mean(scaled_two * normed_two, axis=-1, keepdims=True))
+        grad_first = cot.astype(full) + rate_two * (
+            scaled_two - normed_two * jnp.mean(scaled_two * normed_two, axis=-1, keepdims=True)
         )
         grad_branch = grad_first.astype(low)
-        grad_outw = inner(zed, grad_branch)
-        grad_zed = by_z(outer(grad_branch, w_out))
+        grad_outw = inner(by_z(zed), grad_branch)
+        grad_zed = outer(grad_branch, w_out)
         grad_cpart = grad_zed * mixed
         grad_mixed = grad_zed * cpart
         term_one = keep_one * grad_mixed
@@ -262,19 +577,19 @@
         grad_proj = jnp.concatenate(
             [grad_gated * xpart, grad_cpart, grad_gated * bpart], 1
         ).astype(low)
-        grad_a = inner(h, grad_proj[:, : 2 * width]).astype(low)
-        grad_x = inner(h, grad_proj[:, 2 * width :])
+        hz = by_z(h)
+        grad_a = inner(hz, grad_proj[:, : 2 * width]).astype(low)
+        grad_x = inner(hz, grad_proj[:, 2 * width :])
         grad_normed = outer(grad_proj[:, : 2 * width], w_a) + outer(
             grad_proj[:, 2 * width :], w_x
         )
-        grad_gain_one = jnp.sum(grad_normed * normed_z, axis=0)
+        grad_gain_one = jnp.sum(grad_normed * normed, axis=0)
         scaled_one = grad_normed * gain_one
-        grad_input = grad_first + by_z(
-            rate_one
-            * (scaled_one - normed_z * jnp.mean(scaled_one * normed_z, axis=-1, keepdims=True))
+        grad_input = grad_first + rate_one * (
+            scaled_one - normed * jnp.mean(scaled_one * normed, axis=-1, keepdims=True)
         )
         tail = jnp.stack(
-            [grad_gain_one, grad_gain_two] + [by_z(g[None])[0] for g in grad_taps], 1
+            [by_z(g[None])[0] for g in [grad_gain_one, grad_gain_two] + grad_taps], 1
         )
         tail = jnp.pad(tail, ((0, 0), (0, 128 - tail.shape[1])))
         grad_b = jnp.concatenate([grad_x, grad_outw, tail], 1).astype(low)

time: 597 us -> 541 us (0.906)
  Pallas kernels: 0 us -> 120 us
  starting transfers between devices: 133 us -> 44.9 us
  local copies, waits for them, and re-layouts: 94.7 us -> 32.8 us
  other arithmetic: 65.4 us -> 40.7 us
  matrix products: 106 us -> 95.3 us
  waiting for transfers between devices: 186 us -> 196 us
    pallas_call x0 -> x1, Pallas kernels: none -> 120 us  [gather(): pl.pallas_call(functools.partial(gather_kernel, seq), out_shape=outs, in_...]
    ppermute x12 -> x6, starting transfers between devices: 54.9 us -> 9.38 us  [zflip(): return lax.ppermute(value, 'wsh', [(i, i ^ mask) for i in range(wsh)])]
    ppermute x36 -> x24, starting transfers between devices: 58.1 us -> 22.1 us  [flip(): return lax.ppermute(value, 'seq', [(i, i ^ 1 << bit) for i in range(seq)])]
    ppermute x36 -> x24, waiting for transfers between devices: 138 us -> 153 us  [flip(): return lax.ppermute(value, 'seq', [(i, i ^ 1 << bit) for i in range(seq)])]
    unnamed x187 -> x85, local copies, waits for them, and re-layouts: 26.9 us -> 13.2 us
    dynamic_update_slice x31 -> x15, local copies, waits for them, and re-layouts: 14.4 us -> 0.96 us  [put(): return lax.dynamic_update_slice(buf, value, start)]
    dynamic_slice x31 -> x23, local copies, waits for them, and re-layouts: 17.3 us -> 4.63 us  [by_z(): lax.dynamic_slice_in_dim(value, (z ^ j) * part, part, 1)]
    dot_general x5 -> x2, matrix products: 34.8 us -> 25.2 us  [plain(): return jnp.dot(left, right, preferred_element_type=full)]
  transfers between devices with their start and end apart: 57 -> 36, of which waited for: 23 -> 15; matrix products, arithmetic and copies ran while one was open for 34% -> 18% of each run, Pallas kernels for 0% -> 0%
where the time goes in v2:
time: 541 us; the launch traced here: 532 us
  waiting for transfers between devices  196 us (36%)
  Pallas kernels  120 us (22%)
  matrix products  95.3 us (18%)
  starting transfers between devices  44.9 us (8%)
  other arithmetic  40.7 us (8%)
  local copies, waits for them, and re-layouts  32.8 us (6%)
    ppermute x24, waiting for transfers between devices, flip(): return lax.ppermute(value, 'seq', [(i, i ^ 1 << bit) for i in range(seq)])  153 us
    pallas_call x1, Pallas kernels, gather(): pl.pallas_call(functools.partial(gather_kernel, seq), out_shape=outs, in_...  120 us
    ppermute x6, waiting for transfers between devices, zflip(): return lax.ppermute(value, 'wsh', [(i, i ^ mask) for i in range(wsh)])  42.6 us
    dot_general x5, matrix products, outer(): lax.dot_general(left, right, (((1,), (1,)), ((), ())), preferred_element_...  41.6 us
    dot_general x5, matrix products, inner(): lax.dot_general(left, right, (((0,), (0,)), ((), ())), preferred_element_...  28.5 us
    dot_general x2, matrix products, plain(): return jnp.dot(left, right, preferred_element_type=full)  25.2 us
    ppermute x24, starting transfers between devices, flip(): return lax.ppermute(value, 'seq', [(i, i ^ 1 << bit) for i in range(seq)])  22.1 us
    unnamed x85, local copies, waits for them, and re-layouts  13.2 us
  transfers between devices with their start and end apart: 36, of which 15 were waited for; matrix products, arithmetic and copies ran while one was open for 18% of the time, Pallas kernels for 0%

profile of v2, /device:TPU:1, one launch (start us, length us, event | category | flops | bytes accessed | tf_op | source)
XLA Modules:
  0.0 531.9 jit_solution(463035316597644759)
XLA Ops:
  4.9 120.0 %gather.1 = (bf16[4,4,2,32,4096]{4,3,2,1,0:T(8,128)(2,1)}, bf16[4,256,2304]{2,1,0:T(8,128)(2,1)}, bf16[2,576,1024]{2,1,0:T(8,128)(2,1)}, bf16[4,512,1024]{2,1,0:...) custom-call(bf16[512,1024]{1,0:T(8,128)(2,1)} %bitcast.187, ...), custom_call_target="tpu_custom_call" | custom-call | tf_op jit(solution)/shard_map/gather/pallas_call | solution.py:379
  124.8 16.8 %fusion.85 = f32[2048,2304]{1,0:T(8,128)} fusion(bf16[2048,1024]{1,0:T(8,128)(2,1)} %bitcast.194, bf16[1024,2304]{1,0:T(8,128)(2,1)} %bitcast.227), kind=kOutput, calls=%fused_computation.259 | convolution fusion | flops 9663676416 | bytes 27787264 | tf_op jit(solution)/shard_map/dot_general | solution.py:401
  141.7 18.5 %multiply_convert_fusion.1 = (bf16[2048,1152]{1,0:T(8,128)(2,1)}, bf16[2048,1152]{1,0:T(8,128)(2,1)}, bf16[2048,1152]{1,0:T(8,128)(2,1)}) fusion(f32[2048,2304]{1,0:T(8,128)} %fusion.85, bf16[2048,1024]{1,0:T(8,128)(2,1)} %bitcast.231, bf16[1152,1024]{1,0:T(8,128)(2,1)} %bitcast.233), kind=kOutput, calls=%fused_computation.2 | convolution fusion | flops 4867227648 | bytes 39583744 | tf_op jit(solution)/shard_map/dot_general | solution.py:397
  160.2 12.9 %fusion.2 = f32[2048,1024]{1,0:T(8,128)S(1)} fusion(bf16[1024,2304]{1,0:T(8,128)(2,1)S(1)} %bitcast.230, bf16[2048,1152]{1,0:T(8,128)(2,1)} %get-tuple-element.69, bf16[2048,1152]{1,0:T(8,128)(2,1)} %get-tuple-element.68), kind=kOutput, calls=%fused_computation.7 | convolution fusion | flops 9682550784 | bytes 22544384 | tf_op jit(solution)/shard_map/dot_general | solution.py:397
  176.5 8.4 %fusion.86 = f32[2048,1024]{1,0:T(8,128)S(1)} fusion(bf16[2048,1152]{1,0:T(8,128)(2,1)} %get-tuple-element.70, bf16[1152,1024]{1,0:T(8,128)(2,1)S(1)} %bitcast.234), kind=kOutput, calls=%fused_computation.260 | convolution fusion | flops 4831838208 | bytes 15466496 | tf_op jit(solution)/shard_map/dot_general | solution.py:401
  184.9 3.3 copy-done.7
  189.8 3.5 constant_dynamic-slice_fusion.11
  193.3 14.3 %fusion.3 = bf16[1024,2304]{1,0:T(8,128)(2,1)S(1)} fusion(bf16[2048,1152]{1,0:T(8,128)(2,1)} %get-tuple-element.69, bf16[2048,1152]{1,0:T(8,128)(2,1)} %get-tuple-element.68, bf16[2048,256]{1,0:T(8,128)(2,1)S(1)} %get-tuple-element.75, bf16[2048,256]{1,0:T(8,128)(2,1)S(1)} %get-tuple-element.76, bf16[2048,256]{1,0:T(8,128)(2,1)} %get-tuple-element.77, ...), kind=kOutput, calls=%fused_computation.8 | convolution fusion | flops 9701687296 | bytes 18350080 | tf_op jit(solution)/shard_map/dot_general | solution.py:393
  209.2 1.9 copy-done.6
  212.3 7.9 %convolution_convert_fusion = bf16[1152,1024]{1,0:T(8,128)(2,1)S(1)} fusion(bf16[2048,1152]{1,0:T(8,128)(2,1)} %get-tuple-element.70, bf16[2048,1024]{1,0:T(8,128)(2,1)S(1)} %bitcast.232), kind=kOutput, calls=%fused_computation.26 | convolution fusion | flops 4833017856 | bytes 11272192 | tf_op jit(solution)/shard_map/dot_general | solution.py:393
  224.3 64.7 %collective-permute-done.30 = bf16[1,576,1024]{2,1,0:T(8,128)(2,1)} collective-permute-done((bf16[1,576,1024]{2,1,0:T(8,128)(2,1)}, bf16[1,576,1024]{2,1,0:T(8,128)(2,1)}, u32[]{:S(2)}, u32[]{:S(2)}) %collective-permute-start.30) | collective-permute-done | bytes 1179680 | tf_op jit(solution)/shard_map/ppermute | solution.py:406
  289.1 1.9 add_convert_fusion.5
  291.0 5.3 collective-permute-start.31
  296.3 3.6 slice_add_fusion
  300.1 4.0 collective-permute-start.3
  304.1 2.4 slice_add_fusion.1
  306.9 2.3 add_convert_fusion
  313.6 13.4 %collective-permute-done.3 = bf16[512,1024]{1,0:T(8,128)(2,1)S(1)} collective-permute-done((bf16[512,1024]{1,0:T(8,128)(2,1)S(1)}, bf16[512,1024]{1,0:T(8,128)(2,1)S(1)}, u32[]{:S(2)}, u32[]{:S(2)}) %collective-permute-start.3) | collective-permute-done | bytes 1048608 | tf_op jit(solution)/shard_map/ppermute | solution.py:406
  327.8 21.7 %collective-permute-done.1 = bf16[512,1024]{1,0:T(8,128)(2,1)S(1)} collective-permute-done((bf16[512,1024]{1,0:T(8,128)(2,1)S(1)}, bf16[512,1024]{1,0:T(8,128)(2,1)S(1)}, u32[]{:S(2)}, u32[]{:S(2)}) %collective-permute-start.1) | collective-permute-done | bytes 1048608 | tf_op jit(solution)/shard_map/ppermute | solution.py:406
  349.5 1.9 multiply_add_fusion
  351.5 4.9 multiply_reduce_fusion
  357.6 3.4 collective-permute-start.4
  361.5 2.6 convolution_convert_fusion.2
  366.5 4.0 fusion.24
  370.9 3.2 fusion.23
  378.9 2.4 convolution_convert_fusion.1
  383.3 2.1 add_convert_fusion.3
  386.4 22.5 %collective-permute-done.23 = bf16[128,2304]{1,0:T(8,128)(2,1)S(1)} collective-permute-done((bf16[128,2304]{1,0:T(8,128)(2,1)S(1)}, bf16[128,2304]{1,0:T(8,128)(2,1)S(1)}, u32[]{:S(2)}, u32[]{:S(2)}) %collective-permute-start.23) | collective-permute-done | bytes 589856 | tf_op jit(solution)/shard_map/ppermute | solution.py:409
  410.4 7.3 %collective-permute-done.24 = bf16[1,1,1,128,1152]{4,3,2,1,0:T(8,128)(2,1)S(1)} collective-permute-done((bf16[1,1,1,128,1152]{4,3,2,1,0:T(8,128)(2,1)S(1)}, bf16[1,1,1,128,1152]{4,3,2,1,0:T(8,128)(2,1)S(1)}, u32[]{:S(2)}, u32[]{:S(2)}) %collective-permute-start.24) | collective-permute-done | bytes 294944 | tf_op jit(solution)/shard_map/ppermute | solution.py:406
  421.0 10.4 %collective-permute-done.25 = bf16[2,1,1,128,1152]{4,3,2,1,0:T(8,128)(2,1)S(1)} collective-permute-done((bf16[2,1,1,128,1152]{4,3,2,1,0:T(8,128)(2,1)S(1)}, bf16[2,1,1,128,1152]{4,3,2,1,0:T(8,128)(2,1)S(1)}, u32[]{:S(2)}, u32[]{:S(2)}) %collective-permute-start.25) | collective-permute-done | bytes 589856 | tf_op jit(solution)/shard_map/ppermute | solution.py:406
  431.6 2.2 collective-permute-start.26
  440.3 4.9 convert_element_type.328
  445.2 14.7 %collective-permute-done.14 = bf16[4,2,1,1,32,2048]{5,4,3,2,1,0:T(8,128)(2,1)S(1)} collective-permute-done((bf16[4,2,1,1,32,2048]{5,4,3,2,1,0:T(8,128)(2,1)S(1)}, bf16[4,2,1,1,32,2048]{5,4,3,2,1,0:T(8,128)(2,1)S(1)}, u32[]{:S(2)}, u32[]{:S(2)}) %collective-permute-start.14) | collective-permute-done | bytes 1048608 | tf_op jit(solution)/shard_map/ppermute | solution.py:406
  461.8 2.1 collective-permute-done.6
  464.7 10.5 %collective-permute-done.15 = bf16[4,1,1,1,32,2048]{5,4,3,2,1,0:T(8,128)(2,1)S(1)} collective-permute-done((bf16[4,1,1,1,32,2048]{5,4,3,2,1,0:T(8,128)(2,1)S(1)}, bf16[4,1,1,1,32,2048]{5,4,3,2,1,0:T(8,128)(2,1)S(1)}, u32[]{:S(2)}, u32[]{:S(2)}) %collective-permute-start.15) | collective-permute-done | bytes 524320 | tf_op jit(solution)/shard_map/ppermute | solution.py:406
  475.3 5.7 %collective-permute-start.16 = (bf16[2,32,2048]{2,1,0:T(8,128)(2,1)S(1)}, bf16[2,32,2048]{2,1,0:T(8,128)(2,1)S(1)}, u32[]{:S(2)}, u32[]{:S(2)}) collective-permute-start(bf16[2,32,2048]{2,1,0:T(8,128)(2,1)S(1)} %slice_bitcast_fusion.16), channel_id=1, source_target_pairs={{0,1},{1,0},{2,3},{3,2},{4,5},{5,4},{6,7},{7,6},{8,9},{9,8},{10,11... | collective-permute-start | bytes 786440 | tf_op jit(solution)/shard_map/ppermute | solution.py:409
  481.2 5.3 %collective-permute-done.16 = bf16[2,32,2048]{2,1,0:T(8,128)(2,1)S(1)} collective-permute-done((bf16[2,32,2048]{2,1,0:T(8,128)(2,1)S(1)}, bf16[2,32,2048]{2,1,0:T(8,128)(2,1)S(1)}, u32[]{:S(2)}, u32[]{:S(2)}) %collective-permute-start.16) | collective-permute-done | bytes 262176 | tf_op jit(solution)/shard_map/ppermute | solution.py:409
  486.6 2.9 collective-permute-start.17
  489.6 2.9 collective-permute-done.17
  492.7 2.2 collective-permute-start.18
  494.9 4.2 collective-permute-done.8
  499.8 7.7 %collective-permute-done.9 = bf16[32,2176]{1,0:T(8,128)(2,1)S(1)} collective-permute-done((bf16[32,2176]{1,0:T(8,128)(2,1)S(1)}, bf16[32,2176]{1,0:T(8,128)(2,1)S(1)}, u32[]{:S(2)}, u32[]{:S(2)}) %collective-permute-start.9) | collective-permute-done | bytes 139296 | tf_op jit(solution)/shard_map/ppermute | solution.py:409
  507.6 2.5 collective-permute-start.10
  510.3 2.8 collective-permute-done.10
  513.2 5.5 %collective-permute-done.19 = bf16[2,1,1,32,2048]{4,3,2,1,0:T(8,128)(2,1)S(1)} collective-permute-done((bf16[2,1,1,32,2048]{4,3,2,1,0:T(8,128)(2,1)S(1)}, bf16[2,1,1,32,2048]{4,3,2,1,0:T(8,128)(2,1)S(1)}, u32[]{:S(2)}, u32[]{:S(2)}) %collective-permute-start.19) | collective-permute-done | bytes 262176 | tf_op jit(solution)/shard_map/ppermute | solution.py:406
  520.6 2.3 collective-permute-start.12
  523.5 2.9 bitcast_convert_fusion
  529.5 1.9 pad_maximum_fusion.6
  (264 shorter events, 54.8 us)
Async XLA Ops:
  124.8 35.4 %slice-start.8 = ((s8[4718592]{0:T(1024)(128)(4,1)}), s8[4194304]{0:T(1024)(128)(4,1)S(1)}, s32[]{:S(2)}) async-start(s8[4718592]{0:T(1024)(128)(4,1)} %bitcast.228), calls=%async_computation.8 | async-start | bytes 8388608
  141.7 18.5 %slice-start.9 = ((s8[4718592]{0:T(1024)(128)(4,1)}), s8[524288]{0:T(1024)(128)(4,1)S(1)}, s32[]{:S(2)}) async-start(s8[4718592]{0:T(1024)(128)(4,1)} %bitcast.228), calls=%async_computation.9 | async-start | bytes 1048576
  173.1 11.8 %copy-start.8 = (f32[2048,1024]{1,0:T(8,128)}, f32[2048,1024]{1,0:T(8,128)S(1)}, u32[]{:S(2)}) copy-start(f32[2048,1024]{1,0:T(8,128)S(1)} %fusion.2) | copy-start | bytes 25165828
  174.8 121.5 %collective-permute-start.2 = (bf16[1024,1024]{1,0:T(8,128)(2,1)}, bf16[1024,1024]{1,0:T(8,128)(2,1)}, u32[]{:S(2)}, u32[]{:S(2)}) collective-permute-start(bf16[1024,1024]{1,0:T(8,128)(2,1)} %slice.396), channel_id=1, source_target_pairs={{0,4},{4,0},{8,12},{12,8},{16,20},{20,16},{24,28},{28,24},{1,5},{5... | collective-permute-start | bytes 6291464 | tf_op jit(solution)/shard_map/ppermute | solution.py:406
  189.8 114.3 %collective-permute-start = (bf16[1024,1024]{1,0:T(8,128)(2,1)}, bf16[1024,1024]{1,0:T(8,128)(2,1)}, u32[]{:S(2)}, u32[]{:S(2)}) collective-permute-start(bf16[1024,1024]{1,0:T(8,128)(2,1)} %slice.397), channel_id=1, source_target_pairs={{0,4},{4,0},{8,12},{12,8},{16,20},{20,16},{24,28},{28,24},{1,5},{5... | collective-permute-start | bytes 6291464 | tf_op jit(solution)/shard_map/ppermute | solution.py:406
  211.2 95.7 %collective-permute-start.21 = (bf16[4,1,128,2304]{3,2,1,0:T(8,128)(2,1)}, bf16[4,1,128,2304]{3,2,1,0:T(8,128)(2,1)}, u32[]{:S(2)}, u32[]{:S(2)}) collective-permute-start(bf16[4,1,128,2304]{3,2,1,0:T(8,128)(2,1)} %constant_dynamic-slice_fusion.7), channel_id=1, source_target_pairs={{0,16},{4,20},{8,24},{12,28},{16,0},{20,4},{24,8},{28,12},{1,17},{... | collective-permute-start | bytes 7077896 | tf_op jit(solution)/shard_map/ppermute | solution.py:406
  221.3 67.7 %collective-permute-start.30 = (bf16[1,576,1024]{2,1,0:T(8,128)(2,1)}, bf16[1,576,1024]{2,1,0:T(8,128)(2,1)}, u32[]{:S(2)}, u32[]{:S(2)}) collective-permute-start(bf16[1,576,1024]{2,1,0:T(8,128)(2,1)} %constant_dynamic-slice_fusion), channel_id=1, source_target_pairs={{0,16},{4,20},{8,24},{12,28},{16,0},{20,4},{24,8},{28,12},{1,17},{... | collective-permute-start | bytes 3538952 | tf_op jit(solution)/shard_map/ppermute | solution.py:406
  223.3 65.8 %copy-start.11 = (bf16[1152,1024]{1,0:T(8,128)(2,1)S(1)}, bf16[1152,1024]{1,0:T(8,128)(2,1)}, u32[]{:S(2)}) copy-start(bf16[1152,1024]{1,0:T(8,128)(2,1)} %copy-done.10) | copy-start | bytes 7077892
  289.1 15.0 %slice-start.2 = ((s8[8388608]{0:T(1024)(128)(4,1)}), s8[4194304]{0:T(1024)(128)(4,1)S(1)}, s32[]{:S(2)}) async-start(s8[8388608]{0:T(1024)(128)(4,1)} %bitcast.192), calls=%async_computation.2 | async-start | bytes 8388608
  291.0 13.1 %slice-start.3 = ((s8[8388608]{0:T(1024)(128)(4,1)}), s8[4194304]{0:T(1024)(128)(4,1)S(1)}, s32[]{:S(2)}) async-start(s8[8388608]{0:T(1024)(128)(4,1)} %bitcast.192), calls=%async_computation.3 | async-start | bytes 8388608
  291.0 19.5 %collective-permute-start.31 = (bf16[1,576,1024]{2,1,0:T(8,128)(2,1)S(1)}, bf16[1,576,1024]{2,1,0:T(8,128)(2,1)S(1)}, u32[]{:S(2)}, u32[]{:S(2)}) collective-permute-start(bf16[1,576,1024]{2,1,0:T(8,128)(2,1)S(1)} %add_convert_fusion.5), channel_id=1, source_target_pairs={{1,0},{3,2},{4,5},{6,7},{11,10},{9,8},{14,15},{12,13},{17,16},{19,... | collective-permute-start | bytes 3538952 | tf_op jit(solution)/shard_map/ppermute | solution.py:412
  300.1 27.0 %collective-permute-start.3 = (bf16[512,1024]{1,0:T(8,128)(2,1)S(1)}, bf16[512,1024]{1,0:T(8,128)(2,1)S(1)}, u32[]{:S(2)}, u32[]{:S(2)}) collective-permute-start(bf16[512,1024]{1,0:T(8,128)(2,1)S(1)} %slice.398), channel_id=1, source_target_pairs={{0,8},{4,12},{8,0},{12,4},{16,24},{20,28},{24,16},{28,20},{1,9},{5... | collective-permute-start | bytes 3145736 | tf_op jit(solution)/shard_map/ppermute | solution.py:406
  306.7 42.9 %collective-permute-start.1 = (bf16[512,1024]{1,0:T(8,128)(2,1)S(1)}, bf16[512,1024]{1,0:T(8,128)(2,1)S(1)}, u32[]{:S(2)}, u32[]{:S(2)}) collective-permute-start(bf16[512,1024]{1,0:T(8,128)(2,1)S(1)} %slice.399), channel_id=1, source_target_pairs={{0,8},{4,12},{8,0},{12,4},{16,24},{20,28},{24,16},{28,20},{1,9},{5... | collective-permute-start | bytes 3145736 | tf_op jit(solution)/shard_map/ppermute | solution.py:406
  310.4 70.9 %collective-permute-start.22 = (bf16[2,128,2304]{2,1,0:T(8,128)(2,1)}, bf16[2,128,2304]{2,1,0:T(8,128)(2,1)}, u32[]{:S(2)}, u32[]{:S(2)}) collective-permute-start(bf16[2,128,2304]{2,1,0:T(8,128)(2,1)} %slice_bitcast_fusion), channel_id=1, source_target_pairs={{0,1},{1,0},{2,3},{3,2},{4,5},{5,4},{6,7},{7,6},{8,9},{9,8},{10,11... | collective-permute-start | bytes 3538952 | tf_op jit(solution)/shard_map/ppermute | solution.py:409
  312.0 71.3 %collective-permute-start.32 = (bf16[1,576,1024]{2,1,0:T(8,128)(2,1)}, bf16[1,576,1024]{2,1,0:T(8,128)(2,1)}, u32[]{:S(2)}, u32[]{:S(2)}) collective-permute-start(bf16[1,576,1024]{2,1,0:T(8,128)(2,1)} %add_convert_fusion.4), channel_id=1, source_target_pairs={{2,0},{7,5},{8,10},{13,15},{18,16},{23,21},{24,26},{29,31}} | collective-permute-start | bytes 3538952 | tf_op jit(solution)/shard_map/ppermute | solution.py:412
  327.0 22.5 %copy-start.9 = (bf16[1,512,1024]{2,1,0:T(8,128)(2,1)S(1)}, bf16[1,512,1024]{2,1,0:T(8,128)(2,1)}, u32[]{:S(2)}) copy-start(bf16[1,512,1024]{2,1,0:T(8,128)(2,1)} %param.19) | copy-start | bytes 3145732
  327.8 23.6 %slice-start.4 = ((s8[6291456]{0:T(1024)(128)(4,1)}), s8[4194304]{0:T(1024)(128)(4,1)S(1)}, s32[]{:S(2)}) async-start(s8[6291456]{0:T(1024)(128)(4,1)} %bitcast.199), calls=%async_computation.4 | async-start | bytes 8388608
  327.8 23.6 %slice-start.5 = ((s8[6291456]{0:T(1024)(128)(4,1)}), s8[2097152]{0:T(1024)(128)(4,1)S(1)}, s32[]{:S(2)}) async-start(s8[6291456]{0:T(1024)(128)(4,1)} %bitcast.199), calls=%async_computation.5 | async-start | bytes 4194304
  327.8 23.6 %copy-start.25 = (f32[528,1024]{1,0:T(8,128)S(1)}, f32[528,1024]{1,0:T(8,128)}, u32[]{:S(2)}) copy-start(f32[528,1024]{1,0:T(8,128)} %get-tuple-element.27) | copy-start | bytes 6488068
  351.4 10.0 %copy-start.4 = (f32[512,1024]{1,0:T(8,128)}, f32[512,1024]{1,0:T(8,128)S(1)}, u32[]{:S(2)}) copy-start(f32[512,1024]{1,0:T(8,128)S(1)} %get-tuple-element.83) | copy-start | bytes 6291460
  356.3 10.1 %copy-start.26 = (bf16[512,1024]{1,0:T(8,128)(2,1)}, bf16[512,1024]{1,0:T(8,128)(2,1)S(1)}, u32[]{:S(2)}) copy-start(bf16[512,1024]{1,0:T(8,128)(2,1)S(1)} %get-tuple-element.73) | copy-start | bytes 3145732
  357.6 6.5 %collective-permute-start.4 = (f32[2,1024]{1,0:T(2,128)S(1)}, f32[2,1024]{1,0:T(2,128)S(1)}, u32[]{:S(2)}, u32[]{:S(2)}) collective-permute-start(f32[2,1024]{1,0:T(2,128)S(1)} %pad_add_fusion.1), channel_id=1, source_target_pairs={{4,0},{8,4},{12,8},{16,12},{20,16},{24,20},{28,24},{5,1},{9,5},{13... | collective-permute-start | bytes 24584 | tf_op jit(solution)/shard_map/ppermute | solution.py:575
  377.6 58.9 %collective-permute-start.5 = (bf16[4,2,2,1,32,2176]{5,4,3,2,1,0:T(8,128)(2,1)S(1)}, bf16[4,2,2,1,32,2176]{5,4,3,2,1,0:T(8,128)(2,1)S(1)}, u32[]{:S(2)}, u32[]{:S(2)}) collective-permute-start(bf16[4,2,2,1,32,2176]{5,4,3,2,1,0:T(8,128)(2,1)S(1)} %constant_dynamic-slice_fusion.23), channel_id=1, source_target_pairs={{0,4},{4,0},{8,12},{12,8},{16,20},{20,16},{24,28},{28,24},{1,5},{5... | collective-permute-start | bytes 6684680 | tf_op jit(solution)/shard_map/ppermute | solution.py:406
  383.0 25.9 %collective-permute-start.23 = (bf16[128,2304]{1,0:T(8,128)(2,1)S(1)}, bf16[128,2304]{1,0:T(8,128)(2,1)S(1)}, u32[]{:S(2)}, u32[]{:S(2)}) collective-permute-start(bf16[128,2304]{1,0:T(8,128)(2,1)S(1)} %slice_bitcast_fusion.10), channel_id=1, source_target_pairs={{0,2},{1,3},{2,0},{3,1},{4,6},{5,7},{6,4},{7,5},{8,10},{9,11},{10,... | collective-permute-start | bytes 1769480 | tf_op jit(solution)/shard_map/ppermute | solution.py:409
  383.2 51.1 %collective-permute-start.13 = (bf16[4,2,2,1,32,2048]{5,4,3,2,1,0:T(8,128)(2,1)S(1)}, bf16[4,2,2,1,32,2048]{5,4,3,2,1,0:T(8,128)(2,1)S(1)}, u32[]{:S(2)}, u32[]{:S(2)}) collective-permute-start(bf16[4,2,2,1,32,2048]{5,4,3,2,1,0:T(8,128)(2,1)S(1)} %constant_dynamic-slice_fusion.17), channel_id=1, source_target_pairs={{0,4},{4,0},{8,12},{12,8},{16,20},{20,16},{24,28},{28,24},{1,5},{5... | collective-permute-start | bytes 6291464 | tf_op jit(solution)/shard_map/ppermute | solution.py:406
  385.4 34.0 %collective-permute-start.33 = (bf16[1,576,1024]{2,1,0:T(8,128)(2,1)S(1)}, bf16[1,576,1024]{2,1,0:T(8,128)(2,1)S(1)}, u32[]{:S(2)}, u32[]{:S(2)}) collective-permute-start(bf16[1,576,1024]{2,1,0:T(8,128)(2,1)S(1)} %add_convert_fusion.3), channel_id=1, source_target_pairs={{0,8},{5,13},{10,2},{15,7},{16,24},{21,29},{26,18},{31,23}} | collective-permute-start | bytes 3538952 | tf_op jit(solution)/shard_map/ppermute | solution.py:412
  409.4 8.3 %collective-permute-start.24 = (bf16[1,1,1,128,1152]{4,3,2,1,0:T(8,128)(2,1)S(1)}, bf16[1,1,1,128,1152]{4,3,2,1,0:T(8,128)(2,1)S(1)}, u32[]{:S(2)}, u32[]{:S(2)}) collective-permute-start(bf16[1,1,1,128,1152]{4,3,2,1,0:T(8,128)(2,1)S(1)} %constant_dynamic-slice_fusion.6), channel_id=1, source_target_pairs={{0,8},{4,12},{8,0},{12,4},{16,24},{20,28},{24,16},{28,20},{1,9},{5... | collective-permute-start | bytes 884744 | tf_op jit(solution)/shard_map/ppermute | solution.py:406
  410.2 7.9 %collective-permute-start.27 = (bf16[1,1,1,128,1152]{4,3,2,1,0:T(8,128)(2,1)S(1)}, bf16[1,1,1,128,1152]{4,3,2,1,0:T(8,128)(2,1)S(1)}, u32[]{:S(2)}, u32[]{:S(2)}) collective-permute-start(bf16[1,1,1,128,1152]{4,3,2,1,0:T(8,128)(2,1)S(1)} %constant_dynamic-slice_fusion.3), channel_id=1, source_target_pairs={{0,16},{4,20},{8,24},{12,28},{16,0},{20,4},{24,8},{28,12},{1,17},{... | collective-permute-start | bytes 884744 | tf_op jit(solution)/shard_map/ppermute | solution.py:406
  417.8 13.7 %collective-permute-start.25 = (bf16[2,1,1,128,1152]{4,3,2,1,0:T(8,128)(2,1)S(1)}, bf16[2,1,1,128,1152]{4,3,2,1,0:T(8,128)(2,1)S(1)}, u32[]{:S(2)}, u32[]{:S(2)}) collective-permute-start(bf16[2,1,1,128,1152]{4,3,2,1,0:T(8,128)(2,1)S(1)} %constant_dynamic-slice_fusion.5), channel_id=1, source_target_pairs={{0,16},{4,20},{8,24},{12,28},{16,0},{20,4},{24,8},{28,12},{1,17},{... | collective-permute-start | bytes 1769480 | tf_op jit(solution)/shard_map/ppermute | solution.py:406
  418.2 15.6 %collective-permute-start.28 = (bf16[1,1,2,128,1152]{4,3,2,1,0:T(8,128)(2,1)S(1)}, bf16[1,1,2,128,1152]{4,3,2,1,0:T(8,128)(2,1)S(1)}, u32[]{:S(2)}, u32[]{:S(2)}) collective-permute-start(bf16[1,1,2,128,1152]{4,3,2,1,0:T(8,128)(2,1)S(1)} %constant_dynamic-slice_fusion.2), channel_id=1, source_target_pairs={{0,8},{4,12},{8,0},{12,4},{16,24},{20,28},{24,16},{28,20},{1,9},{5... | collective-permute-start | bytes 1769480 | tf_op jit(solution)/shard_map/ppermute | solution.py:406
  420.3 17.4 %collective-permute-start.34 = (bf16[1,576,1024]{2,1,0:T(8,128)(2,1)S(1)}, bf16[1,576,1024]{2,1,0:T(8,128)(2,1)S(1)}, u32[]{:S(2)}, u32[]{:S(2)}) collective-permute-start(bf16[1,576,1024]{2,1,0:T(8,128)(2,1)S(1)} %get-tuple-element.66), channel_id=1, source_target_pairs={{0,16},{2,18},{5,21},{7,23},{8,24},{10,26},{13,29},{15,31},{16,0},... | collective-permute-start | bytes 3538952 | tf_op jit(solution)/shard_map/ppermute | solution.py:412
  431.6 7.5 %collective-permute-start.26 = (bf16[2,1,2,128,1152]{4,3,2,1,0:T(8,128)(2,1)S(1)}, bf16[2,1,2,128,1152]{4,3,2,1,0:T(8,128)(2,1)S(1)}, u32[]{:S(2)}, u32[]{:S(2)}) collective-permute-start(bf16[2,1,2,128,1152]{4,3,2,1,0:T(8,128)(2,1)S(1)} %constant_dynamic-slice_fusion.4), channel_id=1, source_target_pairs={{0,4},{4,0},{8,12},{12,8},{16,20},{20,16},{24,28},{28,24},{1,5},{5... | collective-permute-start | bytes 3538952 | tf_op jit(solution)/shard_map/ppermute | solution.py:406
  434.0 5.7 %collective-permute-start.29 = (bf16[2,1,2,128,1152]{4,3,2,1,0:T(8,128)(2,1)S(1)}, bf16[2,1,2,128,1152]{4,3,2,1,0:T(8,128)(2,1)S(1)}, u32[]{:S(2)}, u32[]{:S(2)}) collective-permute-start(bf16[2,1,2,128,1152]{4,3,2,1,0:T(8,128)(2,1)S(1)} %constant_dynamic-slice_fusion.1), channel_id=1, source_target_pairs={{0,4},{4,0},{8,12},{12,8},{16,20},{20,16},{24,28},{28,24},{1,5},{5... | collective-permute-start | bytes 3538952 | tf_op jit(solution)/shard_map/ppermute | solution.py:406
  435.3 24.5 %collective-permute-start.14 = (bf16[4,2,1,1,32,2048]{5,4,3,2,1,0:T(8,128)(2,1)S(1)}, bf16[4,2,1,1,32,2048]{5,4,3,2,1,0:T(8,128)(2,1)S(1)}, u32[]{:S(2)}, u32[]{:S(2)}) collective-permute-start(bf16[4,2,1,1,32,2048]{5,4,3,2,1,0:T(8,128)(2,1)S(1)} %constant_dynamic-slice_fusion.16), channel_id=1, source_target_pairs={{0,8},{4,12},{8,0},{12,4},{16,24},{20,28},{24,16},{28,20},{1,9},{5... | collective-permute-start | bytes 3145736 | tf_op jit(solution)/shard_map/ppermute | solution.py:406
  437.2 26.7 %collective-permute-start.6 = (bf16[4,1,2,1,32,2176]{5,4,3,2,1,0:T(8,128)(2,1)S(1)}, bf16[4,1,2,1,32,2176]{5,4,3,2,1,0:T(8,128)(2,1)S(1)}, u32[]{:S(2)}, u32[]{:S(2)}) collective-permute-start(bf16[4,1,2,1,32,2176]{5,4,3,2,1,0:T(8,128)(2,1)S(1)} %constant_dynamic-slice_fusion.22), channel_id=1, source_target_pairs={{0,16},{4,20},{8,24},{12,28},{16,0},{20,4},{24,8},{28,12},{1,17},{... | collective-permute-start | bytes 3342344 | tf_op jit(solution)/shard_map/ppermute | solution.py:406
  437.8 85.5 %collective-permute-start.35 = (bf16[2,576,1024]{2,1,0:T(8,128)(2,1)S(1)}, bf16[2,576,1024]{2,1,0:T(8,128)(2,1)S(1)}, u32[]{:S(2)}, u32[]{:S(2)}) collective-permute-start(bf16[2,576,1024]{2,1,0:T(8,128)(2,1)S(1)} %constant_dynamic-update-slice_fusion), channel_id=1, source_target_pairs={{0,4},{2,6},{5,1},{7,3},{8,12},{10,14},{13,9},{15,11},{16,20},{18,... | collective-permute-start | bytes 7077896 | tf_op jit(solution)/shard_map/ppermute | solution.py:412
  460.3 14.8 %collective-permute-start.15 = (bf16[4,1,1,1,32,2048]{5,4,3,2,1,0:T(8,128)(2,1)S(1)}, bf16[4,1,1,1,32,2048]{5,4,3,2,1,0:T(8,128)(2,1)S(1)}, u32[]{:S(2)}, u32[]{:S(2)}) collective-permute-start(bf16[4,1,1,1,32,2048]{5,4,3,2,1,0:T(8,128)(2,1)S(1)} %constant_dynamic-slice_fusion.15), channel_id=1, source_target_pairs={{0,16},{4,20},{8,24},{12,28},{16,0},{20,4},{24,8},{28,12},{1,17},{... | collective-permute-start | bytes 1572872 | tf_op jit(solution)/shard_map/ppermute | solution.py:406
  464.3 16.8 %collective-permute-start.7 = (bf16[4,1,1,1,32,2176]{5,4,3,2,1,0:T(8,128)(2,1)S(1)}, bf16[4,1,1,1,32,2176]{5,4,3,2,1,0:T(8,128)(2,1)S(1)}, u32[]{:S(2)}, u32[]{:S(2)}) collective-permute-start(bf16[4,1,1,1,32,2176]{5,4,3,2,1,0:T(8,128)(2,1)S(1)} %constant_dynamic-slice_fusion.21), channel_id=1, source_target_pairs={{0,8},{4,12},{8,0},{12,4},{16,24},{20,28},{24,16},{28,20},{1,9},{5... | collective-permute-start | bytes 1671176 | tf_op jit(solution)/shard_map/ppermute | solution.py:406
  475.3 11.2 %collective-permute-start.16 = (bf16[2,32,2048]{2,1,0:T(8,128)(2,1)S(1)}, bf16[2,32,2048]{2,1,0:T(8,128)(2,1)S(1)}, u32[]{:S(2)}, u32[]{:S(2)}) collective-permute-start(bf16[2,32,2048]{2,1,0:T(8,128)(2,1)S(1)} %slice_bitcast_fusion.16), channel_id=1, source_target_pairs={{0,1},{1,0},{2,3},{3,2},{4,5},{5,4},{6,7},{7,6},{8,9},{9,8},{10,11... | collective-permute-start | bytes 786440 | tf_op jit(solution)/shard_map/ppermute | solution.py:409
  486.6 6.0 %collective-permute-start.17 = (bf16[32,2048]{1,0:T(8,128)(2,1)S(1)}, bf16[32,2048]{1,0:T(8,128)(2,1)S(1)}, u32[]{:S(2)}, u32[]{:S(2)}) collective-permute-start(bf16[32,2048]{1,0:T(8,128)(2,1)S(1)} %slice_bitcast_fusion.20), channel_id=1, source_target_pairs={{0,2},{1,3},{2,0},{3,1},{4,6},{5,7},{6,4},{7,5},{8,10},{9,11},{10,... | collective-permute-start | bytes 393224 | tf_op jit(solution)/shard_map/ppermute | solution.py:409
  489.5 9.6 %collective-permute-start.8 = (bf16[2,32,2176]{2,1,0:T(8,128)(2,1)S(1)}, bf16[2,32,2176]{2,1,0:T(8,128)(2,1)S(1)}, u32[]{:S(2)}, u32[]{:S(2)}) collective-permute-start(bf16[2,32,2176]{2,1,0:T(8,128)(2,1)S(1)} %slice_bitcast_fusion.14), channel_id=1, source_target_pairs={{0,1},{1,0},{2,3},{3,2},{4,5},{5,4},{6,7},{7,6},{8,9},{9,8},{10,11... | collective-permute-start | bytes 835592 | tf_op jit(solution)/shard_map/ppermute | solution.py:409
  492.7 7.1 %collective-permute-start.18 = (bf16[1,1,1,32,2048]{4,3,2,1,0:T(8,128)(2,1)S(1)}, bf16[1,1,1,32,2048]{4,3,2,1,0:T(8,128)(2,1)S(1)}, u32[]{:S(2)}, u32[]{:S(2)}) collective-permute-start(bf16[1,1,1,32,2048]{4,3,2,1,0:T(8,128)(2,1)S(1)} %constant_dynamic-slice_fusion.14), channel_id=1, source_target_pairs={{0,16},{4,20},{8,24},{12,28},{16,0},{20,4},{24,8},{28,12},{1,17},{... | collective-permute-start | bytes 393224 | tf_op jit(solution)/shard_map/ppermute | solution.py:406
  499.2 8.2 %collective-permute-start.9 = (bf16[32,2176]{1,0:T(8,128)(2,1)S(1)}, bf16[32,2176]{1,0:T(8,128)(2,1)S(1)}, u32[]{:S(2)}, u32[]{:S(2)}) collective-permute-start(bf16[32,2176]{1,0:T(8,128)(2,1)S(1)} %slice_bitcast_fusion.18), channel_id=1, source_target_pairs={{0,2},{1,3},{2,0},{3,1},{4,6},{5,7},{6,4},{7,5},{8,10},{9,11},{10,... | collective-permute-start | bytes 417800 | tf_op jit(solution)/shard_map/ppermute | solution.py:409
  507.6 5.4 %collective-permute-start.10 = (bf16[1,1,1,32,2176]{4,3,2,1,0:T(8,128)(2,1)S(1)}, bf16[1,1,1,32,2176]{4,3,2,1,0:T(8,128)(2,1)S(1)}, u32[]{:S(2)}, u32[]{:S(2)}) collective-permute-start(bf16[1,1,1,32,2176]{4,3,2,1,0:T(8,128)(2,1)S(1)} %constant_dynamic-slice_fusion.20), channel_id=1, source_target_pairs={{0,8},{4,12},{8,0},{12,4},{16,24},{20,28},{24,16},{28,20},{1,9},{5... | collective-permute-start | bytes 417800 | tf_op jit(solution)/shard_map/ppermute | solution.py:406
  510.2 8.5 %collective-permute-start.19 = (bf16[2,1,1,32,2048]{4,3,2,1,0:T(8,128)(2,1)S(1)}, bf16[2,1,1,32,2048]{4,3,2,1,0:T(8,128)(2,1)S(1)}, u32[]{:S(2)}, u32[]{:S(2)}) collective-permute-start(bf16[2,1,1,32,2048]{4,3,2,1,0:T(8,128)(2,1)S(1)} %constant_dynamic-slice_fusion.13), channel_id=1, source_target_pairs={{0,8},{4,12},{8,0},{12,4},{16,24},{20,28},{24,16},{28,20},{1,9},{5... | collective-permute-start | bytes 786440 | tf_op jit(solution)/shard_map/ppermute | solution.py:406
  513.1 7.4 %collective-permute-start.11 = (bf16[1,2,1,32,2176]{4,3,2,1,0:T(8,128)(2,1)S(1)}, bf16[1,2,1,32,2176]{4,3,2,1,0:T(8,128)(2,1)S(1)}, u32[]{:S(2)}, u32[]{:S(2)}) collective-permute-start(bf16[1,2,1,32,2176]{4,3,2,1,0:T(8,128)(2,1)S(1)} %constant_dynamic-slice_fusion.19), channel_id=1, source_target_pairs={{0,16},{4,20},{8,24},{12,28},{16,0},{20,4},{24,8},{28,12},{1,17},{... | collective-permute-start | bytes 835592 | tf_op jit(solution)/shard_map/ppermute | solution.py:406
  518.8 4.2 collective-permute-start.20
  520.6 5.8 %collective-permute-start.12 = (bf16[2,2,1,32,2176]{4,3,2,1,0:T(8,128)(2,1)S(1)}, bf16[2,2,1,32,2176]{4,3,2,1,0:T(8,128)(2,1)S(1)}, u32[]{:S(2)}, u32[]{:S(2)}) collective-permute-start(bf16[2,2,1,32,2176]{4,3,2,1,0:T(8,128)(2,1)S(1)} %constant_dynamic-slice_fusion.18), channel_id=1, source_target_pairs={{0,4},{4,0},{8,12},{12,8},{16,20},{20,16},{24,28},{28,24},{1,5},{5... | collective-permute-start | bytes 1671176 | tf_op jit(solution)/shard_map/ppermute | solution.py:406
  (26 other events, 88.1 us)

commit v3 on v2

v3 whole, which is shorter than its diff:
```python
import functools
import jax
import jax.numpy as jnp
from jax import lax
from jax.experimental import pallas as pl
from jax.experimental.pallas import tpu as pltpu
from jax.sharding import PartitionSpec as P

low = jnp.bfloat16
full = jnp.float32
MESH = pl.DeviceIdType.MESH
epsilon = 1e-06
MIB = 1 << 20


def mirrored(index, weight):
    return index + weight - 2 * weight * ((index // weight) % 2)


class Net:
    def __init__(self, me, z, send_sems, recv_sems, local_sems):
        self.me, self.z = me, z
        self.send_sems, self.recv_sems, self.local_sems = send_sems, recv_sems, local_sems
        self.count = self.local_count = 0

    def seat(self, name):
        me, z = self.me, self.z
        return {
            "core": {"seq": mirrored(me, 1), "wsh": z},
            "x": {"seq": mirrored(me, 2), "wsh": z},
            "y": {"seq": mirrored(me, 4), "wsh": z},
            "z1": {"seq": me, "wsh": mirrored(z, 1)},
            "z2": {"seq": me, "wsh": mirrored(z, 2)},
            "z3": {"seq": me, "wsh": 3 - z},
        }[name]

    def make(self, src, dst, seat, k=None):
        if k is None:
            k = self.count
            self.count += 1
        return pltpu.make_async_remote_copy(
            src_ref=src,
            dst_ref=dst,
            send_sem=self.send_sems.at[k],
            recv_sem=self.recv_sems.at[k],
            device_id=self.seat(seat) if isinstance(seat, str) else seat,
            device_id_type=MESH,
        )

    def send(self, src, dst, seat):
        copy = self.make(src, dst, seat)
        copy.start()
        return copy

    def move(self, src, dst):
        k = self.local_count
        self.local_count += 1
        copy = pltpu.make_async_copy(src, dst, self.local_sems.at[k])
        copy.start()
        return copy


def greet(seats):
    barrier = pltpu.get_barrier_semaphore()
    for seat in seats:
        pl.semaphore_signal(barrier, inc=1, device_id=seat, device_id_type=MESH)
    pl.semaphore_wait(barrier, len(seats))


def inner(left, right):
    return lax.dot_general(left, right, (((0,), (0,)), ((), ())), preferred_element_type=full)


def outer(left, right):
    return lax.dot_general(left, right, (((1,), (1,)), ((), ())), preferred_element_type=full)


def chunk_sizes(hq):
    chunk = hq // 3
    return chunk, 2 * chunk


def gather_kernel(
    seq,
    x_hbm, e_hbm, starts_ref, small_ref, win_hbm, wout_hbm, wgu_hbm, wdn_hbm,
    wc_out, wgu_out, wdn_out, e_out, h2_out, proj_out, first_out, zed_out, gext_out, small_out,
    wc, winf, woutf, wguf, wdnf, wgu_own, wdn_own, x_ref, h_ref, proj, gext, zed, first, h2, small_all,
    send_sems, recv_sems, local_sems,
):
    me, z = lax.axis_index("seq"), lax.axis_index("wsh")
    net = Net(me, z, send_sems, recv_sems, local_sems)
    core, xbit, ybit = me % 2, (me // 2) % 2, (me // 4) % 2
    quarter = me % 4
    rows, width = x_hbm.shape
    part = width // 4
    hq = wdn_hbm.shape[0]
    hidden = 4 * hq
    half = part // 2
    z1, z2, z3 = mirrored(z, 1), mirrored(z, 2), 3 - z
    after = {"seq": lax.rem(me + 1, seq), "wsh": z}
    before = {"seq": lax.rem(me + seq - 1, seq), "wsh": z}

    load_wout = net.move(wout_hbm, woutf)
    load_win = net.move(win_hbm, winf)
    load_x = net.move(x_hbm, x_ref.at[pl.ds(16, rows)])
    chunk, pair = chunk_sizes(hq)
    load_gu = []
    for k in range(3):
        for base, shift in ((quarter * hq, 0), (hidden + quarter * hq, chunk)):
            cut = pl.ds(pl.multiple_of(base + k * chunk, 128), chunk)
            load_gu.append(
                net.move(wgu_hbm.at[:, cut], wguf.at[:, pl.ds(k * pair + shift, chunk)])
            )
    load_dn = net.move(wdn_hbm, wdnf)
    keep_e = net.move(e_hbm, e_out.at[0])

    greet([net.seat(n) for n in ("core", "x", "y", "z1", "z2", "z3")] + [before])

    small_all[z] = small_ref[...]
    smalls = [net.send(small_ref, small_all.at[z], n) for n in ("z1", "z2", "z3")]
    halo = net.send(x_hbm.at[pl.ds(rows - 16, 16)], x_ref.at[pl.ds(0, 16)], after)

    load_win.wait()
    load_wout.wait()
    piece = part // 8

    def cast_block(i, carry):
        at = pl.ds(pl.multiple_of(i * piece, piece), piece)
        wc[z, i // 2, i % 2, :, : 3 * width] = winf[at].astype(low)
        wc[z, i // 2, i % 2, :, 3 * width :] = woutf[at].astype(low)
        return carry

    lax.fori_loop(0, 8, cast_block, 0)
    spot = ybit * 2 + xbit
    spot_x = ybit * 2 + 1 - xbit
    spot_y = (1 - ybit) * 2 + xbit
    cols = [pl.ds(0, 2 * width), pl.ds(2 * width, 2 * width)]

    def own(zz):
        return wc.at[zz, spot, core]

    a1 = net.send(own(z), own(z), "z1")
    a2 = net.send(own(z), own(z), "z2")

    for copy in load_gu:
        copy.wait()
    wgu_own[...] = wguf[...].astype(low)
    keep_gu = net.move(wgu_own, wgu_out.at[z])
    load_dn.wait()
    cast_rows = hq // 4

    def cast_dn(i, carry):
        at = pl.ds(pl.multiple_of(i * cast_rows, cast_rows), cast_rows)
        wdn_own[at] = wdnf[at].astype(low)
        return carry

    lax.fori_loop(0, 4, cast_dn, 0)

    def spread(zz):
        bx = net.send(own(zz), own(zz), "x")
        by = net.send(own(zz), own(zz), "y")
        return bx, by

    def onward(zz, b):
        bx, by = b
        bx.wait_recv()
        d0 = net.send(wc.at[zz, spot_x, core, :, cols[0]], wc.at[zz, spot_x, core, :, cols[0]], "y")
        by.wait_recv()
        d1 = net.send(wc.at[zz, spot_y, core, :, cols[1]], wc.at[zz, spot_y, core, :, cols[1]], "x")
        return d0, d1

    def across(zz, d):
        d[0].wait_recv()
        d[1].wait_recv()
        return net.send(wc.at[zz, :, core], wc.at[zz, :, core], "core")

    a1.wait_recv()
    b1 = spread(z1)
    a2.wait_recv()
    a3 = net.send(own(z2), own(z2), "z1")
    b2 = spread(z2)

    def gu(zz, yy):
        return wgu_out.at[zz, pl.ds(pl.multiple_of(yy * half, half), half)]

    gu_own = wgu_own.at[pl.ds(pl.multiple_of(ybit * half, half), half)]
    f1 = net.send(gu_own, gu(z, ybit), "z1")
    f2 = net.send(gu_own, gu(z, ybit), "z2")
    d1 = onward(z1, b1)
    d2 = onward(z2, b2)
    a3.wait_recv()
    b3 = spread(z3)
    same0 = (z % 2) == (quarter % 2)
    same1 = (z // 2) == (quarter // 2)
    holder = same0 & same1
    dn_own = wdn_own.at[pl.ds(pl.multiple_of(ybit * (hq // 2), 32), hq // 2)]
    dn_spot = wdn_out.at[ybit]
    dn2 = net.make(dn_own, dn_spot, "z2")
    dn1a = net.make(dn_own, dn_spot, "z1")
    dn1b = net.make(dn_spot, dn_spot, "z1", net.count - 1)
    dny = net.make(dn_spot, dn_spot, "y")
    keep_dn = [
        pltpu.make_async_copy(
            wdn_own.at[pl.ds(i * (hq // 2), hq // 2)], wdn_out.at[i], local_sems.at[24 + i]
        )
        for i in range(2)
    ]

    @pl.when(holder)
    def _():
        dn2.start()
        dn1a.start()
        for copy in keep_dn:
            copy.start()

    ex = net.send(e_hbm, e_out.at[1], "x")
    ec = net.send(e_hbm, e_out.at[2], "core")
    c1 = across(z1, d1)
    c2 = across(z2, d2)
    d3 = onward(z3, b3)
    f1.wait_recv()
    g1 = net.send(gu(z1, ybit), gu(z1, ybit), "y")
    c3 = across(z3, d3)
    f2.wait_recv()
    f3 = net.send(gu(z2, ybit), gu(z2, ybit), "z1")
    g2 = net.send(gu(z2, ybit), gu(z2, ybit), "y")

    for s in smalls:
        s.wait_recv()
    load_x.wait()
    halo.wait_recv()

    def row_of(k):
        return jnp.concatenate([small_all[i, k : k + 1, :] for i in range(4)], 1).astype(full)

    gain_one, gain_two = row_of(0), row_of(1)

    def norm_one(i, carry):
        at = pl.ds(pl.multiple_of(i * 176, 16), 176)
        xf = x_ref[at].astype(full)
        rate = lax.rsqrt(jnp.mean(xf * xf, axis=-1, keepdims=True) + epsilon)
        h_ref[at] = (xf * rate * gain_one).astype(low)
        return carry

    lax.fori_loop(0, (rows + 16) // 176, norm_one, 0)
    for c in (c1, c2, c3):
        c.wait_recv()

    def project(i, carry):
        at = pl.ds(pl.multiple_of(i * 512, 512), 512)
        proj[:, at] = jnp.dot(
            h_ref[...], wc[:, :, :, :, at].reshape(width, 512), preferred_element_type=full
        )
        return carry

    lax.fori_loop(0, 6, project, 0)
    keep_wc = net.move(wc, wc_out)
    keep_proj = net.move(proj.at[pl.ds(16, rows)], proj_out)

    place = me * rows + lax.broadcasted_iota(jnp.int32, (rows, 1), 0)
    starts = starts_ref[...]
    keep_one = (place - 1 >= starts).astype(full)
    keep_two = (place - 2 >= starts).astype(full)
    cw = 128

    def mix(i, carry):
        at = pl.ds(pl.multiple_of(i * cw, cw), cw)
        xat = pl.ds(pl.multiple_of(2 * width + i * cw, cw), cw)
        cat = pl.ds(pl.multiple_of(width + i * cw, cw), cw)
        gext[:, at] = (proj[:, at] * proj[:, xat]).astype(low).astype(full)
        zi = i // (part // cw)
        inside = pl.ds(pl.multiple_of((i % (part // cw)) * cw, cw), cw)
        taps = small_all[zi, :, inside].astype(full)
        mixed = (
            taps[2:3] * gext[16:, at]
            + keep_one * taps[3:4] * gext[15 : rows + 15, at]
            + keep_two * taps[4:5] * gext[14 : rows + 14, at]
        )
        zed[:, at] = (proj[16:, cat] * mixed).astype(low)
        return carry

    lax.fori_loop(0, width // cw, mix, 0)
    keep_zed = net.move(zed, zed_out)
    keep_gext = net.move(gext, gext_out)

    def project_out(i, carry):
        at = pl.ds(pl.multiple_of(i * 512, 512), 512)
        wat = pl.ds(pl.multiple_of(3 * width + i * 512, 512), 512)
        first[:, at] = x_ref[16:, at].astype(full) + jnp.dot(
            zed[...], wc[:, :, :, :, wat].reshape(width, 512), preferred_element_type=full
        )
        return carry

    lax.fori_loop(0, 2, project_out, 0)
    keep_first = net.move(first, first_out)

    def norm_two(i, carry):
        at = pl.ds(pl.multiple_of(i * 128, 128), 128)
        xf = first[at]
        rate = lax.rsqrt(jnp.mean(xf * xf, axis=-1, keepdims=True) + epsilon)
        h2[at] = (xf * rate * gain_two).astype(low)
        return carry

    lax.fori_loop(0, rows // 128, norm_two, 0)
    keep_h2 = net.move(h2, h2_out.at[0])
    hx = net.send(h2, h2_out.at[1], "x")
    hc = net.send(h2, h2_out.at[2], "core")
    keep_small = net.move(small_all, small_out)

    ex.wait_recv()
    exc = net.send(e_out.at[1], e_out.at[3], "core")

    @pl.when(same0 & ~same1)
    def _():
        dn2.wait_recv()
        dn1b.start()
        dny.start()

    f3.wait_recv()
    g3 = net.send(gu(z3, ybit), gu(z3, ybit), "y")

    @pl.when(~same0)
    def _():
        dn1a.wait_recv()
        dny.start()

    hx.wait_recv()
    hxc = net.send(h2_out.at[1], h2_out.at[3], "core")
    for c in (g1, g2, g3, ec, exc, hc, hxc):
        c.wait_recv()

    @pl.when(~holder)
    def _():
        dny.wait()

    @pl.when(holder)
    def _():
        dn2.wait_send()
        dn1a.wait_send()
        for copy in keep_dn:
            copy.wait()

    @pl.when(same0 & ~same1)
    def _():
        dn1b.wait_send()

    for c in (
        *smalls, halo, a1, a2, a3, *b1, *b2, *b3, *d1, *d2, *d3, c1, c2, c3,
        f1, f2, f3, g1, g2, g3, ex, ec, exc, hx, hc, hxc,
    ):
        c.wait_send()
    for c in (keep_e, keep_gu, keep_wc, keep_proj, keep_zed, keep_gext, keep_first, keep_h2, keep_small):
        c.wait()


def gather(seq, x, e, starts, small, win, wout, wgu, wdn):
    rows, width = x.shape
    part = width // 4
    hq = wdn.shape[0]
    shape = jax.ShapeDtypeStruct
    anyspace = pl.BlockSpec(memory_space=pl.ANY)
    vmem = pl.BlockSpec(memory_space=pltpu.VMEM)
    conv = (4, 4, 2, part // 8, 4 * width)
    outs = [
        shape(conv, low),
        shape((4, part, 2 * hq), low),
        shape((2, hq // 2, width), low),
        shape((4, rows, width), low),
        shape((4, rows, width), low),
        shape((rows, 3 * width), full),
        shape((rows, width), full),
        shape((rows, width), low),
        shape((rows + 16, width), full),
        shape((4, 16, part), low),
    ]
    scratch = [
        pltpu.VMEM(conv, low),
        pltpu.VMEM((part, 3 * width), full),
        pltpu.VMEM((part, width), full),
        pltpu.VMEM((part, 2 * hq), full),
        pltpu.VMEM((hq, width), full),
        pltpu.VMEM((part, 2 * hq), low),
        pltpu.VMEM((hq, width), low),
        pltpu.VMEM((rows + 16, width), low),
        pltpu.VMEM((rows + 16, width), low),
        pltpu.VMEM((rows + 16, 3 * width), full),
        pltpu.VMEM((rows + 16, width), full),
        pltpu.VMEM((rows, width), low),
        pltpu.VMEM((rows, width), full),
        pltpu.VMEM((rows, width), low),
        pltpu.VMEM((4, 16, part), low),
        pltpu.SemaphoreType.DMA((48,)),
        pltpu.SemaphoreType.DMA((48,)),
        pltpu.SemaphoreType.DMA((26,)),
    ]
    return pl.pallas_call(
        functools.partial(gather_kernel, seq),
        out_shape=outs,
        in_specs=[anyspace, anyspace, vmem, vmem] + [anyspace] * 4,
        out_specs=[anyspace] * len(outs),
        scratch_shapes=scratch,
        compiler_params=pltpu.CompilerParams(
            collective_id=0, has_side_effects=True, vmem_limit_bytes=56 * MIB
        ),
        name="gather",
    )(x, e, starts, small, win, wout, wgu, wdn)


def feed_kernel(
    seq,
    h2_hbm, e_hbm, wgu_hbm, wdn_hbm, first_hbm,
    result_out, dh2_out, gu0_out, gu1_out, gu2_out, dn_out, land_out,
    h2, h2t, e, wgu, wdn, a, at_ref, du, u, da, dgu, ddn, send_a, send_b, send_x, temp, acc, acc_out, result,
    gu0_y, gu2_y, dn_y, gu0_z1, gu0_z2, gu1_z1, gu1_z2, gu1_y, gu0_s, gu1_s, gu1_t, gu0_f, gu1_f,
    send_sems, recv_sems, local_sems,
):
    me, z = lax.axis_index("seq"), lax.axis_index("wsh")
    net = Net(me, z, send_sems, recv_sems, local_sems)
    ybit = (me // 4) % 2
    rows, width = first_hbm.shape
    hq = wdn.shape[0]
    chunk, pair = chunk_sizes(hq)
    part = width // 4
    half = part // 2
    z1, z2, z3 = mirrored(z, 1), mirrored(z, 2), 3 - z
    block = 4 * rows

    load_h2 = [net.move(h2_hbm.at[j], h2.at[pl.ds(j * rows, rows)]) for j in range(4)]
    load_gu = [net.move(wgu_hbm.at[i], wgu.at[pl.ds(i * part, part)]) for i in range(4)]
    load_e = [net.move(e_hbm.at[j], e.at[pl.ds(j * rows, rows)]) for j in range(4)]
    load_dn = net.move(wdn_hbm, wdn)
    load_first = net.move(first_hbm, acc_out)
    greet([net.seat(n) for n in ("core", "x", "y", "z1", "z2")])
    for c in load_h2:
        c.wait()

    def turn(j, carry):
        at = pl.ds(pl.multiple_of(j * 256, 256), 256)
        h2t[:, at] = h2[at].T
        return carry

    lax.fori_loop(0, block // 256, turn, 0)
    for c in load_gu + load_e + [load_dn]:
        c.wait()

    def forward(k):
        pcols, ccols = pl.ds(k * pair, pair), pl.ds(k * chunk, chunk)

        def one(j, carry):
            at = pl.ds(pl.multiple_of(j * rows, rows), rows)
            u[...] = jnp.dot(h2[at], wgu[:, pcols], preferred_element_type=full)
            da[...] = outer(e[at], wdn[ccols])

            def piece(r, carry):
                rr = pl.ds(pl.multiple_of(r * 64, 64), 64)
                tt = pl.ds(pl.multiple_of(j * rows + r * 64, 64), 64)
                gate, upper, back = u[rr, :chunk], u[rr, chunk:], da[rr]
                sigma = jax.nn.sigmoid(gate)
                swish = gate * sigma
                a[tt, ccols] = (swish * upper).astype(low)
                du[tt, pl.ds(k * pair, chunk)] = (
                    back * upper * (sigma * (1.0 + gate * (1.0 - sigma)))
                ).astype(low)
                du[tt, pl.ds(k * pair + chunk, chunk)] = (back * swish).astype(low)
                return carry

            lax.fori_loop(0, rows // 64, piece, 0)
            at_ref[:, at] = a[at, ccols].T
            return carry

        lax.fori_loop(0, 4, one, 0)

    def weights(k):
        def gate_up(n, carry):
            cols = pl.ds(pl.multiple_of(k * pair + n * 256, 256), 256)
            got = jnp.dot(h2t[...], du[:, cols], preferred_element_type=full).astype(low)
            dgu[:, :, :, cols] = got.reshape(4, 2, half, 256)
            return carry

        lax.fori_loop(0, pair // 256, gate_up, 0)

        def down(n, carry):
            cols = pl.ds(pl.multiple_of(n * 512, 512), 512)
            got = jnp.dot(at_ref[...], e[:, cols], preferred_element_type=full).astype(low)
            ddn[k, :, :, cols] = got.reshape(2, chunk // 2, 512)
            return carry

        lax.fori_loop(0, width // 512, down, 0)

    def cols_of(k):
        return pl.ds(k * pair, pair)

    forward(0)
    weights(0)
    y0 = net.send(dgu.at[:, 1 - ybit, :, cols_of(0)], gu0_y, "y")
    yd0 = net.send(ddn.at[0, 1 - ybit], dn_y.at[0], "y")
    forward(1)
    weights(1)
    m1 = net.send(dgu.at[z1, :, :, cols_of(1)], gu1_z1.at[0], "z1")
    m2 = net.send(dgu.at[z3, :, :, cols_of(1)], gu1_z1.at[1], "z1")
    yd1 = net.send(ddn.at[1, 1 - ybit], dn_y.at[1], "y")
    forward(2)

    def grad_rows(j, put):
        at = pl.ds(j * rows, rows)

        def one(n, carry):
            cols = pl.ds(pl.multiple_of(n * 256, 256), 256)
            put(cols, outer(du[at], wgu[cols]))
            return carry

        lax.fori_loop(0, width // 256, one, 0)

    def out_rows(j, put):
        at = pl.ds(j * rows, rows)

        def one(n, carry):
            cols = pl.ds(pl.multiple_of(n * 256, 256), 256)
            put(cols, jnp.dot(a[at], wdn[:, cols], preferred_element_type=full))
            return carry

        lax.fori_loop(0, width // 256, one, 0)

    def store(ref):
        def put(cols, value):
            ref[:, cols] = value.astype(low)

        return put

    def add(target, other):
        def put(cols, value):
            target[:, cols] = (value + other[:, cols].astype(full)).astype(target.dtype)

        return put

    def fetch(j):
        copy = net.move(land_out.at[j], temp)
        copy.wait()

    grad_rows(3, store(send_a))
    ga = net.send(send_a, land_out.at[0], "core")
    weights(2)
    y2 = net.send(dgu.at[:, 1 - ybit, :, cols_of(2)], gu2_y, "y")
    yd2 = net.send(ddn.at[2, 1 - ybit], dn_y.at[2], "y")
    ga.wait_recv()
    fetch(0)
    grad_rows(1, add(send_x, temp))
    gx = net.send(send_x, land_out.at[1], "x")

    def sum_rows(put, count, step):
        def one(i, carry):
            put(pl.ds(pl.multiple_of(i * step, step), step))
            return carry

        lax.fori_loop(0, count // step, one, 0)

    y0.wait_recv()

    def gu0_sum(i, carry):
        gu0_s[i] = (dgu[i, ybit, :, cols_of(0)].astype(full) + gu0_y[i].astype(full)).astype(low)
        return carry

    lax.fori_loop(0, 4, gu0_sum, 0)
    n1 = net.send(gu0_s.at[z1], gu0_z1.at[0], "z1")
    n2 = net.send(gu0_s.at[z3], gu0_z1.at[1], "z1")
    grad_rows(2, store(send_b))
    gb = net.send(send_b, land_out.at[2], "core")

    def keep(cols, value):
        acc[:, cols] = value

    grad_rows(0, keep)
    m1.wait_recv()
    m2.wait_recv()

    def gu1_sum(i, carry):
        gu1_t[i] = (dgu[z2, i, :, cols_of(1)].astype(full) + gu1_z1[1, i].astype(full)).astype(low)
        gu1_s[i] = (dgu[z, i, :, cols_of(1)].astype(full) + gu1_z1[0, i].astype(full)).astype(low)
        return carry

    lax.fori_loop(0, 2, gu1_sum, 0)
    m3 = net.send(gu1_t, gu1_z2, "z2")
    gb.wait_recv()
    fetch(2)

    def accumulate(target):
        def go(at):
            target[at] = target[at] + temp[at].astype(full)

        return go

    sum_rows(accumulate(acc), rows, 64)
    ga.wait_send()
    out_rows(3, store(send_a))
    oa = net.send(send_a, land_out.at[3], "core")
    n1.wait_recv()
    n2.wait_recv()
    own0 = (gu0_s[z2].astype(full) + gu0_z1[1].astype(full)).astype(low)
    gu0_f[1] = own0
    n3 = net.send(gu0_f.at[1], gu0_z2, "z2")
    gx.wait_recv()
    fetch(1)
    sum_rows(accumulate(acc), rows, 64)
    keep_dh2 = net.move(acc, dh2_out)
    oa.wait_recv()
    fetch(3)
    gx.wait_send()
    out_rows(1, add(send_x, temp))
    ox = net.send(send_x, land_out.at[4], "x")
    gb.wait_send()
    out_rows(2, store(send_b))
    ob = net.send(send_b, land_out.at[5], "core")
    load_first.wait()

    def more(cols, value):
        acc_out[:, cols] = acc_out[:, cols] + value

    out_rows(0, more)
    m3.wait_recv()

    def gu1_more(i, carry):
        gu1_s[i] = (gu1_s[i].astype(full) + gu1_z2[i].astype(full)).astype(low)
        return carry

    lax.fori_loop(0, 2, gu1_more, 0)
    m4 = net.send(gu1_s.at[1 - ybit], gu1_y, "y")
    n3.wait_recv()
    gu0_f[0] = (
        gu0_s[z].astype(full) + gu0_z1[0].astype(full) + gu0_z2[...].astype(full)
    ).astype(low)
    keep_gu0 = net.move(gu0_f.at[0], gu0_out)
    ob.wait_recv()
    fetch(5)
    sum_rows(accumulate(acc_out), rows, 64)
    ox.wait_recv()
    fetch(4)

    def finish(at):
        result[at] = (acc_out[at] + temp[at].astype(full)).astype(low)

    sum_rows(finish, rows, 64)
    keep_result = net.move(result, result_out)

    yd0.wait_recv()
    yd1.wait_recv()
    y2.wait_recv()

    def gu2_sum(i, carry):
        dgu[i, ybit, :, cols_of(2)] = (
            dgu[i, ybit, :, cols_of(2)].astype(full) + gu2_y[i].astype(full)
        ).astype(low)
        return carry

    lax.fori_loop(0, 4, gu2_sum, 0)
    keep_gu2 = net.move(dgu.at[:, ybit, :, cols_of(2)], gu2_out)
    yd2.wait_recv()

    def dn_sum(i, carry):
        ddn[i, ybit] = (ddn[i, ybit].astype(full) + dn_y[i].astype(full)).astype(low)
        return carry

    lax.fori_loop(0, 3, dn_sum, 0)
    keep_dn = net.move(ddn.at[:, ybit], dn_out)
    m4.wait_recv()
    gu1_f[...] = (gu1_s[ybit].astype(full) + gu1_y[...].astype(full)).astype(low)
    keep_gu1 = net.move(gu1_f, gu1_out)
    for c in (y0, yd0, m1, m2, yd1, y2, yd2, n1, n2, m3, oa, n3, ox, ob, m4):
        c.wait_send()
    for c in (keep_dh2, keep_gu0, keep_result, keep_gu2, keep_dn, keep_gu1):
        c.wait()


def feed(seq, h2_all, e_all, wgu, wdn, first):
    rows, width = first.shape
    part = width // 4
    half = part // 2
    hq = wdn.shape[0]
    chunk, pair = chunk_sizes(hq)
    shape = jax.ShapeDtypeStruct
    anyspace = pl.BlockSpec(memory_space=pl.ANY)
    outs = [
        shape((rows, width), low),
        shape((rows, width), full),
        shape((half, pair), low),
        shape((half, pair), low),
        shape((4, half, pair), low),
        shape((3, chunk // 2, width), low),
        shape((6, rows, width), low),
    ]
    v = pltpu.VMEM
    scratch = [
        v((4 * rows, width), low),
        v((width, 4 * rows), low),
        v((4 * rows, width), low),
        v((width, 2 * hq), low),
        v((hq, width), low),
        v((4 * rows, hq), low),
        v((chunk, 4 * rows), low),
        v((4 * rows, 2 * hq), low),
        v((rows, pair), full),
        v((rows, chunk), full),
        v((4, 2, half, 2 * hq), low),
        v((3, 2, chunk // 2, width), low),
        v((rows, width), low),
        v((rows, width), low),
        v((rows, width), low),
        v((rows, width), low),
        v((rows, width), full),
        v((rows, width), full),
        v((rows, width), low),
        v((4, half, pair), low),
        v((4, half, pair), low),
        v((3, chunk // 2, width), low),
        v((2, half, pair), low),
        v((half, pair), low),
        v((2, 2, half, pair), low),
        v((2, half, pair), low),
        v((half, pair), low),
        v((4, half, pair), low),
        v((2, half, pair), low),
        v((2, half, pair), low),
        v((2, half, pair), low),
        v((half, pair), low),
        pltpu.SemaphoreType.DMA((24,)),
        pltpu.SemaphoreType.DMA((24,)),
        pltpu.SemaphoreType.DMA((32,)),
    ]
    return pl.pallas_call(
        functools.partial(feed_kernel, seq),
        out_shape=outs,
        in_specs=[anyspace] * 5,
        out_specs=[anyspace] * len(outs),
        scratch_shapes=scratch,
        compiler_params=pltpu.CompilerParams(
            collective_id=1, has_side_effects=True, vmem_limit_bytes=63 * MIB
        ),
        name="feed",
    )(h2_all, e_all, wgu, wdn, first)


def finish_kernel(
    seq,
    starts_ref, small_all, x_hbm, e_hbm, first_hbm, dh2_hbm, proj_hbm, zed_hbm, gext_hbm, wc_hbm,
    gu0_hbm, gu1_hbm, gu2_hbm, dn_hbm,
    grad_out, gin_out, gout_out, ggu_out, gdn_out, gsmall_out, up_c, up_gu, up_dn,
    wc, first, dh2, x_ref, e_ref, proj, zed, ht, gext, dx1, dp, s1, s2, dwc,
    ret_send, ret_land, sums, sums_core, sums_plane, sums_z, small_out,
    cr, r1, r2, rz1, rz2, fin_c, fin_gu, fin_dn, g2, g2_z1, g2_z2, dnv, dn_z1, dn_z2, stage,
    send_sems, recv_sems, local_sems,
):
    me, z = lax.axis_index("seq"), lax.axis_index("wsh")
    net = Net(me, z, send_sems, recv_sems, local_sems)
    core, xbit, ybit = me % 2, (me // 2) % 2, (me // 4) % 2
    quarter = me % 4
    rows, width = first.shape
    part = width // 4
    half = part // 2
    chunk = dnv.shape[1] * 2
    pair = 2 * chunk
    hq = 3 * chunk
    hidden = 4 * hq
    z1, z2, z3 = mirrored(z, 1), mirrored(z, 2), 3 - z
    after = {"seq": lax.rem(me + 1, seq), "wsh": z}
    before = {"seq": lax.rem(me + seq - 1, seq), "wsh": z}
    cross = {"seq": mirrored(mirrored(me, 2), 4), "wsh": z}
    upper = [
        {"seq": mirrored(me, 1 << bit), "wsh": z} for bit in range(3, seq.bit_length() - 1)
    ]
    same0 = (z % 2) == (quarter % 2)
    same1 = (z // 2) == (quarter // 2)
    holder = same0 & same1
    level = core == z % 2

    load_gu2 = net.move(gu2_hbm, g2)
    load_dn = net.move(dn_hbm, dnv)
    load_gu = [
        net.move(gu0_hbm, fin_gu.at[0, xbit, core, ybit]),
        net.move(gu1_hbm, fin_gu.at[1, xbit, core, ybit]),
    ]
    load_first = net.move(first_hbm, first)
    load_dh2 = net.move(dh2_hbm, dh2)
    load_e = net.move(e_hbm, e_ref)
    load_wc = net.move(wc_hbm, wc)
    load_zed = net.move(zed_hbm, zed)
    zedt, do_ref, out_ref = ht, e_ref, zed
    load_x = net.move(x_hbm, x_ref)
    load_gext = net.move(gext_hbm, gext)
    load_proj = net.move(proj_hbm, proj)
    greet(
        [net.seat(n) for n in ("core", "x", "y", "z1", "z2", "z3")] + [after, cross] + upper
    )

    def plus_upper(ref, land, temp):
        for i, seat in enumerate(upper):
            copy = net.send(ref, land.at[i], seat)
            copy.wait()
            net.move(land.at[i], temp).wait()
            ref[...] = (ref[...].astype(full) + temp[...].astype(full)).astype(ref.dtype)

    load_gu2.wait()
    g1a = net.send(g2.at[z1], g2_z1.at[0], "z1")
    g1b = net.send(g2.at[z3], g2_z1.at[1], "z1")
    load_dn.wait()
    dn1 = net.make(dnv, dn_z1, "z1")
    dn2 = net.make(dnv, dn_z2, "z2")

    @pl.when(~same0)
    def _():
        dn1.start()

    def spread_gu(k):
        own = fin_gu.at[k, xbit, core, ybit]
        return net.send(own, own, "x"), net.send(own, own, "y")

    lo, hi = pl.ds(0, chunk), pl.ds(chunk, chunk)

    def onward_gu(k, b):
        b[0].wait_recv()
        spot = fin_gu.at[k, 1 - xbit, core, ybit, :, lo]
        first_half = net.send(spot, spot, "y")
        b[1].wait_recv()
        spot = fin_gu.at[k, xbit, core, 1 - ybit, :, hi]
        return first_half, net.send(spot, spot, "x")

    def across_gu(k, d):
        d[0].wait_recv()
        d[1].wait_recv()
        return net.send(fin_gu.at[k, :, core], fin_gu.at[k, :, core], "core")

    if not upper:
        for c in load_gu:
            c.wait()
        gu_b = [spread_gu(0), spread_gu(1)]
    else:
        gu_b = []
        for k in range(2):
            load_gu[k].wait()
            up_gu_own = fin_gu.at[k, xbit, core, ybit]
            plus_upper(up_gu_own, up_gu.at[k], dp.at[pl.ds(0, half), pl.ds(0, pair)])
            gu_b.append(spread_gu(k))

    def row_of(k):
        return jnp.concatenate([small_all[i, k : k + 1, :] for i in range(4)], 1).astype(full)

    gain_one, gain_two = row_of(0), row_of(1)
    sums[...] = jnp.zeros_like(sums)
    load_first.wait()
    load_dh2.wait()
    load_e.wait()
    tile = 32

    def folded(value):
        return jnp.sum(value.reshape(value.shape[0] // 8, 8, value.shape[1]), axis=0)

    def norm_two(i, total):
        at = pl.ds(pl.multiple_of(i * tile, tile), tile)
        xf, dh = first[at], dh2[at]
        rate = lax.rsqrt(jnp.mean(xf * xf, axis=-1, keepdims=True) + epsilon)
        normed = xf * rate
        scaled = dh * gain_two
        mean = jnp.mean(scaled * normed, axis=-1, keepdims=True)
        got = e_ref[at].astype(full) + rate * (scaled - normed * mean)
        dx1[at] = got
        do_ref[at] = got.astype(low)
        return total + folded(dh * normed)

    total = lax.fori_loop(0, rows // tile, norm_two, jnp.zeros((8, width), full))
    sums[1:2, :] = jnp.sum(total, axis=0, keepdims=True)

    load_wc.wait()
    dz = first

    def back_out(i, carry):
        cols = pl.ds(pl.multiple_of(i * part, part), part)
        dz[:, cols] = outer(do_ref[...], wc[i, :, :, :, 3 * width :].reshape(part, width))
        return carry

    lax.fori_loop(0, 4, back_out, 0)
    load_zed.wait()
    load_x.wait()

    def turn_zed(i, carry):
        cols = pl.ds(pl.multiple_of(i * 256, 256), 256)
        zedt[:, cols] = zed[cols].T
        return carry

    lax.fori_loop(0, rows // 256, turn_zed, 0)

    def weight_chunk(left, right, at):
        def one(n, carry):
            cols = pl.ds(pl.multiple_of(n * 256, 256), 256)
            into = pl.ds(pl.multiple_of(at + n * 256, 256), 256)
            got = jnp.dot(left[...], right(cols), preferred_element_type=full).astype(low)
            dwc[:, :, :, :, :, into] = got.reshape(4, 2, 2, 2, part // 8, 256)
            return carry

        lax.fori_loop(0, width // 256, one, 0)

    starts_at = [3 * width, width, 0, 2 * width]

    def cols_of(i):
        return pl.ds(starts_at[i], width)

    def to_core(i):
        return net.send(dwc.at[:, :, :, 1 - core, :, cols_of(i)], cr.at[i], "core")

    weight_chunk(zedt, lambda cols: do_ref[:, cols], 3 * width)
    sc = [to_core(0)]

    g1a.wait_recv()
    g1b.wait_recv()
    g2[z2] = (g2[z2].astype(full) + g2_z1[1].astype(full)).astype(low)
    g2s = net.send(g2.at[z2], g2_z2, "z2")

    def add_dn(i, carry):
        dnv[i] = (dnv[i].astype(full) + dn_z1[i].astype(full)).astype(low)
        return carry

    @pl.when(same0)
    def _():
        dn1.wait_recv()
        lax.fori_loop(0, 3, add_dn, 0)

    @pl.when(same0 & ~same1)
    def _():
        dn2.start()

    place = me * rows + lax.broadcasted_iota(jnp.int32, (rows, 1), 0)
    starts = starts_ref[...]
    keep_one = (place - 1 >= starts).astype(full)
    keep_two = (place - 2 >= starts).astype(full)
    load_gext.wait()
    load_proj.wait()
    s1[rows:] = jnp.zeros((s1.shape[0] - rows, 128), full)
    s2[rows:] = jnp.zeros((s2.shape[0] - rows, 128), full)
    dg = dh2
    row8 = lax.broadcasted_iota(jnp.int32, (8, 128), 0)

    def unmix(i, carry):
        at = pl.ds(pl.multiple_of(i * 128, 128), 128)
        cat = pl.ds(pl.multiple_of(width + i * 128, 128), 128)
        zi = i // (part // 128)
        inside = pl.ds(pl.multiple_of((i % (part // 128)) * 128, 128), 128)
        taps = small_all[zi, :, inside].astype(full)
        tap0, tap1, tap2 = taps[2:3], taps[3:4], taps[4:5]
        current, lag_one, lag_two = gext[16:, at], gext[15 : rows + 15, at], gext[14 : rows + 14, at]
        mixed = tap0 * current + keep_one * tap1 * lag_one + keep_two * tap2 * lag_two
        back = dz[:, at]
        dp[:, cat] = (back * mixed).astype(low)
        dm = back * proj[:, cat]
        t1, t2 = keep_one * dm, keep_two * dm
        for k, value in ((2, dm * current), (3, t1 * lag_one), (4, t2 * lag_two)):
            sums[k : k + 1, at] = jnp.sum(folded(value), axis=0, keepdims=True)
        s1[:rows] = tap1 * t1
        s2[:rows] = tap2 * t2
        dg[:, at] = tap0 * dm + s1[1 : rows + 1] + s2[2 : rows + 2]
        ret_send[:, at] = jnp.where(
            row8 == 6, s2[0:1], jnp.where(row8 == 7, s1[0:1] + s2[1:2], 0.0)
        )
        return carry

    lax.fori_loop(0, width // 128, unmix, 0)
    back = net.send(ret_send, ret_land, before)

    def norm_one(i, carry):
        at = pl.ds(pl.multiple_of(i * 128, 128), 128)
        xf = x_ref[at].astype(full)
        rate = lax.rsqrt(jnp.mean(xf * xf, axis=-1, keepdims=True) + epsilon)
        ht[:, at] = (xf * rate * gain_one).astype(low).T
        return carry

    lax.fori_loop(0, rows // 128, norm_one, 0)
    weight_chunk(ht, lambda cols: dp[:, pl.ds(pl.multiple_of(width + cols.start, 256), 256)], width)
    sc.append(to_core(1))

    orders = ["xy", "yx", "xy", "yx"]
    depth = part // 8

    def add_core(i):
        sc[i].wait_recv()

        def one(j, carry):
            zi, yi, xi = j // 4, (j // 2) % 2, j % 2
            spot = (zi, yi, xi, core, slice(None), cols_of(i))
            dwc[spot] = (dwc[spot].astype(full) + cr[i, zi, yi, xi].astype(full)).astype(low)
            return carry

        lax.fori_loop(0, 16, one, 0)
        cols = cols_of(i)
        if orders[i] == "xy":
            return net.send(dwc.at[:, :, 1 - xbit, core, :, cols], r1.at[i], "x")
        return net.send(dwc.at[:, 1 - ybit, :, core, :, cols], r1.at[i], "y")

    def add_first(i, copy):
        copy.wait_recv()

        def one(j, carry):
            zi, oi = j // 2, j % 2
            yi, xi = (oi, xbit) if orders[i] == "xy" else (ybit, oi)
            spot = (zi, yi, xi, core, slice(None), cols_of(i))
            dwc[spot] = (dwc[spot].astype(full) + r1[i, zi, oi].astype(full)).astype(low)
            return carry

        lax.fori_loop(0, 8, one, 0)
        cols = cols_of(i)
        if orders[i] == "xy":
            return net.send(dwc.at[:, 1 - ybit, xbit, core, :, cols], r2.at[i], "y")
        return net.send(dwc.at[:, ybit, 1 - xbit, core, :, cols], r2.at[i], "x")

    def add_second(i, copy):
        copy.wait_recv()

        def one(zi, carry):
            spot = (zi, ybit, xbit, core, slice(None), cols_of(i))
            dwc[spot] = (dwc[spot].astype(full) + r2[i, zi].astype(full)).astype(low)
            return carry

        lax.fori_loop(0, 4, one, 0)
        cols = cols_of(i)
        return (
            net.send(dwc.at[z1, ybit, xbit, core, :, cols], rz1.at[i, 0], "z1"),
            net.send(dwc.at[z3, ybit, xbit, core, :, cols], rz1.at[i, 1], "z1"),
        )

    def add_z1(i, copies):
        for c in copies:
            c.wait_recv()
        spot = (z2, ybit, xbit, core, slice(None), cols_of(i))
        dwc[spot] = (dwc[spot].astype(full) + rz1[i, 1].astype(full)).astype(low)
        return net.send(dwc.at[spot], rz2.at[i], "z2")

    def add_z2(i, copy):
        copy.wait_recv()
        spot = (z, ybit, xbit, core, slice(None), cols_of(i))
        own = fin_c.at[i, ybit, xbit, core]
        own[...] = (
            dwc[spot].astype(full) + rz1[i, 0].astype(full) + rz2[i].astype(full)
        ).astype(low)
        plus_upper(own, up_c.at[i], e_ref.at[pl.ds(0, part // 8)])
        return net.send(own, own, "x"), net.send(own, own, "y")

    def onward_c(i, copies):
        for c in copies:
            c.wait_recv()
        spot = fin_c.at[i, ybit, 1 - xbit, core]
        return net.send(spot, spot, "y")

    def across_c(i, copy):
        copy.wait_recv()
        return net.send(fin_c.at[i, :, :, core], fin_c.at[i, :, :, core], "core")

    a = {}
    b = {}
    a[0] = add_core(0)
    gu_d = [onward_gu(k, gu_b[k]) for k in range(2)]
    back.wait_recv()
    follows = (me < seq - 1).astype(full)
    dg[rows - 8 :] = dg[rows - 8 :] + ret_land[...] * follows

    def unproject(i, carry):
        at = pl.ds(pl.multiple_of(i * 128, 128), 128)
        xat = pl.ds(pl.multiple_of(2 * width + i * 128, 128), 128)
        dp[:, at] = (dg[:, at] * proj[:, xat]).astype(low)
        dp[:, xat] = (dg[:, at] * proj[:, at]).astype(low)
        return carry

    lax.fori_loop(0, width // 128, unproject, 0)
    weight_chunk(ht, lambda cols: dp[:, cols], 0)
    sc.append(to_core(2))
    a[1] = add_core(1)
    b[0] = add_first(0, a[0])
    weight_chunk(ht, lambda cols: dp[:, pl.ds(pl.multiple_of(2 * width + cols.start, 256), 256)], 2 * width)
    sc.append(to_core(3))
    a[2] = add_core(2)

    g2s.wait_recv()
    own = fin_gu.at[2, xbit, core, ybit]
    own[...] = (
        g2[z].astype(full) + g2_z1[0].astype(full) + g2_z2[...].astype(full)
    ).astype(low)
    plus_upper(own, up_gu.at[2], e_ref.at[pl.ds(0, half), pl.ds(0, pair)])
    gu_b.append(spread_gu(2))

    @pl.when(holder)
    def _():
        dn2.wait_recv()

        def one(i, carry):
            dnv[i] = (dnv[i].astype(full) + dn_z2[i].astype(full)).astype(low)
            return carry

        lax.fori_loop(0, 3, one, 0)
        plus_upper(dnv, up_dn, dn_z1)

        def two(i, carry):
            fin_dn[i, ybit] = dnv[i]
            return carry

        lax.fori_loop(0, 3, two, 0)

    dnx = net.make(fin_dn.at[:, ybit], fin_dn.at[:, ybit], "x")
    dny = net.make(fin_dn.at[:, ybit], fin_dn.at[:, ybit], "y")
    dnc = net.make(fin_dn, fin_dn, "core")

    @pl.when(holder)
    def _():
        dnx.start()
        dny.start()

    dh = dg

    def back_in(i, carry):
        cols = pl.ds(pl.multiple_of(i * part, part), part)
        dh[:, cols] = outer(dp[...], wc[i, :, :, :, : 3 * width].reshape(part, 3 * width))
        return carry

    lax.fori_loop(0, 4, back_in, 0)

    def norm_back(i, total):
        at = pl.ds(pl.multiple_of(i * tile, tile), tile)
        xf = x_ref[at].astype(full)
        rate = lax.rsqrt(jnp.mean(xf * xf, axis=-1, keepdims=True) + epsilon)
        normed = xf * rate
        got = dh[at]
        scaled = got * gain_one
        mean = jnp.mean(scaled * normed, axis=-1, keepdims=True)
        out_ref[at] = (dx1[at] + rate * (scaled - normed * mean)).astype(low)
        return total + folded(got * normed)

    total = lax.fori_loop(0, rows // tile, norm_back, jnp.zeros((8, width), full))
    keep_grad = net.move(out_ref, grad_out)
    sums[0:1, :] = jnp.sum(total, axis=0, keepdims=True)
    small_core = net.send(sums, sums_core, "core")
    a[3] = add_core(3)
    b[1] = add_first(1, a[1])
    c = {0: add_second(0, b[0])}
    gu_c = [across_gu(k, gu_d[k]) for k in range(2)]
    b[2] = add_first(2, a[2])
    small_core.wait()
    sums[...] = sums[...] + sums_core[...]
    small_plane = [
        net.send(sums, sums_plane.at[i], seat) for i, seat in enumerate(("x", "y", cross))
    ]
    c[1] = add_second(1, b[1])
    d = {0: add_z1(0, c[0])}
    b[3] = add_first(3, a[3])
    c[2] = add_second(2, b[2])

    @pl.when(level & ~holder)
    def _():
        dnx.wait_recv()
        dny.start()

    gu_d.append(onward_gu(2, gu_b[2]))
    d[1] = add_z1(1, c[1])
    c[3] = add_second(3, b[3])
    f = {0: add_z2(0, d[0])}
    for copy in small_plane:
        copy.wait()
    sums[...] = sums[...] + sums_plane[0] + sums_plane[1] + sums_plane[2]
    for i, seat in enumerate(upper):
        copy = net.send(sums, sums_plane.at[3 + i], seat)
        copy.wait()
        sums[...] = sums[...] + sums_plane[3 + i]
    def slab(zz):
        return sums.at[:, pl.ds(pl.multiple_of(zz * part, part), part)]

    small_z = [
        net.send(slab(zz), sums_z.at[i], seat)
        for i, (zz, seat) in enumerate(((z1, "z1"), (z2, "z2"), (z3, "z3")))
    ]
    d[2] = add_z1(2, c[2])
    f[1] = add_z2(1, d[1])

    ring = []

    def emit(value, targets):
        k = len(ring)
        if k >= 2:
            for copy in ring[k - 2]:
                copy.wait()
        room = stage.at[k % 2]
        room[: value.shape[0], : value.shape[1]] = value
        ring.append([net.move(room.at[r, cc], target) for (r, cc), target in targets])

    def emit_gu(k, got):
        got.wait_recv()
        for q in range(4):
            at = q * hq + k * chunk
            value = fin_gu[k, q // 2, q % 2].astype(full).reshape(part, pair)
            emit(
                value,
                [
                    ((pl.ds(0, part), lo), ggu_out.at[:, pl.ds(at, chunk)]),
                    ((pl.ds(0, part), hi), ggu_out.at[:, pl.ds(hidden + at, chunk)]),
                ],
            )

    def emit_c(i, got):
        got.wait_recv()
        value = fin_c[i].astype(full).reshape(part, width)
        target = gout_out if i == 0 else gin_out.at[:, cols_of(i)]
        emit(value, [((pl.ds(0, part), pl.ds(0, width)), target)])

    emit_gu(0, gu_c[0])
    emit_gu(1, gu_c[1])
    d[3] = add_z1(3, c[3])
    f[2] = add_z2(2, d[2])
    g = {0: onward_c(0, f[0])}

    @pl.when(level)
    def _():
        dny.wait_recv()
        dnc.start()

    gu_c.append(across_gu(2, gu_d[2]))
    g[1] = onward_c(1, f[1])
    f[3] = add_z2(3, d[3])
    h = {0: across_c(0, g[0])}
    g[2] = onward_c(2, f[2])
    h[1] = across_c(1, g[1])

    @pl.when(~level)
    def _():
        dnc.wait_recv()

    block = chunk // 2
    for k in range(6):
        target = gdn_out.at[pl.ds(k * block, block)]
        emit(fin_dn[k // 2, k % 2].astype(full), [((pl.ds(0, block), pl.ds(0, width)), target)])
    emit_gu(2, gu_c[2])
    g[3] = onward_c(3, f[3])
    h[2] = across_c(2, g[2])
    h[3] = across_c(3, g[3])
    for copy in small_z:
        copy.wait()
    small_out[...] = slab(z)[...] + sums_z[0] + sums_z[1] + sums_z[2]
    keep_small = net.move(small_out, gsmall_out)
    for i in range(4):
        emit_c(i, h[i])

    @pl.when(~same0)
    def _():
        dn1.wait_send()

    @pl.when(same0 & ~same1)
    def _():
        dn2.wait_send()

    @pl.when(holder)
    def _():
        dnx.wait_send()

    @pl.when(level)
    def _():
        dny.wait_send()
        dnc.wait_send()

    flat = [g1a, g1b, g2s, back]
    for group in (gu_b, gu_d):
        for pair_of in group:
            flat += list(pair_of)
    flat += gu_c + sc
    for group in (a, b, d, g, h):
        flat += list(group.values())
    for group in (c, f):
        for pair_of in group.values():
            flat += list(pair_of)
    for copy in flat:
        copy.wait_send()
    for k in range(max(0, len(ring) - 2), len(ring)):
        for copy in ring[k]:
            copy.wait()
    keep_grad.wait()
    keep_small.wait()


def finish(seq, starts, small_all, x, e, first, dh2, proj, zed, gext, wc, gu0, gu1, gu2, dn):
    rows, width = first.shape
    part = width // 4
    half, pair = gu0.shape
    chunk = pair // 2
    hq = 3 * chunk
    extra = seq.bit_length() - 4
    room = max(extra, 1)
    shape = jax.ShapeDtypeStruct
    anyspace = pl.BlockSpec(memory_space=pl.ANY)
    vmem = pl.BlockSpec(memory_space=pltpu.VMEM)
    outs = [
        shape((rows, width), low),
        shape((part, 3 * width), full),
        shape((part, width), full),
        shape((part, 8 * hq), full),
        shape((hq, width), full),
        shape((8, part), full),
    ]
    v = pltpu.VMEM
    eighth = part // 8
    outs += [
        shape((4, room, eighth, width), low),
        shape((3, room, half, pair), low),
        shape((room, 3, chunk // 2, width), low),
    ]
    scratch = [
        v((4, 4, 2, eighth, 4 * width), low),
        v((rows, width), full),
        v((rows, width), full),
        v((rows, width), low),
        v((rows, width), low),
        v((rows, 3 * width), full),
        v((rows, width), low),
        v((width, rows), low),
        v((rows + 16, width), full),
        v((rows, width), full),
        v((rows, 3 * width), low),
        v((rows + 8, 128), full),
        v((rows + 8, 128), full),
        v((4, 2, 2, 2, eighth, 4 * width), low),
        v((8, width), full),
        v((8, width), full),
        v((8, width), full),
        v((8, width), full),
        v((3 + room, 8, width), full),
        v((3, 8, part), full),
        v((8, part), full),
        v((4, 4, 2, 2, eighth, width), low),
        v((4, 4, 2, eighth, width), low),
        v((4, 4, eighth, width), low),
        v((4, 2, eighth, width), low),
        v((4, eighth, width), low),
        v((4, 2, 2, 2, eighth, width), low),
        v((3, 2, 2, 2, half, pair), low),
        v((3, 2, chunk // 2, width), low),
        v((4, half, pair), low),
        v((2, half, pair), low),
        v((half, pair), low),
        v((3, chunk // 2, width), low),
        v((3, chunk // 2, width), low),
        v((3, chunk // 2, width), low),
        v((2, part, width), full),
        pltpu.SemaphoreType.DMA((80 + 12 * extra,)),
        pltpu.SemaphoreType.DMA((80 + 12 * extra,)),
        pltpu.SemaphoreType.DMA((60 + 12 * extra,)),
    ]
    return pl.pallas_call(
        functools.partial(finish_kernel, seq),
        out_shape=outs,
        in_specs=[vmem, vmem] + [anyspace] * 12,
        out_specs=[anyspace] * len(outs),
        scratch_shapes=scratch,
        compiler_params=pltpu.CompilerParams(
            collective_id=2, has_side_effects=True, vmem_limit_bytes=63 * MIB
        ),
        name="finish",
    )(starts, small_all, x, e, first, dh2, proj, zed, gext, wc, gu0, gu1, gu2, dn)


def build(seq):
    def local(
        tokens,
        doc_start,
        norm1_gain,
        in_weight,
        conv_weight,
        out_weight,
        norm2_gain,
        gate_up_weight,
        down_weight,
        out_grad,
    ):
        x, cot = tokens[0], out_grad[0]
        starts = doc_start.T
        hq = down_weight.shape[0]
        small = jnp.concatenate(
            [norm1_gain[None], norm2_gain[None], conv_weight.T], 0
        ).astype(low)
        small = jnp.pad(small, ((0, 16 - small.shape[0]), (0, 0)))
        w_c, w_gu, w_down, cot_all, second_all, proj, first, zed, gext, small_all = gather(
            seq, x, cot, starts, small, in_weight, out_weight, gate_up_weight, down_weight
        )
        result, dh2, gu0, gu1, gu2, dn, _ = feed(
            seq, second_all, cot_all, w_gu, w_down.reshape(hq, x.shape[1]), first
        )
        grad_x, grad_in, grad_out, grad_gu, grad_down, grad_small, *_ = finish(
            seq, starts, small_all, x, cot, first, dh2, proj, zed, gext, w_c, gu0, gu1, gu2, dn
        )
        return (
            result[None],
            grad_x[None],
            grad_small[0],
            grad_in,
            grad_small[2:5].T,
            grad_out,
            grad_small[1],
            grad_gu,
            grad_down,
        )

    return local


def solution(mesh):
    in_specs = (
        P("wsh", "seq", None),
        P("wsh", "seq"),
        P("wsh"),
        P("wsh", None),
        P("wsh", None),
        P("wsh", None),
        P("wsh"),
        P("wsh", None),
        P("wsh", None),
        P("wsh", "seq", None),
    )
    out_specs = (
        P("wsh", "seq", None),
        P("wsh", "seq", None),
        P("wsh"),
        P("wsh", None),
        P("wsh", None),
        P("wsh", None),
        P("wsh"),
        P("wsh", None),
        P("wsh", None),
    )
    local = build(mesh.shape["seq"])
    return jax.shard_map(local, mesh=mesh, in_specs=in_specs, out_specs=out_specs, check_vma=False)
```

time: 541 us -> 378 us (0.70); the launches traced: 532 us -> 376 us
  Pallas kernels: 120 us -> 354 us
  waiting for transfers between devices: 196 us -> 0 us
  matrix products: 95.3 us -> 0 us
  starting transfers between devices: 44.9 us -> 0 us
  other arithmetic: 40.7 us -> 2.66 us
  local copies, waits for them, and re-layouts: 32.8 us -> 19.3 us
    pallas_call x0 -> x2, Pallas kernels: none -> 234 us  [the longest x1 121 us: finish(): pl.pallas_call(functools.partial(finish_kernel, seq), out_shape=outs, in_...]
    ppermute x36 -> x0, waiting for transfers between devices: 196 us -> none  [the longest x24 153 us: flip(): return lax.ppermute(value, 'seq', [(i, i ^ 1 << bit) for i in range(seq)])]
    dot_general x12 -> x0, matrix products: 95.3 us -> none  [the longest x5 41.6 us: outer(): lax.dot_general(left, right, (((1,), (1,)), ((), ())), preferred_element_...]
    ppermute x36 -> x0, starting transfers between devices: 44.9 us -> none  [the longest x24 22.1 us: flip(): return lax.ppermute(value, 'seq', [(i, i ^ 1 << bit) for i in range(seq)])]
    convert_element_type x21 -> x0, other arithmetic: 23.6 us -> none  [the longest x14 12.1 us: plus(): return (a.astype(full) + b.astype(full)).astype(low)]
    add x4 -> x0, other arithmetic: 8.63 us -> none  [the longest x2 5.96 us: scatter_group(): mine = mine + flip(theirs.astype(low), 0).astype(full)]
    dynamic_slice x43 -> x0, local copies, waits for them, and re-layouts: 8.5 us -> none  [the longest x23 4.63 us: by_z(): lax.dynamic_slice_in_dim(value, (z ^ j) * part, part, 1)]
    unnamed x85 -> x14, local copies, waits for them, and re-layouts: 13.2 us -> 15 us
  transfers between devices with their start and end apart: 36 -> 0, of which waited for: 15 -> 0; matrix products, arithmetic and copies ran while one was open for 18% -> 0% of each run, Pallas kernels for 0% -> 0%
where the time goes in v3:
time: 378 us; the launch traced here: 376 us
  Pallas kernels  354 us (94%)
  local copies, waits for them, and re-layouts  19.3 us (5%)
    pallas_call x1, Pallas kernels, finish(): pl.pallas_call(functools.partial(finish_kernel, seq), out_shape=outs, in_...  121 us
    pallas_call x1, Pallas kernels, gather(): pl.pallas_call(functools.partial(gather_kernel, seq), out_shape=outs, in_...  120 us
    pallas_call x1, Pallas kernels, feed(): pl.pallas_call(functools.partial(feed_kernel, seq), out_shape=outs, in_sp...  112 us
    unnamed x14, local copies, waits for them, and re-layouts  15 us

profile of v3, /device:TPU:1, one launch (start us, length us, event | category | flops | bytes accessed | tf_op | source)
XLA Modules:
  0.0 376.5 jit_solution(3266973018875868886)
XLA Ops:
  0.6 0.7 convert.12
  1.3 0.7 convert.13
  2.0 0.7 convert_bitcast_fusion
  2.7 0.6 fusion.4.small_ref
  3.3 1.5 copy.19.starts_ref
  4.9 120.0 %gather.1 = (bf16[4,4,2,32,4096]{4,3,2,1,0:T(8,128)(2,1)}, bf16[4,256,2304]{2,1,0:T(8,128)(2,1)}, bf16[2,576,1024]{2,1,0:T(8,128)(2,1)}, bf16[4,512,1024]{2,1,0:...) custom-call(bf16[512,1024]{1,0:T(8,128)(2,1)} %bitcast.14, ...), custom_call_target="tpu_custom_call" | custom-call | tf_op jit(solution)/shard_map/gather/pallas_call | solution.py:396
  124.9 112.4 %feed.1 = (bf16[512,1024]{1,0:T(8,128)(2,1)}, f32[512,1024]{1,0:T(8,128)}, bf16[128,768]{1,0:T(8,128)(2,1)}, bf16[128,768]{1,0:T(8,128)(2,1)}, bf16[4,128,768]{2...) custom-call(bf16[4,512,1024]{2,1,0:T(8,128)(2,1)} %get-tuple-element.31.h2_hbm, ...), custom_call_target="tpu_custom_call" | custom-call | tf_op jit(solution)/shard_map/feed/pallas_call | solution.py:728
  237.3 121.5 %finish.1 = (bf16[512,1024]{1,0:T(8,128)(2,1)}, f32[256,3072]{1,0:T(8,128)}, f32[256,1024]{1,0:T(8,128)}, f32[256,9216]{1,0:T(8,128)}, f32[1152,1024]{1,0:T(8,12...) custom-call(s32[512,1]{1,0:T(8,128)} %copy.19.starts_ref, ...), custom_call_target="tpu_custom_call" | custom-call | tf_op jit(solution)/shard_map/finish/pallas_call | solution.py:1345
  358.7 0.0 copy-start.1
  358.7 1.4 fusion.5
  360.2 1.3 slice_bitcast_fusion
  361.5 2.3 copy.27
  363.7 0.0 copy-start
  363.7 2.4 copy.28
  366.1 0.0 copy-done.1
  366.2 1.7 copy.29
  367.8 0.0 slice-start
  367.8 2.7 copy.30
  370.6 0.0 copy-done
  370.6 0.0 slice-start.1
  370.6 3.7 copy.31
  374.3 0.0 slice-done
  374.3 0.0 slice-done.1
  374.3 2.2 copy.32
  (3 shorter events, 0.0 us)
Async XLA Ops:
  358.7 7.4 %copy-start.1 = (f32[256,3072]{1,0:T(8,128)S(1)}, f32[256,3072]{1,0:T(8,128)}, u32[]{:S(2)}) copy-start(f32[256,3072]{1,0:T(8,128)} %get-tuple-element.67) | copy-start | bytes 9437188
  363.7 6.8 %copy-start = (f32[256,9216]{1,0:T(8,128)S(1)}, f32[256,9216]{1,0:T(8,128)}, u32[]{:S(2)}) copy-start(f32[256,9216]{1,0:T(8,128)} %get-tuple-element.71) | copy-start | bytes 28311556
  367.8 6.5 %slice-start = ((s8[4718592]{0:T(1024)(128)(4,1)}), s8[4194304]{0:T(1024)(128)(4,1)S(1)}, s32[]{:S(2)}) async-start(s8[4718592]{0:T(1024)(128)(4,1)} %bitcast.12), calls=%async_computation | async-start | bytes 8388608
  370.6 3.7 slice-start.1

commit v4 on v3

v4 whole, which is shorter than its diff:
```python
import functools
import jax
import jax.numpy as jnp
from jax import lax
from jax.experimental import pallas as pl
from jax.experimental.pallas import tpu as pltpu
from jax.sharding import PartitionSpec as P

low = jnp.bfloat16
full = jnp.float32
MESH = pl.DeviceIdType.MESH
epsilon = 1e-06
MIB = 1 << 20


def mirrored(index, weight):
    return index + weight - 2 * weight * ((index // weight) % 2)


class Net:
    def __init__(self, me, z, send_sems, recv_sems, local_sems):
        self.me, self.z = me, z
        self.send_sems, self.recv_sems, self.local_sems = send_sems, recv_sems, local_sems
        self.count = self.local_count = 0

    def seat(self, name):
        me, z = self.me, self.z
        return {
            "core": {"seq": mirrored(me, 1), "wsh": z},
            "x": {"seq": mirrored(me, 2), "wsh": z},
            "y": {"seq": mirrored(me, 4), "wsh": z},
            "z1": {"seq": me, "wsh": mirrored(z, 1)},
            "z2": {"seq": me, "wsh": mirrored(z, 2)},
            "z3": {"seq": me, "wsh": 3 - z},
        }[name]

    def make(self, src, dst, seat, k=None):
        if k is None:
            k = self.count
            self.count += 1
        return pltpu.make_async_remote_copy(
            src_ref=src,
            dst_ref=dst,
            send_sem=self.send_sems.at[k],
            recv_sem=self.recv_sems.at[k],
            device_id=self.seat(seat) if isinstance(seat, str) else seat,
            device_id_type=MESH,
        )

    def send(self, src, dst, seat):
        copy = self.make(src, dst, seat)
        copy.start()
        return copy

    def move(self, src, dst):
        k = self.local_count
        self.local_count += 1
        copy = pltpu.make_async_copy(src, dst, self.local_sems.at[k])
        copy.start()
        return copy


def greet(seats):
    barrier = pltpu.get_barrier_semaphore()
    for seat in seats:
        pl.semaphore_signal(barrier, inc=1, device_id=seat, device_id_type=MESH)
    pl.semaphore_wait(barrier, len(seats))


def inner(left, right):
    return lax.dot_general(left, right, (((0,), (0,)), ((), ())), preferred_element_type=full)


def outer(left, right):
    return lax.dot_general(left, right, (((1,), (1,)), ((), ())), preferred_element_type=full)


def chunk_sizes(hq):
    chunk = hq // 3
    return chunk, 2 * chunk


def gather_kernel(
    seq,
    x_hbm, e_hbm, starts_ref, norm_one_ref, norm_two_ref, taps_ref, win_hbm, wout_hbm, wgu_hbm, wdn_hbm,
    wc_out, wgu_out, wdn_out, e_out, h2_out, proj_out, first_out, zed_out, gext_out, small_out,
    wc, ownf, winf, woutf, wguf, wdnf, wgu_own, wdn_own, x_ref, h_ref, proj, gext, zed, first, h2, small_all, small_own,
    send_sems, recv_sems, local_sems,
):
    me, z = lax.axis_index("seq"), lax.axis_index("wsh")
    net = Net(me, z, send_sems, recv_sems, local_sems)
    core, xbit, ybit = me % 2, (me // 2) % 2, (me // 4) % 2
    quarter = me % 4
    rows, width = x_hbm.shape
    part = width // 4
    hq = 6 * wdn_hbm.shape[2]
    hidden = 4 * hq
    half = part // 2
    z1, z2, z3 = mirrored(z, 1), mirrored(z, 2), 3 - z
    after = {"seq": lax.rem(me + 1, seq), "wsh": z}
    before = {"seq": lax.rem(me + seq - 1, seq), "wsh": z}

    piece = part // 8
    turn = (ybit * 2 + xbit) * 2 + core
    mine = pl.ds(pl.multiple_of(turn * piece, piece), piece)
    load_own = [
        net.move(win_hbm.at[mine], ownf.at[:, pl.ds(0, 3 * width)]),
        net.move(wout_hbm.at[mine], ownf.at[:, pl.ds(3 * width, width)]),
    ]
    load_x = net.move(x_hbm, x_ref.at[pl.ds(16, rows)])
    chunk, pair = chunk_sizes(hq)
    load_gu = []
    for k in range(3):
        for base, shift in ((quarter * hq, 0), (hidden + quarter * hq, chunk)):
            cut = pl.ds(pl.multiple_of(base + k * chunk, 128), chunk)
            load_gu.append(
                net.move(wgu_hbm.at[:, cut], wguf.at[:, pl.ds(k * pair + shift, chunk)])
            )
    load_win = net.move(win_hbm, winf)
    load_wout = net.move(wout_hbm, woutf)
    load_dn = net.move(wdn_hbm, wdnf)
    keep_e = net.move(e_hbm, e_out.at[0])
    small_own[...] = jnp.zeros_like(small_own)
    small_own[0:1] = norm_one_ref[...].astype(low).astype(full)
    small_own[1:2] = norm_two_ref[...].astype(low).astype(full)
    small_own[2:5] = taps_ref[...].astype(low).astype(full)
    small_all[z] = small_own[...].astype(low)
    for copy in load_own:
        copy.wait()
    spot = ybit * 2 + xbit
    spot_x = ybit * 2 + 1 - xbit
    spot_y = (1 - ybit) * 2 + xbit
    wc[z, spot, core] = ownf[...].astype(low)

    greet([net.seat(n) for n in ("core", "x", "y", "z1", "z2", "z3")] + [before])

    cols = [pl.ds(0, 2 * width), pl.ds(2 * width, 2 * width)]

    def own(zz):
        return wc.at[zz, spot, core]

    a1 = net.send(own(z), own(z), "z1")
    a2 = net.send(own(z), own(z), "z2")
    smalls = [net.send(small_all.at[z], small_all.at[z], n) for n in ("z1", "z2", "z3")]
    halo = net.send(x_hbm.at[pl.ds(rows - 16, 16)], x_ref.at[pl.ds(0, 16)], after)

    for copy in load_gu:
        copy.wait()
    wgu_own[...] = wguf[...].astype(low)
    keep_gu = net.move(wgu_own, wgu_out.at[z])
    load_win.wait()
    load_wout.wait()

    def cast_block(i, carry):
        @pl.when(i != turn)
        def _():
            at = pl.ds(pl.multiple_of(i * piece, piece), piece)
            wc[z, i // 2, i % 2, :, : 3 * width] = winf[at].astype(low)
            wc[z, i // 2, i % 2, :, 3 * width :] = woutf[at].astype(low)

        return carry

    lax.fori_loop(0, 8, cast_block, 0)
    load_dn.wait()

    def cast_dn(i, carry):
        wdn_own[i // 2, i % 2] = wdnf[i // 2, i % 2].astype(low)
        return carry

    lax.fori_loop(0, 6, cast_dn, 0)

    def spread(zz):
        return net.send(own(zz), own(zz), "x"), net.send(own(zz), own(zz), "y")

    def onward(zz, b):
        b[0].wait_recv()
        place = wc.at[zz, spot_x, core, :, cols[0]]
        d0 = net.send(place, place, "y")
        b[1].wait_recv()
        place = wc.at[zz, spot_y, core, :, cols[1]]
        return d0, net.send(place, place, "x")

    def across(zz, b, d):
        d[0].wait_recv()
        d[1].wait_recv()
        return net.send(wc.at[zz, :, core], wc.at[zz, :, core], "core")

    a1.wait_recv()
    b1 = spread(z1)
    a2.wait_recv()
    a3 = net.send(own(z2), own(z2), "z1")
    b2 = spread(z2)

    def gu(zz, yy, k):
        at = pl.ds(pl.multiple_of(yy * half, half), half)
        return wgu_out.at[zz, at, pl.ds(k * pair, pair)]

    f1, f2, f3, g1, g2, g3 = [], [], [], [], [], []
    for k in range(3):
        source = wgu_own.at[
            pl.ds(pl.multiple_of(ybit * half, half), half), pl.ds(k * pair, pair)
        ]
        f1.append(net.send(source, gu(z, ybit, k), "z1"))
        f2.append(net.send(source, gu(z, ybit, k), "z2"))

    def pass_gu(k):
        f1[k].wait_recv()
        g1.append(net.send(gu(z1, ybit, k), gu(z1, ybit, k), "y"))
        f2[k].wait_recv()
        f3.append(net.send(gu(z2, ybit, k), gu(z2, ybit, k), "z1"))
        g2.append(net.send(gu(z2, ybit, k), gu(z2, ybit, k), "y"))

    def pass_far(k):
        f3[k].wait_recv()
        g3.append(net.send(gu(z3, ybit, k), gu(z3, ybit, k), "y"))

    for copy in smalls:
        copy.wait_recv()
    load_x.wait()
    halo.wait_recv()

    def row_of(k):
        return jnp.concatenate([small_all[i, k : k + 1, :] for i in range(4)], 1).astype(full)

    gain_one, gain_two = row_of(0), row_of(1)

    def norm_one(i, carry):
        at = pl.ds(pl.multiple_of(i * 176, 16), 176)
        xf = x_ref[at].astype(full)
        rate = lax.rsqrt(jnp.mean(xf * xf, axis=-1, keepdims=True) + epsilon)
        h_ref[at] = (xf * rate * gain_one).astype(low)
        return carry

    lax.fori_loop(0, (rows + 16) // 176, norm_one, 0)
    d1 = onward(z1, b1)
    d2 = onward(z2, b2)
    a3.wait_recv()
    b3 = spread(z3)

    same0 = (z % 2) == (quarter % 2)
    same1 = (z // 2) == (quarter // 2)
    holder = same0 & same1
    dn2, dn1a, dn1b, dny = [], [], [], []
    for k in range(3):
        source = wdn_own.at[k, ybit]
        target = wdn_out.at[k, ybit]
        dn2.append(net.make(source, target, "z2"))
        dn1a.append(net.make(source, target, "z1"))
        dn1b.append(net.make(target, target, "z1", net.count - 1))
        dny.append(net.make(target, target, "y"))
    keep_dn = pltpu.make_async_copy(wdn_own, wdn_out, local_sems.at[24])

    def pass_dn(k):
        @pl.when(same0 & ~same1)
        def _():
            dn2[k].wait_recv()
            dn1b[k].start()
            dny[k].start()

        @pl.when(~same0)
        def _():
            dn1a[k].wait_recv()
            dny[k].start()

    c1 = across(z1, b1, d1)
    c2 = across(z2, b2, d2)
    d3 = onward(z3, b3)
    pass_gu(0)
    c3 = across(z3, b3, d3)

    @pl.when(holder)
    def _():
        for k in range(3):
            dn2[k].start()
            dn1a[k].start()
        keep_dn.start()

    for c in (c1, c2, c3):
        c.wait_recv()
    ex = net.send(e_hbm, e_out.at[1], "x")
    ec = net.send(e_hbm, e_out.at[2], "core")
    pass_gu(1)

    def project(i, carry):
        at = pl.ds(pl.multiple_of(i * 512, 512), 512)
        proj[:, at] = jnp.dot(
            h_ref[...], wc[:, :, :, :, at].reshape(width, 512), preferred_element_type=full
        )
        return carry

    lax.fori_loop(0, 6, project, 0)
    keep_wc = net.move(wc, wc_out)
    keep_proj = net.move(proj.at[pl.ds(16, rows)], proj_out)

    pass_gu(2)
    place = me * rows + lax.broadcasted_iota(jnp.int32, (rows, 1), 0)
    starts = jnp.broadcast_to(starts_ref[...], (8, rows)).T[:, 0:1]
    keep_one = (place - 1 >= starts).astype(full)
    keep_two = (place - 2 >= starts).astype(full)
    cw = 128
    def mix(i, carry):
        at = pl.ds(pl.multiple_of(i * cw, cw), cw)
        xat = pl.ds(pl.multiple_of(2 * width + i * cw, cw), cw)
        cat = pl.ds(pl.multiple_of(width + i * cw, cw), cw)
        gext[:, at] = (proj[:, at] * proj[:, xat]).astype(low).astype(full)
        zi = i // (part // cw)
        inside = pl.ds(pl.multiple_of((i % (part // cw)) * cw, cw), cw)
        taps = small_all[zi, :, inside].astype(full)
        mixed = (
            taps[2:3] * gext[16:, at]
            + keep_one * taps[3:4] * gext[15 : rows + 15, at]
            + keep_two * taps[4:5] * gext[14 : rows + 14, at]
        )
        zed[:, at] = (proj[16:, cat] * mixed).astype(low)
        return carry

    lax.fori_loop(0, width // cw, mix, 0)
    keep_zed = net.move(zed, zed_out)
    keep_gext = net.move(gext, gext_out)

    pass_far(0)
    pass_dn(0)

    def project_out(i, carry):
        at = pl.ds(pl.multiple_of(i * 512, 512), 512)
        wat = pl.ds(pl.multiple_of(3 * width + i * 512, 512), 512)
        first[:, at] = x_ref[16:, at].astype(full) + jnp.dot(
            zed[...], wc[:, :, :, :, wat].reshape(width, 512), preferred_element_type=full
        )
        return carry

    lax.fori_loop(0, 2, project_out, 0)
    keep_first = net.move(first, first_out)
    pass_far(1)

    def norm_two(i, carry):
        at = pl.ds(pl.multiple_of(i * 128, 128), 128)
        xf = first[at]
        rate = lax.rsqrt(jnp.mean(xf * xf, axis=-1, keepdims=True) + epsilon)
        h2[at] = (xf * rate * gain_two).astype(low)
        return carry

    lax.fori_loop(0, rows // 128, norm_two, 0)
    keep_h2 = net.move(h2, h2_out.at[0])
    hx = net.send(h2, h2_out.at[1], "x")
    hc = net.send(h2, h2_out.at[2], "core")
    keep_small = net.move(small_all, small_out)

    pass_far(2)
    ex.wait_recv()
    exc = net.send(e_out.at[1], e_out.at[3], "core")
    pass_dn(1)
    pass_dn(2)
    hx.wait_recv()
    hxc = net.send(h2_out.at[1], h2_out.at[3], "core")
    for c in (*g1, *g2, *g3, ec, exc, hc, hxc):
        c.wait_recv()

    @pl.when(~holder)
    def _():
        for copy in dny:
            copy.wait()

    @pl.when(holder)
    def _():
        for copy in dn2 + dn1a:
            copy.wait_send()
        keep_dn.wait()

    @pl.when(same0 & ~same1)
    def _():
        for copy in dn1b:
            copy.wait_send()

    for c in (
        *smalls, halo, a1, a2, a3, *b1, *b2, *b3, *d1, *d2, *d3, c1, c2, c3,
        *f1, *f2, *f3, *g1, *g2, *g3, ex, ec, exc, hx, hc, hxc,
    ):
        c.wait_send()
    for c in (keep_e, keep_gu, keep_wc, keep_proj, keep_zed, keep_gext, keep_first, keep_h2, keep_small):
        c.wait()


def gather(seq, x, e, starts, norm_one, norm_two, taps, win, wout, wgu, wdn):
    rows, width = x.shape
    part = width // 4
    hq = wdn.shape[0]
    thirds = (3, 2, hq // 6, width)
    wdn = wdn.reshape(thirds)
    shape = jax.ShapeDtypeStruct
    anyspace = pl.BlockSpec(memory_space=pl.ANY)
    vmem = pl.BlockSpec(memory_space=pltpu.VMEM)
    conv = (4, 4, 2, part // 8, 4 * width)
    outs = [
        shape(conv, low),
        shape((4, part, 2 * hq), low),
        shape(thirds, low),
        shape((4, rows, width), low),
        shape((4, rows, width), low),
        shape((rows, 3 * width), full),
        shape((rows, width), full),
        shape((rows, width), low),
        shape((rows + 16, width), full),
        shape((4, 16, part), low),
    ]
    scratch = [
        pltpu.VMEM(conv, low),
        pltpu.VMEM((part // 8, 4 * width), full),
        pltpu.VMEM((part, 3 * width), full),
        pltpu.VMEM((part, width), full),
        pltpu.VMEM((part, 2 * hq), full),
        pltpu.VMEM(thirds, full),
        pltpu.VMEM((part, 2 * hq), low),
        pltpu.VMEM(thirds, low),
        pltpu.VMEM((rows + 16, width), low),
        pltpu.VMEM((rows + 16, width), low),
        pltpu.VMEM((rows + 16, 3 * width), full),
        pltpu.VMEM((rows + 16, width), full),
        pltpu.VMEM((rows, width), low),
        pltpu.VMEM((rows, width), full),
        pltpu.VMEM((rows, width), low),
        pltpu.VMEM((4, 16, part), low),
        pltpu.VMEM((16, part), full),
        pltpu.SemaphoreType.DMA((64,)),
        pltpu.SemaphoreType.DMA((64,)),
        pltpu.SemaphoreType.DMA((26,)),
    ]
    return pl.pallas_call(
        functools.partial(gather_kernel, seq),
        out_shape=outs,
        in_specs=[anyspace, anyspace] + [vmem] * 4 + [anyspace] * 4,
        out_specs=[anyspace] * len(outs),
        scratch_shapes=scratch,
        compiler_params=pltpu.CompilerParams(
            collective_id=0, has_side_effects=True, vmem_limit_bytes=56 * MIB
        ),
        name="gather",
    )(x, e, starts, norm_one, norm_two, taps, win, wout, wgu, wdn)


def feed_kernel(
    seq,
    h2_hbm, e_hbm, wgu_hbm, wdn_hbm, first_hbm,
    result_out, dh2_out, gu0_out, gu1_out, gu2_out, dn_out, dn2_out, land_out,
    h2, h2t, e, wgu, wdn, a, at_ref, du, u, da, dgu, ddn, send_a, send_b, send_x, send_o, temp, acc, acc_out,
    gu0_y, gu2_y, dn_y, gu0_z1, gu0_z2, gu1_z1, gu1_z2, gu1_y, gu0_s, gu1_s, gu1_t, gu0_f, gu1_f,
    send_sems, recv_sems, local_sems,
):
    me, z = lax.axis_index("seq"), lax.axis_index("wsh")
    net = Net(me, z, send_sems, recv_sems, local_sems)
    ybit = (me // 4) % 2
    rows, width = first_hbm.shape
    hq = wdn.shape[0]
    chunk, pair = chunk_sizes(hq)
    part = width // 4
    half = part // 2
    z1, z2, z3 = mirrored(z, 1), mirrored(z, 2), 3 - z
    block = 4 * rows

    load_h2, load_e, load_gu, load_dn = [], [], [], []

    def load_block(j):
        load_h2.append(net.move(h2_hbm.at[j], h2.at[pl.ds(j * rows, rows)]))
        load_e.append(net.move(e_hbm.at[j], e.at[pl.ds(j * rows, rows)]))

    def load_chunk(k):
        pcols, ccols = pl.ds(k * pair, pair), pl.ds(k * chunk, chunk)
        for i in range(4):
            load_gu.append(net.move(wgu_hbm.at[i, :, pcols], wgu.at[pl.ds(i * part, part), pcols]))
        load_dn.append(net.move(wdn_hbm.at[ccols], wdn.at[ccols]))

    load_chunk(0)
    for j in range(4):
        load_block(j)
    load_chunk(1)
    load_chunk(2)
    load_first = net.move(first_hbm, acc_out)
    greet([net.seat(n) for n in ("core", "x", "y", "z1", "z2")])

    def turn(j, carry):
        at = pl.ds(pl.multiple_of(j * 256, 256), 256)
        h2t[:, at] = h2[at].T
        return carry

    def forward(k, slots, step):
        pcols, ccols = pl.ds(k * pair, pair), pl.ds(k * chunk, chunk)

        def one(i, carry):
            j = slots + i * step
            at = pl.ds(pl.multiple_of(j * rows, rows), rows)
            u[...] = jnp.dot(h2[at], wgu[:, pcols], preferred_element_type=full)
            da[...] = outer(e[at], wdn[ccols])

            def piece(r, carry):
                rr = pl.ds(pl.multiple_of(r * 64, 64), 64)
                tt = pl.ds(pl.multiple_of(j * rows + r * 64, 64), 64)
                gate, upper, back = u[rr, :chunk], u[rr, chunk:], da[rr]
                sigma = jax.nn.sigmoid(gate)
                swish = gate * sigma
                a[tt, ccols] = (swish * upper).astype(low)
                du[tt, pl.ds(k * pair, chunk)] = (
                    back * upper * (sigma * (1.0 + gate * (1.0 - sigma)))
                ).astype(low)
                du[tt, pl.ds(k * pair + chunk, chunk)] = (back * swish).astype(low)
                return carry

            lax.fori_loop(0, rows // 64, piece, 0)
            return carry

        lax.fori_loop(0, 4 // step, one, 0)

    def weights(k):
        def turn_a(j, carry):
            at = pl.ds(pl.multiple_of(j * rows, rows), rows)
            at_ref[:, at] = a[at, pl.ds(k * chunk, chunk)].T
            return carry

        lax.fori_loop(0, 4, turn_a, 0)

        def gate_up(n, carry):
            cols = pl.ds(pl.multiple_of(k * pair + n * 256, 256), 256)
            got = jnp.dot(h2t[...], du[:, cols], preferred_element_type=full).astype(low)
            dgu[:, :, :, cols] = got.reshape(4, 2, half, 256)
            return carry

        lax.fori_loop(0, pair // 256, gate_up, 0)

        def down(n, carry):
            cols = pl.ds(pl.multiple_of(n * 512, 512), 512)
            got = jnp.dot(at_ref[...], e[:, cols], preferred_element_type=full).astype(low)
            ddn[k, :, :, cols] = got.reshape(2, chunk // 2, 512)
            return carry

        lax.fori_loop(0, width // 512, down, 0)

    def cols_of(k):
        return pl.ds(k * pair, pair)

    for copy in load_gu[:4] + load_dn[:1]:
        copy.wait()
    for j in range(4):
        load_h2[j].wait()
        load_e[j].wait()
        forward(0, j, 4)
    lax.fori_loop(0, block // 256, turn, 0)
    weights(0)
    for copy in load_gu[4:] + load_dn[1:]:
        copy.wait()
    y0 = net.send(dgu.at[:, 1 - ybit, :, cols_of(0)], gu0_y, "y")
    yd0 = net.send(ddn.at[0, 1 - ybit], dn_y.at[0], "y")
    forward(1, 1, 2)
    forward(2, 1, 2)

    def sum_rows(put, count, step):
        def one(i, carry):
            put(pl.ds(pl.multiple_of(i * step, step), step))
            return carry

        lax.fori_loop(0, count // step, one, 0)

    def accumulate(target):
        def go(at):
            target[at] = target[at] + temp[at].astype(full)

        return go

    def keep(cols, value):
        acc[:, cols] = value

    def more(cols, value):
        acc_out[:, cols] = acc_out[:, cols] + value

    def gu0_sum(i, carry):
        gu0_s[i] = (dgu[i, ybit, :, cols_of(0)].astype(full) + gu0_y[i].astype(full)).astype(low)
        return carry

    def gu1_sum(i, carry):
        gu1_t[i] = (dgu[z2, i, :, cols_of(1)].astype(full) + gu1_z1[1, i].astype(full)).astype(low)
        gu1_s[i] = (dgu[z, i, :, cols_of(1)].astype(full) + gu1_z1[0, i].astype(full)).astype(low)
        return carry

    def gu1_more(i, carry):
        gu1_s[i] = (gu1_s[i].astype(full) + gu1_z2[i].astype(full)).astype(low)
        return carry

    def finish(at):
        send_a[at] = (acc_out[at] + temp[at].astype(full)).astype(low)

    def grad_rows(j, put):
        at = pl.ds(j * rows, rows)

        def one(n, carry):
            cols = pl.ds(pl.multiple_of(n * 256, 256), 256)
            put(cols, outer(du[at], wgu[cols]))
            return carry

        lax.fori_loop(0, width // 256, one, 0)

    def out_rows(j, put):
        at = pl.ds(j * rows, rows)

        def one(n, carry):
            cols = pl.ds(pl.multiple_of(n * 256, 256), 256)
            put(cols, jnp.dot(a[at], wdn[:, cols], preferred_element_type=full))
            return carry

        lax.fori_loop(0, width // 256, one, 0)

    def store(ref):
        def put(cols, value):
            ref[:, cols] = value.astype(low)

        return put

    def add(target, other):
        def put(cols, value):
            target[:, cols] = (value + other[:, cols].astype(full)).astype(target.dtype)

        return put

    def fetch(j):
        copy = net.move(land_out.at[j], temp)
        copy.wait()

    grad_rows(3, store(send_a))
    ga = net.send(send_a, land_out.at[0], "core")
    out_rows(3, store(send_b))
    oa = net.send(send_b, land_out.at[3], "core")
    ga.wait_recv()
    fetch(0)
    grad_rows(1, add(send_x, temp))
    gx = net.send(send_x, land_out.at[1], "x")
    oa.wait_recv()
    fetch(3)
    out_rows(1, add(send_o, temp))
    ox = net.send(send_o, land_out.at[4], "x")
    forward(1, 0, 2)
    weights(1)
    m1 = net.send(dgu.at[z1, :, :, cols_of(1)], gu1_z1.at[0], "z1")
    m2 = net.send(dgu.at[z3, :, :, cols_of(1)], gu1_z1.at[1], "z1")
    yd1 = net.send(ddn.at[1, 1 - ybit], dn_y.at[1], "y")
    forward(2, 0, 2)
    weights(2)
    y2 = net.send(dgu.at[:, 1 - ybit, :, cols_of(2)], gu2_y, "y")
    keep_dn2 = net.move(ddn.at[2], dn2_out)
    y0.wait_recv()
    lax.fori_loop(0, 4, gu0_sum, 0)
    n1 = net.send(gu0_s.at[z1], gu0_z1.at[0], "z1")
    n2 = net.send(gu0_s.at[z3], gu0_z1.at[1], "z1")
    m1.wait_recv()
    m2.wait_recv()
    lax.fori_loop(0, 2, gu1_sum, 0)
    m3 = net.send(gu1_t, gu1_z2, "z2")
    ga.wait_send()
    grad_rows(2, store(send_a))
    gb = net.send(send_a, land_out.at[2], "core")
    oa.wait_send()
    out_rows(2, store(send_b))
    ob = net.send(send_b, land_out.at[5], "core")
    grad_rows(0, keep)
    gb.wait_recv()
    fetch(2)
    sum_rows(accumulate(acc), rows, 64)
    load_first.wait()
    out_rows(0, more)
    ob.wait_recv()
    fetch(5)
    sum_rows(accumulate(acc_out), rows, 64)
    n1.wait_recv()
    n2.wait_recv()
    gu0_f[1] = (gu0_s[z2].astype(full) + gu0_z1[1].astype(full)).astype(low)
    n3 = net.send(gu0_f.at[1], gu0_z2, "z2")
    m3.wait_recv()
    lax.fori_loop(0, 2, gu1_more, 0)
    m4 = net.send(gu1_s.at[1 - ybit], gu1_y, "y")
    gx.wait_recv()
    fetch(1)
    sum_rows(accumulate(acc), rows, 64)
    keep_dh2 = net.move(acc, dh2_out)
    n3.wait_recv()
    gu0_f[0] = (
        gu0_s[z].astype(full) + gu0_z1[0].astype(full) + gu0_z2[...].astype(full)
    ).astype(low)
    keep_gu0 = net.move(gu0_f.at[0], gu0_out)
    ox.wait_recv()
    fetch(4)
    gb.wait_send()
    sum_rows(finish, rows, 64)
    keep_result = net.move(send_a, result_out)

    yd0.wait_recv()
    yd1.wait_recv()
    y2.wait_recv()

    def gu2_sum(i, carry):
        dgu[i, ybit, :, cols_of(2)] = (
            dgu[i, ybit, :, cols_of(2)].astype(full) + gu2_y[i].astype(full)
        ).astype(low)
        return carry

    lax.fori_loop(0, 4, gu2_sum, 0)
    keep_gu2 = net.move(dgu.at[:, ybit, :, cols_of(2)], gu2_out)

    def dn_sum(i, carry):
        ddn[i, ybit] = (ddn[i, ybit].astype(full) + dn_y[i].astype(full)).astype(low)
        return carry

    lax.fori_loop(0, 2, dn_sum, 0)
    keep_dn = net.move(ddn.at[pl.ds(0, 2), ybit], dn_out)
    m4.wait_recv()
    gu1_f[...] = (gu1_s[ybit].astype(full) + gu1_y[...].astype(full)).astype(low)
    keep_gu1 = net.move(gu1_f, gu1_out)
    for c in (y0, yd0, m1, m2, yd1, y2, n1, n2, m3, n3, ox, ob, m4, gx):
        c.wait_send()
    for c in (keep_dh2, keep_gu0, keep_result, keep_gu2, keep_dn, keep_dn2, keep_gu1):
        c.wait()


def feed(seq, h2_all, e_all, wgu, wdn, first):
    rows, width = first.shape
    part = width // 4
    half = part // 2
    hq = wdn.shape[0]
    chunk, pair = chunk_sizes(hq)
    shape = jax.ShapeDtypeStruct
    anyspace = pl.BlockSpec(memory_space=pl.ANY)
    outs = [
        shape((rows, width), low),
        shape((rows, width), full),
        shape((half, pair), low),
        shape((half, pair), low),
        shape((4, half, pair), low),
        shape((2, chunk // 2, width), low),
        shape((2, chunk // 2, width), low),
        shape((6, rows, width), low),
    ]
    v = pltpu.VMEM
    scratch = [
        v((4 * rows, width), low),
        v((width, 4 * rows), low),
        v((4 * rows, width), low),
        v((width, 2 * hq), low),
        v((hq, width), low),
        v((4 * rows, hq), low),
        v((chunk, 4 * rows), low),
        v((4 * rows, 2 * hq), low),
        v((rows, pair), full),
        v((rows, chunk), full),
        v((4, 2, half, 2 * hq), low),
        v((3, 2, chunk // 2, width), low),
        v((rows, width), low),
        v((rows, width), low),
        v((rows, width), low),
        v((rows, width), low),
        v((rows, width), low),
        v((rows, width), full),
        v((rows, width), full),
        v((4, half, pair), low),
        v((4, half, pair), low),
        v((2, chunk // 2, width), low),
        v((2, half, pair), low),
        v((half, pair), low),
        v((2, 2, half, pair), low),
        v((2, half, pair), low),
        v((half, pair), low),
        v((4, half, pair), low),
        v((2, half, pair), low),
        v((2, half, pair), low),
        v((2, half, pair), low),
        v((half, pair), low),
        pltpu.SemaphoreType.DMA((24,)),
        pltpu.SemaphoreType.DMA((24,)),
        pltpu.SemaphoreType.DMA((44,)),
    ]
    return pl.pallas_call(
        functools.partial(feed_kernel, seq),
        out_shape=outs,
        in_specs=[anyspace] * 5,
        out_specs=[anyspace] * len(outs),
        scratch_shapes=scratch,
        compiler_params=pltpu.CompilerParams(
            collective_id=1, has_side_effects=True, vmem_limit_bytes=63 * MIB
        ),
        name="feed",
    )(h2_all, e_all, wgu, wdn, first)


def finish_kernel(
    seq,
    starts_ref, small_all, x_hbm, e_hbm, first_hbm, dh2_hbm, proj_hbm, zed_hbm, gext_hbm, wc_hbm,
    gu0_hbm, gu1_hbm, gu2_hbm, dn_hbm, dn2_hbm,
    grad_out, gin_out, gout_out, ggu_out, gdn_out, gsmall_out, up_c, up_gu, up_dn,
    wc, first, dh2, x_ref, e_ref, proj, zed, ht, gext, dx1, dp, s1, s2, dwc,
    ret_send, ret_land, sums, sums_core, sums_plane, sums_z, small_out,
    cr, r1, r2, rz, fin_c, fin_gu, fin_dn, g2, g2_z1, g2_z2, dnv, dn_z1, dn_z2, dn_o, dn_y,
    send_sems, recv_sems, local_sems,
):
    me, z = lax.axis_index("seq"), lax.axis_index("wsh")
    net = Net(me, z, send_sems, recv_sems, local_sems)
    core, xbit, ybit = me % 2, (me // 2) % 2, (me // 4) % 2
    quarter = me % 4
    rows, width = first.shape
    part = width // 4
    half = part // 2
    chunk = dnv.shape[1] * 2
    pair = 2 * chunk
    hq = 3 * chunk
    hidden = 4 * hq
    z1, z2, z3 = mirrored(z, 1), mirrored(z, 2), 3 - z
    after = {"seq": lax.rem(me + 1, seq), "wsh": z}
    before = {"seq": lax.rem(me + seq - 1, seq), "wsh": z}
    cross = {"seq": mirrored(mirrored(me, 2), 4), "wsh": z}
    upper = [
        {"seq": mirrored(me, 1 << bit), "wsh": z} for bit in range(3, seq.bit_length() - 1)
    ]
    same0 = (z % 2) == (quarter % 2)
    same1 = (z // 2) == (quarter // 2)
    holder = same0 & same1
    level = core == z % 2

    load_gu2 = net.move(gu2_hbm, g2)
    load_dn = [
        net.move(dn2_hbm.at[ybit], dnv.at[2]),
        net.move(dn2_hbm.at[1 - ybit], dn_o),
        net.move(dn_hbm, dnv.at[pl.ds(0, 2)]),
    ]
    load_gu = [
        net.move(gu0_hbm, fin_gu.at[0, xbit, core, ybit]),
        net.move(gu1_hbm, fin_gu.at[1, xbit, core, ybit]),
    ]
    load_first = net.move(first_hbm, first)
    load_dh2 = net.move(dh2_hbm, dh2)
    load_e = net.move(e_hbm, e_ref)
    outer_cols = pl.ds(3 * width, width)
    inner_cols = pl.ds(0, 3 * width)
    load_wc = net.move(
        wc_hbm.at[:, :, :, :, outer_cols], wc.at[:, :, :, :, outer_cols]
    )
    load_zed = net.move(zed_hbm, zed)
    zedt, do_ref, out_ref = ht, e_ref, zed
    load_x = net.move(x_hbm, x_ref)
    load_gext = net.move(gext_hbm, gext)
    load_proj = net.move(proj_hbm, proj)
    load_win = net.move(
        wc_hbm.at[:, :, :, :, inner_cols], wc.at[:, :, :, :, inner_cols]
    )
    greet(
        [net.seat(n) for n in ("core", "x", "y", "z1", "z2", "z3")] + [after, cross] + upper
    )

    def plus_upper(ref, land, temp):
        for i, seat in enumerate(upper):
            copy = net.send(ref, land.at[i], seat)
            copy.wait()
            net.move(land.at[i], temp).wait()
            ref[...] = (ref[...].astype(full) + temp[...].astype(full)).astype(ref.dtype)

    load_gu2.wait()
    g1a = net.send(g2.at[z1], g2_z1.at[0], "z1")
    g1b = net.send(g2.at[z3], g2_z1.at[1], "z1")
    for copy in load_dn:
        copy.wait()
    dn0 = net.send(dn_o, dn_y, "y")
    dn1 = [net.make(dnv.at[k], dn_z1.at[k], "z1") for k in range(3)]
    dn2 = [net.make(dnv.at[k], dn_z2.at[k], "z2") for k in range(3)]
    dnx, dny, dnc = [], [], []
    for k in range(3):
        spot = fin_dn.at[k, ybit]
        dnx.append(net.make(spot, spot, "x"))
        dny.append(net.make(spot, spot, "y"))
        dnc.append(net.make(fin_dn.at[k], fin_dn.at[k], "core"))

    @pl.when(~same0)
    def _():
        for k in range(2):
            dn1[k].start()

    def dn_first():
        dn0.wait_recv()
        dnv[2] = (dnv[2].astype(full) + dn_y[...].astype(full)).astype(low)

        @pl.when(~same0)
        def _():
            dn1[2].start()

    def dn_second(k):
        @pl.when(same0)
        def _():
            dn1[k].wait_recv()
            dnv[k] = (dnv[k].astype(full) + dn_z1[k].astype(full)).astype(low)

        @pl.when(same0 & ~same1)
        def _():
            dn2[k].start()

    def dn_third(k):
        @pl.when(holder)
        def _():
            dn2[k].wait_recv()
            dnv[k] = (dnv[k].astype(full) + dn_z2[k].astype(full)).astype(low)
            plus_upper(dnv.at[k], up_dn.at[k], dn_z1.at[k])
            fin_dn[k, ybit] = dnv[k]
            dnx[k].start()
            dny[k].start()

    def dn_fourth(k):
        @pl.when(level & ~holder)
        def _():
            dnx[k].wait_recv()
            dny[k].start()

    def dn_fifth(k):
        @pl.when(level)
        def _():
            dny[k].wait_recv()
            dnc[k].start()

    def dn_last(k):
        @pl.when(~level)
        def _():
            dnc[k].wait_recv()

        for y in range(2):
            at = (2 * k + y) * (chunk // 2)
            results.append(net.move(fin_dn.at[k, y], gdn_out.at[pl.ds(at, chunk // 2)]))

    results = []

    def spread_gu(k):
        own = fin_gu.at[k, xbit, core, ybit]
        return net.send(own, own, "x"), net.send(own, own, "y")

    lo, hi = pl.ds(0, chunk), pl.ds(chunk, chunk)

    def onward_gu(k, b):
        b[0].wait_recv()
        spot = fin_gu.at[k, 1 - xbit, core, ybit, :, lo]
        first_half = net.send(spot, spot, "y")
        b[1].wait_recv()
        spot = fin_gu.at[k, xbit, core, 1 - ybit, :, hi]
        return first_half, net.send(spot, spot, "x")

    def across_gu(k, d):
        d[0].wait_recv()
        d[1].wait_recv()
        return net.send(fin_gu.at[k, :, core], fin_gu.at[k, :, core], "core")

    if not upper:
        for c in load_gu:
            c.wait()
        gu_b = [spread_gu(0), spread_gu(1)]
    else:
        gu_b = []
        for k in range(2):
            load_gu[k].wait()
            up_gu_own = fin_gu.at[k, xbit, core, ybit]
            plus_upper(up_gu_own, up_gu.at[k], dp.at[pl.ds(0, half), pl.ds(0, pair)])
            gu_b.append(spread_gu(k))

    def row_of(k):
        return jnp.concatenate([small_all[i, k : k + 1, :] for i in range(4)], 1).astype(full)

    gain_one, gain_two = row_of(0), row_of(1)
    sums[...] = jnp.zeros_like(sums)
    load_first.wait()
    load_dh2.wait()
    load_e.wait()
    tile = 32

    def folded(value):
        return jnp.sum(value.reshape(value.shape[0] // 8, 8, value.shape[1]), axis=0)

    def norm_two(i, total):
        at = pl.ds(pl.multiple_of(i * tile, tile), tile)
        xf, dh = first[at], dh2[at]
        rate = lax.rsqrt(jnp.mean(xf * xf, axis=-1, keepdims=True) + epsilon)
        normed = xf * rate
        scaled = dh * gain_two
        mean = jnp.mean(scaled * normed, axis=-1, keepdims=True)
        got = e_ref[at].astype(full) + rate * (scaled - normed * mean)
        dx1[at] = got
        do_ref[at] = got.astype(low)
        return total + folded(dh * normed)

    total = lax.fori_loop(0, rows // tile, norm_two, jnp.zeros((8, width), full))
    sums[1:2, :] = jnp.sum(total, axis=0, keepdims=True)

    load_wc.wait()
    dz = first

    def back_out(i, carry):
        cols = pl.ds(pl.multiple_of(i * part, part), part)
        dz[:, cols] = outer(do_ref[...], wc[i, :, :, :, 3 * width :].reshape(part, width))
        return carry

    lax.fori_loop(0, 4, back_out, 0)
    load_zed.wait()
    load_x.wait()

    def turn_zed(i, carry):
        cols = pl.ds(pl.multiple_of(i * 256, 256), 256)
        zedt[:, cols] = zed[cols].T
        return carry

    lax.fori_loop(0, rows // 256, turn_zed, 0)

    def weight_chunk(left, right, at):
        def one(n, carry):
            cols = pl.ds(pl.multiple_of(n * 256, 256), 256)
            into = pl.ds(pl.multiple_of(at + n * 256, 256), 256)
            got = jnp.dot(left[...], right(cols), preferred_element_type=full).astype(low)
            dwc[:, :, :, :, :, into] = got.reshape(4, 2, 2, 2, part // 8, 256)
            return carry

        lax.fori_loop(0, width // 256, one, 0)

    starts_at = [3 * width, width, 0, 2 * width]

    def cols_of(i):
        return pl.ds(starts_at[i], width)

    def to_core(i):
        return net.send(dwc.at[:, :, :, 1 - core, :, cols_of(i)], cr.at[i], "core")

    weight_chunk(zedt, lambda cols: do_ref[:, cols], 3 * width)
    sc = [to_core(0)]

    g1a.wait_recv()
    g1b.wait_recv()
    g2[z2] = (g2[z2].astype(full) + g2_z1[1].astype(full)).astype(low)
    g2s = net.send(g2.at[z2], g2_z2, "z2")

    dn_first()
    dn_second(0)
    dn_second(1)

    place = me * rows + lax.broadcasted_iota(jnp.int32, (rows, 1), 0)
    starts = jnp.broadcast_to(starts_ref[...], (8, rows)).T[:, 0:1]
    keep_one = (place - 1 >= starts).astype(full)
    keep_two = (place - 2 >= starts).astype(full)
    load_gext.wait()
    load_proj.wait()
    s1[rows:] = jnp.zeros((s1.shape[0] - rows, 128), full)
    s2[rows:] = jnp.zeros((s2.shape[0] - rows, 128), full)
    dg = dh2
    row8 = lax.broadcasted_iota(jnp.int32, (8, 128), 0)

    def unmix(i, carry):
        at = pl.ds(pl.multiple_of(i * 128, 128), 128)
        cat = pl.ds(pl.multiple_of(width + i * 128, 128), 128)
        zi = i // (part // 128)
        inside = pl.ds(pl.multiple_of((i % (part // 128)) * 128, 128), 128)
        taps = small_all[zi, :, inside].astype(full)
        tap0, tap1, tap2 = taps[2:3], taps[3:4], taps[4:5]
        current, lag_one, lag_two = gext[16:, at], gext[15 : rows + 15, at], gext[14 : rows + 14, at]
        mixed = tap0 * current + keep_one * tap1 * lag_one + keep_two * tap2 * lag_two
        back = dz[:, at]
        dp[:, cat] = (back * mixed).astype(low)
        dm = back * proj[:, cat]
        t1, t2 = keep_one * dm, keep_two * dm
        for k, value in ((2, dm * current), (3, t1 * lag_one), (4, t2 * lag_two)):
            sums[k : k + 1, at] = jnp.sum(folded(value), axis=0, keepdims=True)
        s1[:rows] = tap1 * t1
        s2[:rows] = tap2 * t2
        dg[:, at] = tap0 * dm + s1[1 : rows + 1] + s2[2 : rows + 2]
        ret_send[:, at] = jnp.where(
            row8 == 6, s2[0:1], jnp.where(row8 == 7, s1[0:1] + s2[1:2], 0.0)
        )
        return carry

    lax.fori_loop(0, width // 128, unmix, 0)
    back = net.send(ret_send, ret_land, before)

    def norm_one(i, carry):
        at = pl.ds(pl.multiple_of(i * 128, 128), 128)
        xf = x_ref[at].astype(full)
        rate = lax.rsqrt(jnp.mean(xf * xf, axis=-1, keepdims=True) + epsilon)
        ht[:, at] = (xf * rate * gain_one).astype(low).T
        return carry

    lax.fori_loop(0, rows // 128, norm_one, 0)
    weight_chunk(ht, lambda cols: dp[:, pl.ds(pl.multiple_of(width + cols.start, 256), 256)], width)
    sc.append(to_core(1))

    orders = ["xy", "yx", "xy", "all"]
    def spot_of(i, zi, yi, xi):
        return (zi, yi, xi, core, slice(None), cols_of(i))

    def add_core(i):
        sc[i].wait_recv()

        def one(j, carry):
            zi, yi, xi = j // 4, (j // 2) % 2, j % 2
            spot = spot_of(i, zi, yi, xi)
            dwc[spot] = (dwc[spot].astype(full) + cr[i, zi, yi, xi].astype(full)).astype(low)
            return carry

        lax.fori_loop(0, 16, one, 0)
        cols = cols_of(i)
        if orders[i] == "xy":
            return net.send(dwc.at[:, :, 1 - xbit, core, :, cols], r1.at[i], "x")
        if orders[i] == "yx":
            return net.send(dwc.at[:, 1 - ybit, :, core, :, cols], r1.at[i], "y")
        return [
            net.send(dwc.at[:, yi, xi, core, :, cols], land, seat)
            for yi, xi, land, seat in (
                (ybit, 1 - xbit, r1.at[i, :, 0], "x"),
                (1 - ybit, xbit, r1.at[i, :, 1], "y"),
                (1 - ybit, 1 - xbit, r2.at[i], cross),
            )
        ]

    def add_first(i, copy):
        copy.wait_recv()

        def one(j, carry):
            zi, oi = j // 2, j % 2
            yi, xi = (oi, xbit) if orders[i] == "xy" else (ybit, oi)
            spot = spot_of(i, zi, yi, xi)
            dwc[spot] = (dwc[spot].astype(full) + r1[i, zi, oi].astype(full)).astype(low)
            return carry

        lax.fori_loop(0, 8, one, 0)
        cols = cols_of(i)
        if orders[i] == "xy":
            return net.send(dwc.at[:, 1 - ybit, xbit, core, :, cols], r2.at[i], "y")
        return net.send(dwc.at[:, ybit, 1 - xbit, core, :, cols], r2.at[i], "x")

    def add_second(i, copy):
        if orders[i] == "all":
            for c in copy:
                c.wait_recv()
        else:
            copy.wait_recv()

        def one(zi, carry):
            spot = spot_of(i, zi, ybit, xbit)
            got = dwc[spot].astype(full) + r2[i, zi].astype(full)
            if orders[i] == "all":
                got = got + r1[i, zi, 0].astype(full) + r1[i, zi, 1].astype(full)
            dwc[spot] = got.astype(low)
            return carry

        lax.fori_loop(0, 4, one, 0)
        return [
            net.send(dwc.at[spot_of(i, zz, ybit, xbit)], rz.at[i, k], seat)
            for k, (zz, seat) in enumerate(((z1, "z1"), (z2, "z2"), (z3, "z3")))
        ]

    def add_z(i, copies):
        for c in copies:
            c.wait_recv()
        own = fin_c.at[i, ybit, xbit, core]
        own[...] = (
            dwc[spot_of(i, z, ybit, xbit)].astype(full)
            + rz[i, 0].astype(full)
            + rz[i, 1].astype(full)
            + rz[i, 2].astype(full)
        ).astype(low)
        plus_upper(own, up_c.at[i], e_ref.at[pl.ds(0, part // 8)])
        return [net.send(own, own, seat) for seat in ("x", "y", cross)]

    def across_c(i, copies):
        for c in copies:
            c.wait_recv()
        return net.send(fin_c.at[i, :, :, core], fin_c.at[i, :, :, core], "core")

    def last_c(i, copy):
        copy.wait_recv()
        target = gout_out if i == 0 else gin_out.at[:, :, :, :, cols_of(i)]
        results.append(net.move(fin_c.at[i], target))

    def last_gu(k, copy):
        copy.wait_recv()
        for q in range(4):
            at = q * hq + k * chunk
            spot = fin_gu.at[k, q // 2, q % 2]
            results.append(net.move(spot.at[:, :, lo], ggu_out.at[:, :, pl.ds(at, chunk)]))
            results.append(
                net.move(spot.at[:, :, hi], ggu_out.at[:, :, pl.ds(hidden + at, chunk)])
            )

    a = {}
    b = {}
    a[0] = add_core(0)
    gu_d = [onward_gu(k, gu_b[k]) for k in range(2)]
    back.wait_recv()
    follows = (me < seq - 1).astype(full)
    dg[rows - 8 :] = dg[rows - 8 :] + ret_land[...] * follows

    def unproject(i, carry):
        at = pl.ds(pl.multiple_of(i * 128, 128), 128)
        xat = pl.ds(pl.multiple_of(2 * width + i * 128, 128), 128)
        dp[:, at] = (dg[:, at] * proj[:, xat]).astype(low)
        dp[:, xat] = (dg[:, at] * proj[:, at]).astype(low)
        return carry

    lax.fori_loop(0, width // 128, unproject, 0)
    weight_chunk(ht, lambda cols: dp[:, cols], 0)
    sc.append(to_core(2))
    a[1] = add_core(1)
    weight_chunk(ht, lambda cols: dp[:, pl.ds(pl.multiple_of(2 * width + cols.start, 256), 256)], 2 * width)
    sc.append(to_core(3))
    a[2] = add_core(2)
    b[0] = add_first(0, a[0])
    a[3] = add_core(3)

    g2s.wait_recv()
    own = fin_gu.at[2, xbit, core, ybit]
    own[...] = (
        g2[z].astype(full) + g2_z1[0].astype(full) + g2_z2[...].astype(full)
    ).astype(low)
    plus_upper(own, up_gu.at[2], e_ref.at[pl.ds(0, half), pl.ds(0, pair)])
    gu_b.append(spread_gu(2))
    dn_second(2)
    dn_third(0)

    load_win.wait()
    dh = dg

    def back_in(i, carry):
        cols = pl.ds(pl.multiple_of(i * part, part), part)
        dh[:, cols] = outer(dp[...], wc[i, :, :, :, : 3 * width].reshape(part, 3 * width))
        return carry

    lax.fori_loop(0, 4, back_in, 0)
    b[1] = add_first(1, a[1])
    c = {0: add_second(0, b[0])}

    def norm_back(i, total):
        at = pl.ds(pl.multiple_of(i * tile, tile), tile)
        xf = x_ref[at].astype(full)
        rate = lax.rsqrt(jnp.mean(xf * xf, axis=-1, keepdims=True) + epsilon)
        normed = xf * rate
        got = dh[at]
        scaled = got * gain_one
        mean = jnp.mean(scaled * normed, axis=-1, keepdims=True)
        out_ref[at] = (dx1[at] + rate * (scaled - normed * mean)).astype(low)
        return total + folded(got * normed)

    total = lax.fori_loop(0, rows // tile, norm_back, jnp.zeros((8, width), full))
    keep_grad = net.move(out_ref, grad_out)
    sums[0:1, :] = jnp.sum(total, axis=0, keepdims=True)
    small_core = net.send(sums, sums_core, "core")
    dn_third(1)
    b[2] = add_first(2, a[2])
    small_core.wait()
    sums[...] = sums[...] + sums_core[...]
    small_plane = [
        net.send(sums, sums_plane.at[i], seat) for i, seat in enumerate(("x", "y", cross))
    ]
    gu_c = [across_gu(k, gu_d[k]) for k in range(2)]
    dn_third(2)
    dn_fourth(0)
    c[1] = add_second(1, b[1])
    c[3] = add_second(3, a[3])
    c[2] = add_second(2, b[2])
    dn_fourth(1)
    d = {0: add_z(0, c[0])}
    gu_d.append(onward_gu(2, gu_b[2]))
    dn_fourth(2)
    dn_fifth(0)
    for copy in small_plane:
        copy.wait()
    sums[...] = sums[...] + sums_plane[0] + sums_plane[1] + sums_plane[2]
    for i, seat in enumerate(upper):
        copy = net.send(sums, sums_plane.at[3 + i], seat)
        copy.wait()
        sums[...] = sums[...] + sums_plane[3 + i]

    def slab(zz):
        return sums.at[:, pl.ds(pl.multiple_of(zz * part, part), part)]

    small_z = [
        net.send(slab(zz), sums_z.at[i], seat)
        for i, (zz, seat) in enumerate(((z1, "z1"), (z2, "z2"), (z3, "z3")))
    ]
    d[1] = add_z(1, c[1])
    d[3] = add_z(3, c[3])
    d[2] = add_z(2, c[2])
    f = {0: across_c(0, d[0])}
    last_gu(0, gu_c[0])
    last_gu(1, gu_c[1])
    dn_fifth(1)
    dn_fifth(2)
    gu_c.append(across_gu(2, gu_d[2]))
    for i in (1, 3, 2):
        f[i] = across_c(i, d[i])
    for copy in small_z:
        copy.wait()
    small_out[...] = slab(z)[...] + sums_z[0] + sums_z[1] + sums_z[2]
    keep_small = net.move(small_out, gsmall_out)
    for k in range(3):
        dn_last(k)
    for i in (0, 1, 3, 2):
        last_c(i, f[i])
    last_gu(2, gu_c[2])

    @pl.when(~same0)
    def _():
        for copy in dn1:
            copy.wait_send()

    @pl.when(same0 & ~same1)
    def _():
        for copy in dn2:
            copy.wait_send()

    @pl.when(holder)
    def _():
        for copy in dnx:
            copy.wait_send()

    @pl.when(level)
    def _():
        for copy in dny + dnc:
            copy.wait_send()

    flat = [g1a, g1b, g2s, back, dn0] + gu_c + sc
    for group in gu_b + gu_d:
        flat += list(group)
    for group in (a, b, c, d, f):
        for copies in group.values():
            flat += copies if isinstance(copies, list) else [copies]
    for copy in flat:
        copy.wait_send()
    for copy in results:
        copy.wait()
    keep_grad.wait()
    keep_small.wait()


def finish(seq, starts, small_all, x, e, first, dh2, proj, zed, gext, wc, gu0, gu1, gu2, dn, dn2):
    rows, width = first.shape
    part = width // 4
    half, pair = gu0.shape
    chunk = pair // 2
    hq = 3 * chunk
    extra = seq.bit_length() - 4
    room = max(extra, 1)
    eighth = part // 8
    shape = jax.ShapeDtypeStruct
    anyspace = pl.BlockSpec(memory_space=pl.ANY)
    vmem = pl.BlockSpec(memory_space=pltpu.VMEM)
    outs = [
        shape((rows, width), low),
        shape((2, 2, 2, eighth, 3 * width), low),
        shape((2, 2, 2, eighth, width), low),
        shape((2, half, 8 * hq), low),
        shape((hq, width), low),
        shape((8, part), full),
    ]
    v = pltpu.VMEM
    outs += [
        shape((4, room, eighth, width), low),
        shape((3, room, half, pair), low),
        shape((3, room, chunk // 2, width), low),
    ]
    scratch = [
        v((4, 4, 2, eighth, 4 * width), low),
        v((rows, width), full),
        v((rows, width), full),
        v((rows, width), low),
        v((rows, width), low),
        v((rows, 3 * width), full),
        v((rows, width), low),
        v((width, rows), low),
        v((rows + 16, width), full),
        v((rows, width), full),
        v((rows, 3 * width), low),
        v((rows + 8, 128), full),
        v((rows + 8, 128), full),
        v((4, 2, 2, 2, eighth, 4 * width), low),
        v((8, width), full),
        v((8, width), full),
        v((8, width), full),
        v((8, width), full),
        v((3 + room, 8, width), full),
        v((3, 8, part), full),
        v((8, part), full),
        v((4, 4, 2, 2, eighth, width), low),
        v((4, 4, 2, eighth, width), low),
        v((4, 4, eighth, width), low),
        v((4, 3, eighth, width), low),
        v((4, 2, 2, 2, eighth, width), low),
        v((3, 2, 2, 2, half, pair), low),
        v((3, 2, chunk // 2, width), low),
        v((4, half, pair), low),
        v((2, half, pair), low),
        v((half, pair), low),
        v((3, chunk // 2, width), low),
        v((3, chunk // 2, width), low),
        v((3, chunk // 2, width), low),
        v((chunk // 2, width), low),
        v((chunk // 2, width), low),
        pltpu.SemaphoreType.DMA((100 + 12 * extra,)),
        pltpu.SemaphoreType.DMA((100 + 12 * extra,)),
        pltpu.SemaphoreType.DMA((60 + 12 * extra,)),
    ]
    return pl.pallas_call(
        functools.partial(finish_kernel, seq),
        out_shape=outs,
        in_specs=[vmem, vmem] + [anyspace] * 13,
        out_specs=[anyspace] * len(outs),
        scratch_shapes=scratch,
        compiler_params=pltpu.CompilerParams(
            collective_id=2, has_side_effects=True, vmem_limit_bytes=63 * MIB
        ),
        name="finish",
    )(starts, small_all, x, e, first, dh2, proj, zed, gext, wc, gu0, gu1, gu2, dn, dn2)


def cast_kernel(gu_ref, dn_ref, win_ref, wout_ref, res_ref, gx_ref, small_ref, *outs):
    ggu, gdn, gin, gout, res, gx, norm_one, norm_two, taps = outs
    ggu[...] = gu_ref[...].astype(full)
    gdn[...] = dn_ref[...].astype(full)
    gin[...] = win_ref[...].astype(full)
    gout[...] = wout_ref[...].astype(full)
    res[0] = res_ref[...]
    gx[0] = gx_ref[...]
    norm_one[...] = small_ref[0:1]
    norm_two[...] = small_ref[1:2]
    taps[...] = small_ref[2:5]


def cast(gu, dn, win, wout, result, grad_x, small):
    steps = 8
    arrays = (gu, dn, win, wout, result, grad_x)

    def cut(v, lead=False):
        rows, cols = v.shape
        if lead:
            return pl.BlockSpec((1, rows // steps, cols), lambda i: (0, i, 0))
        return pl.BlockSpec((rows // steps, cols), lambda i: (i, 0))

    def whole(shape):
        return pl.BlockSpec(shape, lambda i: (0, 0))

    part = small.shape[1]
    rows = ((1, part), (1, part), (3, part))
    moved = sum(v.size for v in arrays)
    return pl.pallas_call(
        cast_kernel,
        grid=(steps,),
        out_shape=[jax.ShapeDtypeStruct(v.shape, full) for v in arrays[:4]]
        + [jax.ShapeDtypeStruct((1, *v.shape), low) for v in arrays[4:]]
        + [jax.ShapeDtypeStruct(r, full) for r in rows],
        in_specs=[cut(v) for v in arrays] + [whole(small.shape)],
        out_specs=[cut(v) for v in arrays[:4]]
        + [cut(v, True) for v in arrays[4:]]
        + [whole(r) for r in rows],
        cost_estimate=pl.CostEstimate(flops=0, bytes_accessed=6 * moved, transcendentals=0),
        compiler_params=pltpu.CompilerParams(vmem_limit_bytes=63 * MIB),
        name="cast",
    )(*arrays, small)


def build(seq):
    def local(
        tokens,
        doc_start,
        norm1_gain,
        in_weight,
        conv_weight,
        out_weight,
        norm2_gain,
        gate_up_weight,
        down_weight,
        out_grad,
    ):
        x, cot = tokens[0], out_grad[0]
        starts = doc_start
        hq = down_weight.shape[0]
        small = (norm1_gain[None], norm2_gain[None], conv_weight.T)
        w_c, w_gu, w_down, cot_all, second_all, proj, first, zed, gext, small_all = gather(
            seq, x, cot, starts, *small, in_weight, out_weight, gate_up_weight, down_weight
        )
        result, dh2, gu0, gu1, gu2, dn, dn2, _ = feed(
            seq, second_all, cot_all, w_gu, w_down.reshape(hq, x.shape[1]), first
        )
        grad_x, grad_in, grad_out, grad_gu, grad_down, grad_small, *_ = finish(
            seq, starts, small_all, x, cot, first, dh2, proj, zed, gext, w_c, gu0, gu1, gu2, dn, dn2
        )
        grad_gu, grad_down, grad_in, grad_out, result, grad_x, norm_one, norm_two, taps = cast(
            grad_gu.reshape(gate_up_weight.shape),
            grad_down,
            grad_in.reshape(in_weight.shape),
            grad_out.reshape(out_weight.shape),
            result,
            grad_x,
            grad_small,
        )
        return (
            result,
            grad_x,
            norm_one[0],
            grad_in,
            taps.T,
            grad_out,
            norm_two[0],
            grad_gu,
            grad_down,
        )

    return local


def solution(mesh):
    in_specs = (
        P("wsh", "seq", None),
        P("wsh", "seq"),
        P("wsh"),
        P("wsh", None),
        P("wsh", None),
        P("wsh", None),
        P("wsh"),
        P("wsh", None),
        P("wsh", None),
        P("wsh", "seq", None),
    )
    out_specs = (
        P("wsh", "seq", None),
        P("wsh", "seq", None),
        P("wsh"),
        P("wsh", None),
        P("wsh", None),
        P("wsh", None),
        P("wsh"),
        P("wsh", None),
        P("wsh", None),
    )
    local = build(mesh.shape["seq"])
    return jax.shard_map(local, mesh=mesh, in_specs=in_specs, out_specs=out_specs, check_vma=False)
```

time: 378 us -> 344 us (0.910)
  local copies, waits for them, and re-layouts: 19.3 us -> 0 us
  Pallas kernels: 354 us -> 339 us
    pallas_call x1, Pallas kernels: 120 us -> 104 us  [gather(): pl.pallas_call(functools.partial(gather_kernel, seq), out_shape=outs, in_...]
    unnamed x14 -> x0, local copies, waits for them, and re-layouts: 15 us -> none
    pallas_call x0 -> x1, Pallas kernels: none -> 12.5 us  [cast(): pl.pallas_call(cast_kernel, grid=(steps,), out_shape=[jax.ShapeDtypeStruc...]
    pallas_call x1, Pallas kernels: 121 us -> 109 us  [finish(): pl.pallas_call(functools.partial(finish_kernel, seq), out_shape=outs, in_...]
where the time goes in v4:
time: 344 us; the launch traced here: 340 us
  Pallas kernels  339 us (99%)
    pallas_call x1, Pallas kernels, feed(): pl.pallas_call(functools.partial(feed_kernel, seq), out_shape=outs, in_sp...  113 us
    pallas_call x1, Pallas kernels, finish(): pl.pallas_call(functools.partial(finish_kernel, seq), out_shape=outs, in_...  109 us
    pallas_call x1, Pallas kernels, gather(): pl.pallas_call(functools.partial(gather_kernel, seq), out_shape=outs, in_...  104 us
    pallas_call x1, Pallas kernels, cast(): pl.pallas_call(cast_kernel, grid=(steps,), out_shape=[jax.ShapeDtypeStruc...  12.5 us

profile of v4, /device:TPU:1, one launch (start us, length us, event | category | flops | bytes accessed | tf_op | source)
XLA Modules:
  0.0 339.6 jit_solution(15788874206137572472)
XLA Ops:
  0.6 104.1 %gather.1 = (bf16[4,4,2,32,4096]{4,3,2,1,0:T(8,128)(2,1)}, bf16[4,256,2304]{2,1,0:T(8,128)(2,1)}, bf16[3,2,192,1024]{3,2,1,0:T(8,128)(2,1)}, bf16[4,512,1024]{2,...) custom-call(bf16[512,1024]{1,0:T(8,128)(2,1)} %bitcast.15, ...), custom_call_target="tpu_custom_call" | custom-call | tf_op jit(solution)/shard_map/gather/pallas_call | solution.py:428
  104.8 113.0 %feed.1 = (bf16[512,1024]{1,0:T(8,128)(2,1)}, f32[512,1024]{1,0:T(8,128)}, bf16[128,768]{1,0:T(8,128)(2,1)}, bf16[128,768]{1,0:T(8,128)(2,1)}, bf16[4,128,768]{2...) custom-call(bf16[4,512,1024]{2,1,0:T(8,128)(2,1)} %get-tuple-element, ...), custom_call_target="tpu_custom_call" | custom-call | tf_op jit(solution)/shard_map/feed/pallas_call | solution.py:775
  217.7 109.2 %finish.1 = (bf16[512,1024]{1,0:T(8,128)(2,1)}, bf16[2,2,2,32,3072]{4,3,2,1,0:T(8,128)(2,1)}, bf16[2,2,2,32,1024]{4,3,2,1,0:T(8,128)(2,1)}, bf16[2,128,9216]{2,1...) custom-call(s32[1,512]{1,0:T(1,128)} %starts_ref.3, ...), custom_call_target="tpu_custom_call" | custom-call | tf_op jit(solution)/shard_map/finish/pallas_call | solution.py:1400
  327.0 12.5 %cast.1 = (f32[256,9216]{1,0:T(8,128)}, f32[1152,1024]{1,0:T(8,128)}, f32[256,3072]{1,0:T(8,128)}, f32[256,1024]{1,0:T(8,128)}, bf16[1,512,1024]{2,1,0:T(8,128)(...) custom-call(bf16[256,9216]{1,0:T(8,128)(2,1)} %bitcast.13, ...), custom_call_target="tpu_custom_call" | custom-call | bytes 33816576 | tf_op jit(solution)/shard_map/cast/pallas_call | solution.py:1442

commit v5 on v4

--- a/solution.py
+++ b/solution.py
@@ -203,40 +203,6 @@
         f1.append(net.send(source, gu(z, ybit, k), "z1"))
         f2.append(net.send(source, gu(z, ybit, k), "z2"))
 
-    def pass_gu(k):
-        f1[k].wait_recv()
-        g1.append(net.send(gu(z1, ybit, k), gu(z1, ybit, k), "y"))
-        f2[k].wait_recv()
-        f3.append(net.send(gu(z2, ybit, k), gu(z2, ybit, k), "z1"))
-        g2.append(net.send(gu(z2, ybit, k), gu(z2, ybit, k), "y"))
-
-    def pass_far(k):
-        f3[k].wait_recv()
-        g3.append(net.send(gu(z3, ybit, k), gu(z3, ybit, k), "y"))
-
-    for copy in smalls:
-        copy.wait_recv()
-    load_x.wait()
-    halo.wait_recv()
-
-    def row_of(k):
-        return jnp.concatenate([small_all[i, k : k + 1, :] for i in range(4)], 1).astype(full)
-
-    gain_one, gain_two = row_of(0), row_of(1)
-
-    def norm_one(i, carry):
-        at = pl.ds(pl.multiple_of(i * 176, 16), 176)
-        xf = x_ref[at].astype(full)
-        rate = lax.rsqrt(jnp.mean(xf * xf, axis=-1, keepdims=True) + epsilon)
-        h_ref[at] = (xf * rate * gain_one).astype(low)
-        return carry
-
-    lax.fori_loop(0, (rows + 16) // 176, norm_one, 0)
-    d1 = onward(z1, b1)
-    d2 = onward(z2, b2)
-    a3.wait_recv()
-    b3 = spread(z3)
-
     same0 = (z % 2) == (quarter % 2)
     same1 = (z // 2) == (quarter // 2)
     holder = same0 & same1
@@ -250,6 +216,46 @@
         dny.append(net.make(target, target, "y"))
     keep_dn = pltpu.make_async_copy(wdn_own, wdn_out, local_sems.at[24])
 
+    @pl.when(holder)
+    def _():
+        for k in range(3):
+            dn2[k].start()
+        keep_dn.start()
+
+    def pass_gu(k):
+        f1[k].wait_recv()
+        g1.append(net.send(gu(z1, ybit, k), gu(z1, ybit, k), "y"))
+        f2[k].wait_recv()
+        f3.append(net.send(gu(z2, ybit, k), gu(z2, ybit, k), "z1"))
+        g2.append(net.send(gu(z2, ybit, k), gu(z2, ybit, k), "y"))
+
+    def pass_far(k):
+        f3[k].wait_recv()
+        g3.append(net.send(gu(z3, ybit, k), gu(z3, ybit, k), "y"))
+
+    for copy in smalls:
+        copy.wait_recv()
+    load_x.wait()
+    halo.wait_recv()
+
+    def row_of(k):
+        return jnp.concatenate([small_all[i, k : k + 1, :] for i in range(4)], 1).astype(full)
+
+    gain_one, gain_two = row_of(0), row_of(1)
+
+    def norm_one(i, carry):
+        at = pl.ds(pl.multiple_of(i * 176, 16), 176)
+        xf = x_ref[at].astype(full)
+        rate = lax.rsqrt(jnp.mean(xf * xf, axis=-1, keepdims=True) + epsilon)
+        h_ref[at] = (xf * rate * gain_one).astype(low)
+        return carry
+
+    lax.fori_loop(0, (rows + 16) // 176, norm_one, 0)
+    d1 = onward(z1, b1)
+    d2 = onward(z2, b2)
+    a3.wait_recv()
+    b3 = spread(z3)
+
     def pass_dn(k):
         @pl.when(same0 & ~same1)
         def _():
@@ -271,9 +277,7 @@
     @pl.when(holder)
     def _():
         for k in range(3):
-            dn2[k].start()
             dn1a[k].start()
-        keep_dn.start()
 
     for c in (c1, c2, c3):
         c.wait_recv()
@@ -318,8 +322,9 @@
     keep_zed = net.move(zed, zed_out)
     keep_gext = net.move(gext, gext_out)
 
+    pass_dn(0)
     pass_far(0)
-    pass_dn(0)
+    pass_dn(1)
 
     def project_out(i, carry):
         at = pl.ds(pl.multiple_of(i * 512, 512), 512)
@@ -349,7 +354,6 @@
     pass_far(2)
     ex.wait_recv()
     exc = net.send(e_out.at[1], e_out.at[3], "core")
-    pass_dn(1)
     pass_dn(2)
     hx.wait_recv()
     hxc = net.send(h2_out.at[1], h2_out.at[3], "core")
@@ -443,7 +447,7 @@
     h2_hbm, e_hbm, wgu_hbm, wdn_hbm, first_hbm,
     result_out, dh2_out, gu0_out, gu1_out, gu2_out, dn_out, dn2_out, land_out,
     h2, h2t, e, wgu, wdn, a, at_ref, du, u, da, dgu, ddn, send_a, send_b, send_x, send_o, temp, acc, acc_out,
-    gu0_y, gu2_y, dn_y, gu0_z1, gu0_z2, gu1_z1, gu1_z2, gu1_y, gu0_s, gu1_s, gu1_t, gu0_f, gu1_f,
+    gu0_y, gu2_y, dn_y, gu0_z1, gu0_z2, gu1_z1, gu1_z2, gu0_s, gu1_s, gu1_t, gu0_f,
     send_sems, recv_sems, local_sems,
 ):
     me, z = lax.axis_index("seq"), lax.axis_index("wsh")
@@ -548,7 +552,7 @@
         copy.wait()
     y0 = net.send(dgu.at[:, 1 - ybit, :, cols_of(0)], gu0_y, "y")
     yd0 = net.send(ddn.at[0, 1 - ybit], dn_y.at[0], "y")
-    forward(1, 1, 2)
+    forward(1, 0, 1)
     forward(2, 1, 2)
 
     def sum_rows(put, count, step):
@@ -630,23 +634,22 @@
     fetch(0)
     grad_rows(1, add(send_x, temp))
     gx = net.send(send_x, land_out.at[1], "x")
+    weights(1)
+    m1 = net.send(dgu.at[z1, :, :, cols_of(1)], gu1_z1.at[0], "z1")
+    m2 = net.send(dgu.at[z3, :, :, cols_of(1)], gu1_z1.at[1], "z1")
+    yd1 = net.send(ddn.at[1, 1 - ybit], dn_y.at[1], "y")
     oa.wait_recv()
     fetch(3)
     out_rows(1, add(send_o, temp))
     ox = net.send(send_o, land_out.at[4], "x")
-    forward(1, 0, 2)
-    weights(1)
-    m1 = net.send(dgu.at[z1, :, :, cols_of(1)], gu1_z1.at[0], "z1")
-    m2 = net.send(dgu.at[z3, :, :, cols_of(1)], gu1_z1.at[1], "z1")
-    yd1 = net.send(ddn.at[1, 1 - ybit], dn_y.at[1], "y")
     forward(2, 0, 2)
-    weights(2)
-    y2 = net.send(dgu.at[:, 1 - ybit, :, cols_of(2)], gu2_y, "y")
-    keep_dn2 = net.move(ddn.at[2], dn2_out)
     y0.wait_recv()
     lax.fori_loop(0, 4, gu0_sum, 0)
     n1 = net.send(gu0_s.at[z1], gu0_z1.at[0], "z1")
     n2 = net.send(gu0_s.at[z3], gu0_z1.at[1], "z1")
+    weights(2)
+    y2 = net.send(dgu.at[:, 1 - ybit, :, cols_of(2)], gu2_y, "y")
+    keep_dn2 = net.move(ddn.at[2], dn2_out)
     m1.wait_recv()
     m2.wait_recv()
     lax.fori_loop(0, 2, gu1_sum, 0)
@@ -654,6 +657,10 @@
     ga.wait_send()
     grad_rows(2, store(send_a))
     gb = net.send(send_a, land_out.at[2], "core")
+    n1.wait_recv()
+    n2.wait_recv()
+    gu0_f[1] = (gu0_s[z2].astype(full) + gu0_z1[1].astype(full)).astype(low)
+    n3 = net.send(gu0_f.at[1], gu0_z2, "z2")
     oa.wait_send()
     out_rows(2, store(send_b))
     ob = net.send(send_b, land_out.at[5], "core")
@@ -666,13 +673,9 @@
     ob.wait_recv()
     fetch(5)
     sum_rows(accumulate(acc_out), rows, 64)
-    n1.wait_recv()
-    n2.wait_recv()
-    gu0_f[1] = (gu0_s[z2].astype(full) + gu0_z1[1].astype(full)).astype(low)
-    n3 = net.send(gu0_f.at[1], gu0_z2, "z2")
     m3.wait_recv()
     lax.fori_loop(0, 2, gu1_more, 0)
-    m4 = net.send(gu1_s.at[1 - ybit], gu1_y, "y")
+    keep_gu1 = net.move(gu1_s, gu1_out)
     gx.wait_recv()
     fetch(1)
     sum_rows(accumulate(acc), rows, 64)
@@ -707,10 +710,7 @@
 
     lax.fori_loop(0, 2, dn_sum, 0)
     keep_dn = net.move(ddn.at[pl.ds(0, 2), ybit], dn_out)
-    m4.wait_recv()
-    gu1_f[...] = (gu1_s[ybit].astype(full) + gu1_y[...].astype(full)).astype(low)
-    keep_gu1 = net.move(gu1_f, gu1_out)
-    for c in (y0, yd0, m1, m2, yd1, y2, n1, n2, m3, n3, ox, ob, m4, gx):
+    for c in (y0, yd0, m1, m2, yd1, y2, n1, n2, m3, n3, ox, ob, gx):
         c.wait_send()
     for c in (keep_dh2, keep_gu0, keep_result, keep_gu2, keep_dn, keep_dn2, keep_gu1):
         c.wait()
@@ -728,7 +728,7 @@
         shape((rows, width), low),
         shape((rows, width), full),
         shape((half, pair), low),
-        shape((half, pair), low),
+        shape((2, half, pair), low),
         shape((4, half, pair), low),
         shape((2, chunk // 2, width), low),
         shape((2, chunk // 2, width), low),
@@ -762,12 +762,10 @@
         v((half, pair), low),
         v((2, 2, half, pair), low),
         v((2, half, pair), low),
-        v((half, pair), low),
         v((4, half, pair), low),
         v((2, half, pair), low),
         v((2, half, pair), low),
         v((2, half, pair), low),
-        v((half, pair), low),
         pltpu.SemaphoreType.DMA((24,)),
         pltpu.SemaphoreType.DMA((24,)),
         pltpu.SemaphoreType.DMA((44,)),
@@ -792,7 +790,7 @@
     grad_out, gin_out, gout_out, ggu_out, gdn_out, gsmall_out, up_c, up_gu, up_dn,
     wc, first, dh2, x_ref, e_ref, proj, zed, ht, gext, dx1, dp, s1, s2, dwc,
     ret_send, ret_land, sums, sums_core, sums_plane, sums_z, small_out,
-    cr, r1, r2, rz, fin_c, fin_gu, fin_dn, g2, g2_z1, g2_z2, dnv, dn_z1, dn_z2, dn_o, dn_y,
+    cr, r1, r2, rz, fin_c, fin_gu, fin_dn, g2, g2_z1, g2_z2, g1_o, g1_y, dnv, dn_z1, dn_z2, dn_o, dn_y,
     send_sems, recv_sems, local_sems,
 ):
     me, z = lax.axis_index("seq"), lax.axis_index("wsh")
@@ -826,7 +824,8 @@
     ]
     load_gu = [
         net.move(gu0_hbm, fin_gu.at[0, xbit, core, ybit]),
-        net.move(gu1_hbm, fin_gu.at[1, xbit, core, ybit]),
+        net.move(gu1_hbm.at[ybit], fin_gu.at[1, xbit, core, ybit]),
+        net.move(gu1_hbm.at[1 - ybit], g1_o),
     ]
     load_first = net.move(first_hbm, first)
     load_dh2 = net.move(dh2_hbm, dh2)
@@ -945,17 +944,19 @@
         d[1].wait_recv()
         return net.send(fin_gu.at[k, :, core], fin_gu.at[k, :, core], "core")
 
-    if not upper:
-        for c in load_gu:
-            c.wait()
-        gu_b = [spread_gu(0), spread_gu(1)]
-    else:
-        gu_b = []
-        for k in range(2):
-            load_gu[k].wait()
-            up_gu_own = fin_gu.at[k, xbit, core, ybit]
-            plus_upper(up_gu_own, up_gu.at[k], dp.at[pl.ds(0, half), pl.ds(0, pair)])
-            gu_b.append(spread_gu(k))
+    for copy in load_gu:
+        copy.wait()
+    g1y = net.send(g1_o, g1_y, "y")
+    room_gu = pl.ds(0, half), pl.ds(0, pair)
+    plus_upper(fin_gu.at[0, xbit, core, ybit], up_gu.at[0], dp.at[room_gu])
+    gu_b = [spread_gu(0)]
+
+    def gu_first():
+        g1y.wait_recv()
+        own = fin_gu.at[1, xbit, core, ybit]
+        own[...] = (own[...].astype(full) + g1_y[...].astype(full)).astype(low)
+        plus_upper(own, up_gu.at[1], dp.at[room_gu])
+        gu_b.append(spread_gu(1))
 
     def row_of(k):
         return jnp.concatenate([small_all[i, k : k + 1, :] for i in range(4)], 1).astype(full)
@@ -1030,6 +1031,7 @@
     g2[z2] = (g2[z2].astype(full) + g2_z1[1].astype(full)).astype(low)
     g2s = net.send(g2.at[z2], g2_z2, "z2")
 
+    gu_first()
     dn_first()
     dn_second(0)
     dn_second(1)
@@ -1082,7 +1084,7 @@
     weight_chunk(ht, lambda cols: dp[:, pl.ds(pl.multiple_of(width + cols.start, 256), 256)], width)
     sc.append(to_core(1))
 
-    orders = ["xy", "yx", "xy", "all"]
+    orders = ["xy", "yx", "yx", "xy"]
     def spot_of(i, zi, yi, xi):
         return (zi, yi, xi, core, slice(None), cols_of(i))
 
@@ -1224,9 +1226,6 @@
         return carry
 
     lax.fori_loop(0, 4, back_in, 0)
-    b[1] = add_first(1, a[1])
-    c = {0: add_second(0, b[0])}
-
     def norm_back(i, total):
         at = pl.ds(pl.multiple_of(i * tile, tile), tile)
         xf = x_ref[at].astype(full)
@@ -1242,8 +1241,10 @@
     keep_grad = net.move(out_ref, grad_out)
     sums[0:1, :] = jnp.sum(total, axis=0, keepdims=True)
     small_core = net.send(sums, sums_core, "core")
+    b[1] = add_first(1, a[1])
+    c = {0: add_second(0, b[0])}
+    b[2] = add_first(2, a[2])
     dn_third(1)
-    b[2] = add_first(2, a[2])
     small_core.wait()
     sums[...] = sums[...] + sums_core[...]
     small_plane = [
@@ -1253,8 +1254,9 @@
     dn_third(2)
     dn_fourth(0)
     c[1] = add_second(1, b[1])
-    c[3] = add_second(3, a[3])
+    b[3] = add_first(3, a[3])
     c[2] = add_second(2, b[2])
+    c[3] = add_second(3, b[3])
     dn_fourth(1)
     d = {0: add_z(0, c[0])}
     gu_d.append(onward_gu(2, gu_b[2]))
@@ -1276,15 +1278,15 @@
         for i, (zz, seat) in enumerate(((z1, "z1"), (z2, "z2"), (z3, "z3")))
     ]
     d[1] = add_z(1, c[1])
+    d[2] = add_z(2, c[2])
     d[3] = add_z(3, c[3])
-    d[2] = add_z(2, c[2])
     f = {0: across_c(0, d[0])}
     last_gu(0, gu_c[0])
     last_gu(1, gu_c[1])
     dn_fifth(1)
     dn_fifth(2)
     gu_c.append(across_gu(2, gu_d[2]))
-    for i in (1, 3, 2):
+    for i in (1, 2, 3):
         f[i] = across_c(i, d[i])
     for copy in small_z:
         copy.wait()
@@ -1292,7 +1294,7 @@
     keep_small = net.move(small_out, gsmall_out)
     for k in range(3):
         dn_last(k)
-    for i in (0, 1, 3, 2):
+    for i in (0, 1, 2, 3):
         last_c(i, f[i])
     last_gu(2, gu_c[2])
 
@@ -1316,7 +1318,7 @@
         for copy in dny + dnc:
             copy.wait_send()
 
-    flat = [g1a, g1b, g2s, back, dn0] + gu_c + sc
+    flat = [g1a, g1b, g2s, back, dn0, g1y] + gu_c + sc
     for group in gu_b + gu_d:
         flat += list(group)
     for group in (a, b, c, d, f):
@@ -1388,6 +1390,8 @@
         v((4, half, pair), low),
         v((2, half, pair), low),
         v((half, pair), low),
+        v((half, pair), low),
+        v((half, pair), low),
         v((3, chunk // 2, width), low),
         v((3, chunk // 2, width), low),
         v((3, chunk // 2, width), low),

time: 344 us -> 340 us (0.988)
    pallas_call x1, Pallas kernels: 113 us -> 108 us  [feed(): pl.pallas_call(functools.partial(feed_kernel, seq), out_shape=outs, in_sp...]
where the time goes in v5:
time: 340 us; the launch traced here: 339 us
  Pallas kernels  338 us (99%)
    pallas_call x1, Pallas kernels, finish(): pl.pallas_call(functools.partial(finish_kernel, seq), out_shape=outs, in_...  111 us
    pallas_call x1, Pallas kernels, feed(): pl.pallas_call(functools.partial(feed_kernel, seq), out_shape=outs, in_sp...  108 us
    pallas_call x1, Pallas kernels, gather(): pl.pallas_call(functools.partial(gather_kernel, seq), out_shape=outs, in_...  106 us
    pallas_call x1, Pallas kernels, cast(): pl.pallas_call(cast_kernel, grid=(steps,), out_shape=[jax.ShapeDtypeStruc...  12.5 us

profile of v5, /device:TPU:1, one launch (start us, length us, event | category | flops | bytes accessed | tf_op | source)
XLA Modules:
  0.0 338.5 jit_solution(16102158441071943324)
XLA Ops:
  0.6 106.0 %gather.1 = (bf16[4,4,2,32,4096]{4,3,2,1,0:T(8,128)(2,1)}, bf16[4,256,2304]{2,1,0:T(8,128)(2,1)}, bf16[3,2,192,1024]{3,2,1,0:T(8,128)(2,1)}, bf16[4,512,1024]{2,...) custom-call(bf16[512,1024]{1,0:T(8,128)(2,1)} %bitcast.15, ...), custom_call_target="tpu_custom_call" | custom-call | tf_op jit(solution)/shard_map/gather/pallas_call | solution.py:432
  106.6 107.7 %feed.1 = (bf16[512,1024]{1,0:T(8,128)(2,1)}, f32[512,1024]{1,0:T(8,128)}, bf16[128,768]{1,0:T(8,128)(2,1)}, bf16[2,128,768]{2,1,0:T(8,128)(2,1)}, bf16[4,128,76...) custom-call(bf16[4,512,1024]{2,1,0:T(8,128)(2,1)} %get-tuple-element, ...), custom_call_target="tpu_custom_call" | custom-call | tf_op jit(solution)/shard_map/feed/pallas_call | solution.py:773
  214.4 111.5 %finish.1 = (bf16[512,1024]{1,0:T(8,128)(2,1)}, bf16[2,2,2,32,3072]{4,3,2,1,0:T(8,128)(2,1)}, bf16[2,2,2,32,1024]{4,3,2,1,0:T(8,128)(2,1)}, bf16[2,128,9216]{2,1...) custom-call(s32[1,512]{1,0:T(1,128)} %starts_ref.3, ...), custom_call_target="tpu_custom_call" | custom-call | tf_op jit(solution)/shard_map/finish/pallas_call | solution.py:1404
  325.9 12.5 %cast.1 = (f32[256,9216]{1,0:T(8,128)}, f32[1152,1024]{1,0:T(8,128)}, f32[256,3072]{1,0:T(8,128)}, f32[256,1024]{1,0:T(8,128)}, bf16[1,512,1024]{2,1,0:T(8,128)(...) custom-call(bf16[256,9216]{1,0:T(8,128)(2,1)} %bitcast.13, ...), custom_call_target="tpu_custom_call" | custom-call | bytes 33816576 | tf_op jit(solution)/shard_map/cast/pallas_call | solution.py:1446

commit v6 on v5

--- a/solution.py
+++ b/solution.py
@@ -1084,7 +1084,7 @@
     weight_chunk(ht, lambda cols: dp[:, pl.ds(pl.multiple_of(width + cols.start, 256), 256)], width)
     sc.append(to_core(1))
 
-    orders = ["xy", "yx", "yx", "xy"]
+    orders = ["z", "xy", "yx", "xy"]
     def spot_of(i, zi, yi, xi):
         return (zi, yi, xi, core, slice(None), cols_of(i))
 
@@ -1103,6 +1103,11 @@
             return net.send(dwc.at[:, :, 1 - xbit, core, :, cols], r1.at[i], "x")
         if orders[i] == "yx":
             return net.send(dwc.at[:, 1 - ybit, :, core, :, cols], r1.at[i], "y")
+        if orders[i] == "z":
+            return [
+                net.send(dwc.at[zz, :, :, core, :, cols], r1.at[i, pl.ds(2 * k, 2)], "z1")
+                for k, zz in enumerate((z1, z3))
+            ]
         return [
             net.send(dwc.at[:, yi, xi, core, :, cols], land, seat)
             for yi, xi, land, seat in (
@@ -1113,6 +1118,25 @@
         ]
 
     def add_first(i, copy):
+        if orders[i] == "z":
+            for c in copy:
+                c.wait_recv()
+
+            def pair_of(j, carry):
+                yi, xi = j // 2, j % 2
+                for k, zz in enumerate((z2, z)):
+                    spot = spot_of(i, zz, yi, xi)
+                    land = r1[i, 2 - 2 * k + yi, xi]
+                    dwc[spot] = (dwc[spot].astype(full) + land.astype(full)).astype(low)
+                return carry
+
+            lax.fori_loop(0, 4, pair_of, 0)
+            return [
+                net.send(
+                    dwc.at[z2, yi, :, core, :, cols_of(i)], r2.at[i, pl.ds(2 * yi, 2)], "z2"
+                )
+                for yi in range(2)
+            ]
         copy.wait_recv()
 
         def one(j, carry):
@@ -1129,6 +1153,22 @@
         return net.send(dwc.at[:, ybit, 1 - xbit, core, :, cols], r2.at[i], "x")
 
     def add_second(i, copy):
+        if orders[i] == "z":
+            for c in copy:
+                c.wait_recv()
+
+            def one_of(j, carry):
+                spot = spot_of(i, z, j // 2, j % 2)
+                dwc[spot] = (dwc[spot].astype(full) + r2[i, j].astype(full)).astype(low)
+                return carry
+
+            lax.fori_loop(0, 4, one_of, 0)
+            return [
+                net.send(dwc.at[spot_of(i, z, yi, xi)], rz.at[i, k], seat)
+                for k, (yi, xi, seat) in enumerate(
+                    ((ybit, 1 - xbit, "x"), (1 - ybit, xbit, "y"), (1 - ybit, 1 - xbit, cross))
+                )
+            ]
         if orders[i] == "all":
             for c in copy:
                 c.wait_recv()
@@ -1428,7 +1468,7 @@
 
 
 def cast(gu, dn, win, wout, result, grad_x, small):
-    steps = 8
+    steps = 4
     arrays = (gu, dn, win, wout, result, grad_x)
 
     def cut(v, lead=False):

time: 340 us -> 339 us (level); the launches traced: 339 us -> 334 us
  Pallas kernels: 338 us -> 333 us
    pallas_call x1, Pallas kernels: 111 us -> 107 us  [finish(): pl.pallas_call(functools.partial(finish_kernel, seq), out_shape=outs, in_...]
where the time goes in v6:
time: 339 us; the launch traced here: 334 us
  Pallas kernels  333 us (98%)
    pallas_call x1, Pallas kernels, feed(): pl.pallas_call(functools.partial(feed_kernel, seq), out_shape=outs, in_sp...  108 us
    pallas_call x1, Pallas kernels, finish(): pl.pallas_call(functools.partial(finish_kernel, seq), out_shape=outs, in_...  107 us
    pallas_call x1, Pallas kernels, gather(): pl.pallas_call(functools.partial(gather_kernel, seq), out_shape=outs, in_...  106 us
    pallas_call x1, Pallas kernels, cast(): pl.pallas_call(cast_kernel, grid=(steps,), out_shape=[jax.ShapeDtypeStruc...  11.9 us

profile of v6, /device:TPU:1, one launch (start us, length us, event | category | flops | bytes accessed | tf_op | source)
XLA Modules:
  0.0 333.7 jit_solution(13500122033619350184)
XLA Ops:
  0.6 106.0 %gather.1 = (bf16[4,4,2,32,4096]{4,3,2,1,0:T(8,128)(2,1)}, bf16[4,256,2304]{2,1,0:T(8,128)(2,1)}, bf16[3,2,192,1024]{3,2,1,0:T(8,128)(2,1)}, bf16[4,512,1024]{2,...) custom-call(bf16[512,1024]{1,0:T(8,128)(2,1)} %bitcast.15, ...), custom_call_target="tpu_custom_call" | custom-call | tf_op jit(solution)/shard_map/gather/pallas_call | solution.py:432
  106.6 107.7 %feed.1 = (bf16[512,1024]{1,0:T(8,128)(2,1)}, f32[512,1024]{1,0:T(8,128)}, bf16[128,768]{1,0:T(8,128)(2,1)}, bf16[2,128,768]{2,1,0:T(8,128)(2,1)}, bf16[4,128,76...) custom-call(bf16[4,512,1024]{2,1,0:T(8,128)(2,1)} %get-tuple-element, ...), custom_call_target="tpu_custom_call" | custom-call | tf_op jit(solution)/shard_map/feed/pallas_call | solution.py:773
  214.4 107.3 %finish.1 = (bf16[512,1024]{1,0:T(8,128)(2,1)}, bf16[2,2,2,32,3072]{4,3,2,1,0:T(8,128)(2,1)}, bf16[2,2,2,32,1024]{4,3,2,1,0:T(8,128)(2,1)}, bf16[2,128,9216]{2,1...) custom-call(s32[1,512]{1,0:T(1,128)} %starts_ref.3, ...), custom_call_target="tpu_custom_call" | custom-call | tf_op jit(solution)/shard_map/finish/pallas_call | solution.py:1444
  321.7 11.9 %cast.1 = (f32[256,9216]{1,0:T(8,128)}, f32[1152,1024]{1,0:T(8,128)}, f32[256,3072]{1,0:T(8,128)}, f32[256,1024]{1,0:T(8,128)}, bf16[1,512,1024]{2,1,0:T(8,128)(...) custom-call(bf16[256,9216]{1,0:T(8,128)(2,1)} %bitcast.13, ...), custom_call_target="tpu_custom_call" | custom-call | bytes 33816576 | tf_op jit(solution)/shard_map/cast/pallas_call | solution.py:1486

commit v7 on v6

--- a/solution.py
+++ b/solution.py
@@ -642,11 +642,11 @@
     fetch(3)
     out_rows(1, add(send_o, temp))
     ox = net.send(send_o, land_out.at[4], "x")
-    forward(2, 0, 2)
     y0.wait_recv()
     lax.fori_loop(0, 4, gu0_sum, 0)
     n1 = net.send(gu0_s.at[z1], gu0_z1.at[0], "z1")
     n2 = net.send(gu0_s.at[z3], gu0_z1.at[1], "z1")
+    forward(2, 0, 2)
     weights(2)
     y2 = net.send(dgu.at[:, 1 - ybit, :, cols_of(2)], gu2_y, "y")
     keep_dn2 = net.move(ddn.at[2], dn2_out)

time: 339 us -> 339 us (level)
  no operation moved by 1% of the time
where the time goes in v7:
time: 339 us; the launch traced here: 334 us
  Pallas kernels  333 us (98%)
    pallas_call x1, Pallas kernels, feed(): pl.pallas_call(functools.partial(feed_kernel, seq), out_shape=outs, in_sp...  108 us
    pallas_call x1, Pallas kernels, finish(): pl.pallas_call(functools.partial(finish_kernel, seq), out_shape=outs, in_...  107 us
    pallas_call x1, Pallas kernels, gather(): pl.pallas_call(functools.partial(gather_kernel, seq), out_shape=outs, in_...  106 us
    pallas_call x1, Pallas kernels, cast(): pl.pallas_call(cast_kernel, grid=(steps,), out_shape=[jax.ShapeDtypeStruc...  11.9 us

profile of v7, /device:TPU:1, one launch (start us, length us, event | category | flops | bytes accessed | tf_op | source)
XLA Modules:
  0.0 333.7 jit_solution(12803547693319274608)
XLA Ops:
  0.6 106.0 %gather.1 = (bf16[4,4,2,32,4096]{4,3,2,1,0:T(8,128)(2,1)}, bf16[4,256,2304]{2,1,0:T(8,128)(2,1)}, bf16[3,2,192,1024]{3,2,1,0:T(8,128)(2,1)}, bf16[4,512,1024]{2,...) custom-call(bf16[512,1024]{1,0:T(8,128)(2,1)} %bitcast.15, ...), custom_call_target="tpu_custom_call" | custom-call | tf_op jit(solution)/shard_map/gather/pallas_call | solution.py:432
  106.6 107.7 %feed.1 = (bf16[512,1024]{1,0:T(8,128)(2,1)}, f32[512,1024]{1,0:T(8,128)}, bf16[128,768]{1,0:T(8,128)(2,1)}, bf16[2,128,768]{2,1,0:T(8,128)(2,1)}, bf16[4,128,76...) custom-call(bf16[4,512,1024]{2,1,0:T(8,128)(2,1)} %get-tuple-element, ...), custom_call_target="tpu_custom_call" | custom-call | tf_op jit(solution)/shard_map/feed/pallas_call | solution.py:773
  214.4 107.3 %finish.1 = (bf16[512,1024]{1,0:T(8,128)(2,1)}, bf16[2,2,2,32,3072]{4,3,2,1,0:T(8,128)(2,1)}, bf16[2,2,2,32,1024]{4,3,2,1,0:T(8,128)(2,1)}, bf16[2,128,9216]{2,1...) custom-call(s32[1,512]{1,0:T(1,128)} %starts_ref.3, ...), custom_call_target="tpu_custom_call" | custom-call | tf_op jit(solution)/shard_map/finish/pallas_call | solution.py:1444
  321.7 11.9 %cast.1 = (f32[256,9216]{1,0:T(8,128)}, f32[1152,1024]{1,0:T(8,128)}, f32[256,3072]{1,0:T(8,128)}, f32[256,1024]{1,0:T(8,128)}, bf16[1,512,1024]{2,1,0:T(8,128)(...) custom-call(bf16[256,9216]{1,0:T(8,128)(2,1)} %bitcast.13, ...), custom_call_target="tpu_custom_call" | custom-call | bytes 33816576 | tf_op jit(solution)/shard_map/cast/pallas_call | solution.py:1486
